TPU v7x, 1024 devices: a whole 8x8x8 slice. The times are simulated.
1024 devices in a mesh: gx: 64 (over z, y), gy: 8 (over x), gz: 2 (over core).
Axes of the slice: x: 8, y: 8, z: 8, core: 2. Of those that a mesh axis runs over, the one named last changes fastest.
Arguments:
- fine_rhs: float32 [32768, 8, 64], P(('gx', 'gy', 'gz')), may hold values from -15 to 15
- fine_coef: bfloat16 [32768, 8, 64], P(('gx', 'gy', 'gz')), may hold values from 0.25 to 2
- coarse_rhs: float32 [512, 128, 256], P('gx', 'gy', 'gz'), may hold values from -15 to 15
- coarse_coef: bfloat16 [512, 128, 256], P('gx', 'gy', 'gz'), may hold values from 0.25 to 2
- patch_count: int32 [1024], P(('gx', 'gy', 'gz')), may hold values from 1 to 32, as said below
- patch_target: int32 [32768], P(('gx', 'gy', 'gz')), may hold values from 0 to 4095, as said below
Outputs:
- fine_solution: float32 [32768, 8, 64], P(('gx', 'gy', 'gz'))
- coarse_solution: float32 [512, 128, 256], P('gx', 'gy', 'gz')
- deep_solution: float32 [64, 16, 32], P('gx', 'gy', 'gz')
Inputs may be any that keep to these rules, and one draw needn't show every extreme that they name: A device's live patches fill its slots 0 to patch_count - 1; in every gx slab some device has all 32 slots live. `patch_target`: A target is owner * 256 + local block, owner being the gy+gz index of a device in the holder's gx slab. The targets of all slots of one gx slab differ. At most 2 slots of one device name one owner, and a device with all slots live names every owner exactly 2 times.
All inputs are finite; a program needn't handle non-finite values.
Results may differ from a plain program's by a relative error of at most 0.0003.
Values may be sent and summed in bfloat16 or wider, within the bound.
No kernel may reach another device: no remote copies, remote signals or barrier semaphores. Data moves between devices by JAX's collectives and lax.ppermute only.
A program may use at most 128 MiB of HBM per device.

v0:
```python
import jax
import jax.numpy as jnp
from jax import lax
from jax.sharding import PartitionSpec as P

DEEP = 3


DAMPING = 6.0 / 7.0
PRECISE = lax.Precision.HIGHEST


def padded_2(block, sides, width):
    for axis, dim in sides:
        count = lax.axis_size(axis)
        forward = [(i, i + 1) for i in range(count - 1)]
        backward = [(target, source) for source, target in forward]
        low = lax.ppermute(
            lax.slice_in_dim(block, block.shape[dim] - width, None, axis=dim), axis, forward
        )
        high = lax.ppermute(lax.slice_in_dim(block, 0, width, axis=dim), axis, backward)
        block = jnp.concatenate([low, block, high], axis=dim)
    return block


def cell_faces(values):
    return padded_2(values, (("gx", 0), ("gy", 1), ("gz", 2)), 1)


def grid_sides(padded):
    return (
        padded[:-2, 1:-1, 1:-1],
        padded[2:, 1:-1, 1:-1],
        padded[1:-1, :-2, 1:-1],
        padded[1:-1, 2:, 1:-1],
        padded[1:-1, 1:-1, :-2],
        padded[1:-1, 1:-1, 2:],
    )


def patch_sides(values, zcoord, patch_side):
    zeros_row = jnp.zeros_like(values[:, :1])
    lower_x = jnp.concatenate([zeros_row, values[:, :-1]], axis=1)
    upper_x = jnp.concatenate([values[:, 1:], zeros_row], axis=1)
    zeros_y = jnp.zeros_like(values[:, :, :patch_side])
    lower_y = jnp.concatenate([zeros_y, values[:, :, :-patch_side]], axis=2)
    upper_y = jnp.concatenate([values[:, :, patch_side:], zeros_y], axis=2)
    zeros_z = jnp.zeros_like(values[:, :, :1])
    lower_z = jnp.where(zcoord == 0, 0.0, jnp.concatenate([zeros_z, values[:, :, :-1]], axis=2))
    upper_z = jnp.where(
        zcoord == patch_side - 1, 0.0, jnp.concatenate([values[:, :, 1:], zeros_z], axis=2)
    )
    return (lower_x, upper_x, lower_y, upper_y, lower_z, upper_z)


def combine_sides(weights, side_values):
    summed = weights[0] * side_values[0]
    for number in range(1, 6):
        summed = summed + weights[number] * side_values[number]
    return summed


def face_weights(conduct, side_values):
    weights = tuple((0.5 * (conduct + neighbour) for neighbour in side_values))
    diagonal = weights[0]
    for number in range(1, 6):
        diagonal = diagonal + weights[number]
    return (weights, diagonal)


def smooth(source, weights, diagonal, sides_of, last_level):
    first_pass = DAMPING * source / diagonal
    second_pass = (
        first_pass
        + DAMPING
        * (source - diagonal * first_pass + combine_sides(weights, sides_of(first_pass)))
        / diagonal
    )
    if last_level:
        return (second_pass, None)
    residue = source - diagonal * second_pass + combine_sides(weights, sides_of(second_pass))
    return (second_pass, residue)


def grid_level(source, conduct, extend, last_level):
    weights, diagonal = face_weights(conduct, grid_sides(extend(conduct)))

    def sides_of(values):
        return grid_sides(extend(values))

    return smooth(source, weights, diagonal, sides_of, last_level)


def halve_sum(values):
    return (
        values.reshape(
            values.shape[0] // 2, 2, values.shape[1] // 2, 2, values.shape[2] // 2, 2
        ).sum(axis=(1, 3, 5))
        * 0.5
    )


def eighth_sum(values):
    return (
        values.reshape(
            values.shape[0] // 2, 2, values.shape[1] // 2, 2, values.shape[2] // 2, 2
        ).sum(axis=(1, 3, 5))
        * 0.125
    )


def per_device(fine_rhs, fine_coef, coarse_rhs, coarse_coef, patch_count, patch_target):
    slot_total = fine_rhs.shape[0]
    patch_side = fine_rhs.shape[1]
    block_side = patch_side // 2
    block_cells = block_side**3
    group_size = 8
    live_count = patch_count[0]
    zcoord = (lax.iota(jnp.int32, patch_side * patch_side) % patch_side)[None, None, :]

    def fine_group(group_id, state_pair):
        solved, reduced = state_pair
        first_slot = group_id * group_size
        source = lax.dynamic_slice_in_dim(fine_rhs, first_slot, group_size, 0)
        conduct = lax.dynamic_slice_in_dim(fine_coef, first_slot, group_size, 0).astype(jnp.float32)
        weights, diagonal = face_weights(conduct, patch_sides(conduct, zcoord, patch_side))

        def sides_of(values):
            return patch_sides(values, zcoord, patch_side)

        second_pass, residue = smooth(source, weights, diagonal, sides_of, False)
        alive_rows = (first_slot + lax.iota(jnp.int32, group_size) < live_count)[:, None, None]
        second_pass = jnp.where(alive_rows, second_pass, 0.0)
        coarse_part = (
            residue.reshape(group_size, block_side, 2, block_side, 2, block_side, 2).sum(
                axis=(2, 4, 6)
            )
            * 0.5
        )
        coarse_part = coarse_part.reshape(group_size, block_cells)
        solved = lax.dynamic_update_slice_in_dim(solved, second_pass, first_slot, 0)
        reduced = lax.dynamic_update_slice_in_dim(reduced, coarse_part, first_slot, 0)
        return (solved, reduced)

    group_count = (live_count + group_size - 1) // group_size
    fine_solution, restricted = lax.fori_loop(
        0,
        group_count,
        fine_group,
        (jnp.zeros(fine_rhs.shape, jnp.float32), jnp.zeros((slot_total, block_cells), jnp.float32)),
    )
    size_x, size_y, size_z = coarse_rhs.shape
    blocks_x = size_x // block_side
    blocks_y = size_y // block_side
    blocks_z = size_z // block_side
    block_total = blocks_x * blocks_y * blocks_z
    alive_slots = lax.iota(jnp.int32, slot_total) < live_count
    block_ids = lax.iota(jnp.int32, block_total)
    my_rank = lax.axis_index(("gy", "gz"))
    slot_tags = jnp.where(alive_slots, patch_target + 1, 0).astype(jnp.float32)
    wanted = (my_rank * block_total + block_ids + 1).astype(jnp.float32)
    placing = (
        lax.all_gather(slot_tags, ("gy", "gz"), axis=0, tiled=True)[None, :] == wanted[:, None]
    ).astype(jnp.float32)
    placed = jnp.dot(
        placing, lax.all_gather(restricted, ("gy", "gz"), axis=0, tiled=True), precision=PRECISE
    )
    covered = jnp.sum(placing, axis=1)
    block_shape = (blocks_x, blocks_y, blocks_z, block_side, block_side, block_side)
    placed_grid = (
        placed.reshape(block_shape).transpose(0, 3, 1, 4, 2, 5).reshape(size_x, size_y, size_z)
    )
    covered_grid = jnp.broadcast_to(
        covered.reshape(blocks_x, blocks_y, blocks_z)[:, None, :, None, :, None],
        (blocks_x, block_side, blocks_y, block_side, blocks_z, block_side),
    ).reshape(size_x, size_y, size_z)
    source = jnp.where(covered_grid > 0.5, placed_grid, coarse_rhs)
    conduct = coarse_coef.astype(jnp.float32)
    coarse_solution, residue = grid_level(source, conduct, cell_faces, False)
    deep_solution = coarse_solution
    for level_number in range(1, DEEP + 1):
        source = halve_sum(residue)
        conduct = eighth_sum(conduct)
        deep_solution, residue = grid_level(source, conduct, cell_faces, level_number == DEEP)
    return (fine_solution, coarse_solution, deep_solution)


def solution(mesh):
    return jax.shard_map(
        per_device,
        mesh=mesh,
        in_specs=(
            P(("gx", "gy", "gz"), None, None),
            P(("gx", "gy", "gz"), None, None),
            P("gx", "gy", "gz"),
            P("gx", "gy", "gz"),
            P(("gx", "gy", "gz")),
            P(("gx", "gy", "gz")),
        ),
        out_specs=(P(("gx", "gy", "gz"), None, None), P("gx", "gy", "gz"), P("gx", "gy", "gz")),
        check_vma=False,
    )
```

profile of v0, /device:TPU:519, one launch (start us, length us, event | category | flops | bytes accessed | tf_op | source)
XLA Modules:
  0.0 321.9 jit_solution(17700654399430212229)
XLA Ops:
  4.7 5.3 %collective-permute-start.1 = (f32[1,16,128]{2,1,0:T(8,128)S(1)}, f32[1,16,128]{2,1,0:T(8,128)S(1)}, u32[]{:S(2)}, u32[]{:S(2)}) collective-permute-start(f32[1,16,128]{2,1,0:T(8,128)S(1)} %get-tuple-element.207), channel_id=1, source_target_pairs={{16,0},{32,16},{48,32},{64,48},{80,64},{96,80},{112,96},{128,112},... | collective-permute-start | bytes 24584 | tf_op jit(solution)/shard_map/ppermute | solution.py:21
  10.6 6.2 %reshape.126 = f32[4,2,8,2,64,2]{5,4,3,2,1,0:T(8,128)} reshape(bf16[8,16,128]{2,1,0:T(8,128)(2,1)} %param.11) | data formatting | bytes 98304 | tf_op jit(solution)/shard_map/reshape | solution.py:105
  18.9 23.6 %all-reduce.18 = f32[512]{0:T(512)S(1)} all-reduce(f32[512]{0:T(512)S(1)} %fusion.145), channel_id=1, replica_groups=mesh['gx'=64,'gy'=8,'gz'=2] {'gy','gz'}, use_global_device_ids=true, to_apply=%add.18 | all-reduce | flops 512 | bytes 4096
  42.5 9.1 %while.14 = (s32[]{:T(128)}, f32[32,8,64]{2,1,0:T(8,128)S(1)}, f32[32,64]{1,0:T(8,128)S(1)}, s32[]{:T(128)}, s32[]{:T(128)}, /*index=5*/f32[32,8,64]{2,1,0:T(8,1...) while((s32[]{:T(128)}, f32[32,8,64]{2,1,0:T(8,128)S(1)}, ...), condition=%wide.region_2.3_spmd.clone.clone, body=%wide.region_0.2_spmd.clone.clone.sunk | while | flops 414230 | bytes 1373391 | solution.py:146
  51.6 21.8 %all_gather.7 = f32[512,64]{1,0:T(8,128)S(1)} all-gather(f32[32,64]{1,0:T(8,128)S(1)} %get-tuple-element.63), channel_id=1, replica_groups=mesh['gx'=64,'gy'=8,'gz'=2] {'gy','gz'}, dimensions={0}, use_global_device_ids=true | all-gather | bytes 139264 | tf_op jit(solution)/shard_map/all_gather | solution.py:166
  94.8 5.4 %collective-permute-start.6 = (f32[1,16,128]{2,1,0:T(8,128)S(1)}, f32[1,16,128]{2,1,0:T(8,128)S(1)}, u32[]{:S(2)}, u32[]{:S(2)}) collective-permute-start(f32[1,16,128]{2,1,0:T(8,128)S(1)} %get-tuple-element.198), channel_id=1, source_target_pairs={{0,16},{16,32},{32,48},{48,64},{64,80},{80,96},{96,112},{112,128},... | collective-permute-start | bytes 24584 | tf_op jit(solution)/shard_map/ppermute | solution.py:18
  109.8 6.6 %collective-permute-start.55 = (f32[1,2,16]{2,1,0:T(2,128)S(1)}, f32[1,2,16]{2,1,0:T(2,128)S(1)}, u32[]{:S(2)}, u32[]{:S(2)}) collective-permute-start(f32[1,2,16]{2,1,0:T(2,128)S(1)} %multiply_bitcast_fusion), channel_id=1, source_target_pairs={{16,0},{32,16},{48,32},{64,48},{80,64},{96,80},{112,96},{128,112},... | collective-permute-start | bytes 392 | tf_op jit(solution)/shard_map/ppermute | solution.py:21
  119.8 5.3 %collective-permute-start.11 = (f32[10,18,1]{2,1,0:T(8,128)S(1)}, f32[10,18,1]{2,1,0:T(8,128)S(1)}, u32[]{:S(2)}, u32[]{:S(2)}) collective-permute-start(f32[10,18,1]{2,1,0:T(8,128)S(1)} %get-tuple-element.187), channel_id=1, source_target_pairs={{1,0},{3,2},{5,4},{7,6},{9,8},{11,10},{13,12},{15,14},{17,16},{19,... | collective-permute-start | bytes 2168 | tf_op jit(solution)/shard_map/ppermute | solution.py:21
  125.1 7.0 %collective-permute-start.19 = (f32[1,8,64]{2,1,0:T(8,128)S(1)}, f32[1,8,64]{2,1,0:T(8,128)S(1)}, u32[]{:S(2)}, u32[]{:S(2)}) collective-permute-start(f32[1,8,64]{2,1,0:T(8,128)S(1)} %get-tuple-element.224), channel_id=1, source_target_pairs={{16,0},{32,16},{48,32},{64,48},{80,64},{96,80},{112,96},{128,112},... | collective-permute-start | bytes 6152 | tf_op jit(solution)/shard_map/ppermute | solution.py:21
  136.2 6.7 %collective-permute-start.13 = (f32[1,16,128]{2,1,0:T(8,128)S(1)}, f32[1,16,128]{2,1,0:T(8,128)S(1)}, u32[]{:S(2)}, u32[]{:S(2)}) collective-permute-start(f32[1,16,128]{2,1,0:T(8,128)S(1)} %get-tuple-element.197), channel_id=1, source_target_pairs={{16,0},{32,16},{48,32},{64,48},{80,64},{96,80},{112,96},{128,112},... | collective-permute-start | bytes 24584 | tf_op jit(solution)/shard_map/ppermute | solution.py:21
  144.9 4.5 %collective-permute-start.20 = (f32[6,1,64]{2,1,0:T(1,128)S(1)}, f32[6,1,64]{2,1,0:T(1,128)S(1)}, u32[]{:S(2)}, u32[]{:S(2)}) collective-permute-start(f32[6,1,64]{2,1,0:T(1,128)S(1)} %get-tuple-element.213), channel_id=1, source_target_pairs={{0,2},{2,4},{4,6},{6,8},{8,10},{10,12},{12,14},{1,3},{3,5},{5,7},{... | collective-permute-start | bytes 4616 | tf_op jit(solution)/shard_map/ppermute | solution.py:18
  159.6 4.1 %collective-permute-start.17 = (f32[10,18,1]{2,1,0:T(8,128)S(1)}, f32[10,18,1]{2,1,0:T(8,128)S(1)}, u32[]{:S(2)}, u32[]{:S(2)}) collective-permute-start(f32[10,18,1]{2,1,0:T(8,128)S(1)} %get-tuple-element.185), channel_id=1, source_target_pairs={{1,0},{3,2},{5,4},{7,6},{9,8},{11,10},{13,12},{15,14},{17,16},{19,... | collective-permute-start | bytes 2168 | tf_op jit(solution)/shard_map/ppermute | solution.py:21
  166.7 5.6 %reshape.125 = f32[4,2,8,2,64,2]{5,4,3,2,1,0:T(8,128)} reshape(f32[8,16,128]{2,1,0:T(8,128)S(1)} %fusion.22) | data formatting | bytes 131072 | tf_op jit(solution)/shard_map/reshape | solution.py:96
  176.9 6.7 %collective-permute-start.25 = (f32[1,8,64]{2,1,0:T(8,128)S(1)}, f32[1,8,64]{2,1,0:T(8,128)S(1)}, u32[]{:S(2)}, u32[]{:S(2)}) collective-permute-start(f32[1,8,64]{2,1,0:T(8,128)S(1)} %get-tuple-element.223), channel_id=1, source_target_pairs={{16,0},{32,16},{48,32},{64,48},{80,64},{96,80},{112,96},{128,112},... | collective-permute-start | bytes 6152 | tf_op jit(solution)/shard_map/ppermute | solution.py:21
  197.8 5.3 %collective-permute-start.29 = (f32[6,10,1]{2,1,0:T(8,128)S(1)}, f32[6,10,1]{2,1,0:T(8,128)S(1)}, u32[]{:S(2)}, u32[]{:S(2)}) collective-permute-start(f32[6,10,1]{2,1,0:T(8,128)S(1)} %get-tuple-element.203), channel_id=1, source_target_pairs={{1,0},{3,2},{5,4},{7,6},{9,8},{11,10},{13,12},{15,14},{17,16},{19,... | collective-permute-start | bytes 728 | tf_op jit(solution)/shard_map/ppermute | solution.py:21
  205.6 4.1 %collective-permute-start.38 = (f32[4,1,32]{2,1,0:T(1,128)S(1)}, f32[4,1,32]{2,1,0:T(1,128)S(1)}, u32[]{:S(2)}, u32[]{:S(2)}) collective-permute-start(f32[4,1,32]{2,1,0:T(1,128)S(1)} %get-tuple-element.231), channel_id=1, source_target_pairs={{0,2},{2,4},{4,6},{6,8},{8,10},{10,12},{12,14},{1,3},{3,5},{5,7},{... | collective-permute-start | bytes 1544 | tf_op jit(solution)/shard_map/ppermute | solution.py:18
  211.7 6.7 %collective-permute-start.31 = (f32[1,8,64]{2,1,0:T(8,128)S(1)}, f32[1,8,64]{2,1,0:T(8,128)S(1)}, u32[]{:S(2)}, u32[]{:S(2)}) collective-permute-start(f32[1,8,64]{2,1,0:T(8,128)S(1)} %get-tuple-element.221), channel_id=1, source_target_pairs={{16,0},{32,16},{48,32},{64,48},{80,64},{96,80},{112,96},{128,112},... | collective-permute-start | bytes 6152 | tf_op jit(solution)/shard_map/ppermute | solution.py:21
  228.0 4.1 %collective-permute-start.35 = (f32[6,10,1]{2,1,0:T(8,128)S(1)}, f32[6,10,1]{2,1,0:T(8,128)S(1)}, u32[]{:S(2)}, u32[]{:S(2)}) collective-permute-start(f32[6,10,1]{2,1,0:T(8,128)S(1)} %get-tuple-element.201), channel_id=1, source_target_pairs={{1,0},{3,2},{5,4},{7,6},{9,8},{11,10},{13,12},{15,14},{17,16},{19,... | collective-permute-start | bytes 728 | tf_op jit(solution)/shard_map/ppermute | solution.py:21
  238.6 7.2 %collective-permute-start.43 = (f32[1,4,32]{2,1,0:T(4,128)S(1)}, f32[1,4,32]{2,1,0:T(4,128)S(1)}, u32[]{:S(2)}, u32[]{:S(2)}) collective-permute-start(f32[1,4,32]{2,1,0:T(4,128)S(1)} %get-tuple-element.241), channel_id=1, source_target_pairs={{16,0},{32,16},{48,32},{64,48},{80,64},{96,80},{112,96},{128,112},... | collective-permute-start | bytes 1544 | tf_op jit(solution)/shard_map/ppermute | solution.py:21
  254.3 4.1 %collective-permute-start.56 = (f32[3,1,16]{2,1,0:T(1,128)S(1)}, f32[3,1,16]{2,1,0:T(1,128)S(1)}, u32[]{:S(2)}, u32[]{:S(2)}) collective-permute-start(f32[3,1,16]{2,1,0:T(1,128)S(1)} %get-tuple-element.247), channel_id=1, source_target_pairs={{0,2},{2,4},{4,6},{6,8},{8,10},{10,12},{12,14},{1,3},{3,5},{5,7},{... | collective-permute-start | bytes 584 | tf_op jit(solution)/shard_map/ppermute | solution.py:18
  266.7 7.2 %collective-permute-start.49 = (f32[1,4,32]{2,1,0:T(4,128)S(1)}, f32[1,4,32]{2,1,0:T(4,128)S(1)}, u32[]{:S(2)}, u32[]{:S(2)}) collective-permute-start(f32[1,4,32]{2,1,0:T(4,128)S(1)} %get-tuple-element.239), channel_id=1, source_target_pairs={{16,0},{32,16},{48,32},{64,48},{80,64},{96,80},{112,96},{128,112},... | collective-permute-start | bytes 1544 | tf_op jit(solution)/shard_map/ppermute | solution.py:21
  290.6 7.2 %collective-permute-start.61 = (f32[1,2,16]{2,1,0:T(2,128)S(1)}, f32[1,2,16]{2,1,0:T(2,128)S(1)}, u32[]{:S(2)}, u32[]{:S(2)}) collective-permute-start(f32[1,2,16]{2,1,0:T(2,128)S(1)} %bitcast_divide_fusion), channel_id=1, source_target_pairs={{16,0},{32,16},{48,32},{64,48},{80,64},{96,80},{112,96},{128,112},... | collective-permute-start | bytes 392 | tf_op jit(solution)/shard_map/ppermute | solution.py:21
  299.8 5.7 %collective-permute-done.60 = f32[1,2,16]{2,1,0:T(2,128)S(1)} collective-permute-done((f32[1,2,16]{2,1,0:T(2,128)S(1)}, f32[1,2,16]{2,1,0:T(2,128)S(1)}, u32[]{:S(2)}, u32[]{:S(2)}) %collective-permute-start.60) | collective-permute-done | bytes 160 | tf_op jit(solution)/shard_map/ppermute | solution.py:18
  315.3 5.1 %collective-permute-start.65 = (f32[3,4,1]{2,1,0:T(4,128)S(1)}, f32[3,4,1]{2,1,0:T(4,128)S(1)}, u32[]{:S(2)}, u32[]{:S(2)}) collective-permute-start(f32[3,4,1]{2,1,0:T(4,128)S(1)} %get-tuple-element.233), channel_id=1, source_target_pairs={{1,0},{3,2},{5,4},{7,6},{9,8},{11,10},{13,12},{15,14},{17,16},{19,... | collective-permute-start | bytes 152 | tf_op jit(solution)/shard_map/ppermute | solution.py:21
  (255 shorter events, 152.9 us)
Async XLA Ops:
  1.4 75.1 %collective-permute-start = (f32[1,16,128]{2,1,0:T(8,128)S(1)}, f32[1,16,128]{2,1,0:T(8,128)S(1)}, u32[]{:S(2)}, u32[]{:S(2)}) collective-permute-start(f32[1,16,128]{2,1,0:T(8,128)S(1)} %get-tuple-element.206), channel_id=1, source_target_pairs={{0,16},{16,32},{32,48},{48,64},{64,80},{80,96},{96,112},{112,128},... | collective-permute-start | bytes 24584 | tf_op jit(solution)/shard_map/ppermute | solution.py:18
  4.7 71.8 %collective-permute-start.1 = (f32[1,16,128]{2,1,0:T(8,128)S(1)}, f32[1,16,128]{2,1,0:T(8,128)S(1)}, u32[]{:S(2)}, u32[]{:S(2)}) collective-permute-start(f32[1,16,128]{2,1,0:T(8,128)S(1)} %get-tuple-element.207), channel_id=1, source_target_pairs={{16,0},{32,16},{48,32},{64,48},{80,64},{96,80},{112,96},{128,112},... | collective-permute-start | bytes 24584 | tf_op jit(solution)/shard_map/ppermute | solution.py:21
  84.1 10.4 %collective-permute-start.5 = (f32[10,18,1]{2,1,0:T(8,128)S(1)}, f32[10,18,1]{2,1,0:T(8,128)S(1)}, u32[]{:S(2)}, u32[]{:S(2)}) collective-permute-start(f32[10,18,1]{2,1,0:T(8,128)S(1)} %get-tuple-element.188), channel_id=1, source_target_pairs={{1,0},{3,2},{5,4},{7,6},{9,8},{11,10},{13,12},{15,14},{17,16},{19,... | collective-permute-start | bytes 2168 | tf_op jit(solution)/shard_map/ppermute | solution.py:21
  104.5 13.8 %collective-permute-start.8 = (f32[10,1,128]{2,1,0:T(1,128)S(1)}, f32[10,1,128]{2,1,0:T(1,128)S(1)}, u32[]{:S(2)}, u32[]{:S(2)}) collective-permute-start(f32[10,1,128]{2,1,0:T(1,128)S(1)} %get-tuple-element.192), channel_id=1, source_target_pairs={{0,2},{2,4},{4,6},{6,8},{8,10},{10,12},{12,14},{1,3},{3,5},{5,7},{... | collective-permute-start | bytes 15368 | tf_op jit(solution)/shard_map/ppermute | solution.py:18
  107.3 11.1 %collective-permute-start.9 = (f32[10,1,128]{2,1,0:T(1,128)S(1)}, f32[10,1,128]{2,1,0:T(1,128)S(1)}, u32[]{:S(2)}, u32[]{:S(2)}) collective-permute-start(f32[10,1,128]{2,1,0:T(1,128)S(1)} %get-tuple-element.193), channel_id=1, source_target_pairs={{2,0},{4,2},{6,4},{8,6},{10,8},{12,10},{14,12},{3,1},{5,3},{7,5},{... | collective-permute-start | bytes 15368 | tf_op jit(solution)/shard_map/ppermute | solution.py:21
  109.8 136.0 %collective-permute-start.55 = (f32[1,2,16]{2,1,0:T(2,128)S(1)}, f32[1,2,16]{2,1,0:T(2,128)S(1)}, u32[]{:S(2)}, u32[]{:S(2)}) collective-permute-start(f32[1,2,16]{2,1,0:T(2,128)S(1)} %multiply_bitcast_fusion), channel_id=1, source_target_pairs={{16,0},{32,16},{48,32},{64,48},{80,64},{96,80},{112,96},{128,112},... | collective-permute-start | bytes 392 | tf_op jit(solution)/shard_map/ppermute | solution.py:21
  116.4 129.4 %collective-permute-start.54 = (f32[1,2,16]{2,1,0:T(2,128)S(1)}, f32[1,2,16]{2,1,0:T(2,128)S(1)}, u32[]{:S(2)}, u32[]{:S(2)}) collective-permute-start(f32[1,2,16]{2,1,0:T(2,128)S(1)} %multiply_bitcast_fusion), channel_id=1, source_target_pairs={{0,16},{16,32},{32,48},{48,64},{64,80},{80,96},{96,112},{112,128},... | collective-permute-start | bytes 392 | tf_op jit(solution)/shard_map/ppermute | solution.py:18
  118.5 13.6 %collective-permute-start.10 = (f32[10,18,1]{2,1,0:T(8,128)S(1)}, f32[10,18,1]{2,1,0:T(8,128)S(1)}, u32[]{:S(2)}, u32[]{:S(2)}) collective-permute-start(f32[10,18,1]{2,1,0:T(8,128)S(1)} %get-tuple-element.186), channel_id=1, source_target_pairs={{0,1},{2,3},{4,5},{6,7},{8,9},{10,11},{12,13},{14,15},{16,17},{18,... | collective-permute-start | bytes 2168 | tf_op jit(solution)/shard_map/ppermute | solution.py:18
  119.8 14.2 %collective-permute-start.11 = (f32[10,18,1]{2,1,0:T(8,128)S(1)}, f32[10,18,1]{2,1,0:T(8,128)S(1)}, u32[]{:S(2)}, u32[]{:S(2)}) collective-permute-start(f32[10,18,1]{2,1,0:T(8,128)S(1)} %get-tuple-element.187), channel_id=1, source_target_pairs={{1,0},{3,2},{5,4},{7,6},{9,8},{11,10},{13,12},{15,14},{17,16},{19,... | collective-permute-start | bytes 2168 | tf_op jit(solution)/shard_map/ppermute | solution.py:21
  125.1 11.0 %collective-permute-start.19 = (f32[1,8,64]{2,1,0:T(8,128)S(1)}, f32[1,8,64]{2,1,0:T(8,128)S(1)}, u32[]{:S(2)}, u32[]{:S(2)}) collective-permute-start(f32[1,8,64]{2,1,0:T(8,128)S(1)} %get-tuple-element.224), channel_id=1, source_target_pairs={{16,0},{32,16},{48,32},{64,48},{80,64},{96,80},{112,96},{128,112},... | collective-permute-start | bytes 6152 | tf_op jit(solution)/shard_map/ppermute | solution.py:21
  132.1 10.8 %collective-permute-start.18 = (f32[1,8,64]{2,1,0:T(8,128)S(1)}, f32[1,8,64]{2,1,0:T(8,128)S(1)}, u32[]{:S(2)}, u32[]{:S(2)}) collective-permute-start(f32[1,8,64]{2,1,0:T(8,128)S(1)} %get-tuple-element.225), channel_id=1, source_target_pairs={{0,16},{16,32},{32,48},{48,64},{64,80},{80,96},{96,112},{112,128},... | collective-permute-start | bytes 6152 | tf_op jit(solution)/shard_map/ppermute | solution.py:18
  134.2 10.6 %collective-permute-start.12 = (f32[1,16,128]{2,1,0:T(8,128)S(1)}, f32[1,16,128]{2,1,0:T(8,128)S(1)}, u32[]{:S(2)}, u32[]{:S(2)}) collective-permute-start(f32[1,16,128]{2,1,0:T(8,128)S(1)} %get-tuple-element.196), channel_id=1, source_target_pairs={{0,16},{16,32},{32,48},{48,64},{64,80},{80,96},{96,112},{112,128},... | collective-permute-start | bytes 24584 | tf_op jit(solution)/shard_map/ppermute | solution.py:18
  136.2 13.2 %collective-permute-start.13 = (f32[1,16,128]{2,1,0:T(8,128)S(1)}, f32[1,16,128]{2,1,0:T(8,128)S(1)}, u32[]{:S(2)}, u32[]{:S(2)}) collective-permute-start(f32[1,16,128]{2,1,0:T(8,128)S(1)} %get-tuple-element.197), channel_id=1, source_target_pairs={{16,0},{32,16},{48,32},{64,48},{80,64},{96,80},{112,96},{128,112},... | collective-permute-start | bytes 24584 | tf_op jit(solution)/shard_map/ppermute | solution.py:21
  163.8 11.1 %collective-permute-start.23 = (f32[6,10,1]{2,1,0:T(8,128)S(1)}, f32[6,10,1]{2,1,0:T(8,128)S(1)}, u32[]{:S(2)}, u32[]{:S(2)}) collective-permute-start(f32[6,10,1]{2,1,0:T(8,128)S(1)} %get-tuple-element.204), channel_id=1, source_target_pairs={{1,0},{3,2},{5,4},{7,6},{9,8},{11,10},{13,12},{15,14},{17,16},{19,... | collective-permute-start | bytes 728 | tf_op jit(solution)/shard_map/ppermute | solution.py:21
  175.0 10.6 %collective-permute-start.24 = (f32[1,8,64]{2,1,0:T(8,128)S(1)}, f32[1,8,64]{2,1,0:T(8,128)S(1)}, u32[]{:S(2)}, u32[]{:S(2)}) collective-permute-start(f32[1,8,64]{2,1,0:T(8,128)S(1)} %get-tuple-element.222), channel_id=1, source_target_pairs={{0,16},{16,32},{32,48},{48,64},{64,80},{80,96},{96,112},{112,128},... | collective-permute-start | bytes 6152 | tf_op jit(solution)/shard_map/ppermute | solution.py:18
  176.9 12.0 %collective-permute-start.25 = (f32[1,8,64]{2,1,0:T(8,128)S(1)}, f32[1,8,64]{2,1,0:T(8,128)S(1)}, u32[]{:S(2)}, u32[]{:S(2)}) collective-permute-start(f32[1,8,64]{2,1,0:T(8,128)S(1)} %get-tuple-element.223), channel_id=1, source_target_pairs={{16,0},{32,16},{48,32},{64,48},{80,64},{96,80},{112,96},{128,112},... | collective-permute-start | bytes 6152 | tf_op jit(solution)/shard_map/ppermute | solution.py:21
  197.8 11.8 %collective-permute-start.29 = (f32[6,10,1]{2,1,0:T(8,128)S(1)}, f32[6,10,1]{2,1,0:T(8,128)S(1)}, u32[]{:S(2)}, u32[]{:S(2)}) collective-permute-start(f32[6,10,1]{2,1,0:T(8,128)S(1)} %get-tuple-element.203), channel_id=1, source_target_pairs={{1,0},{3,2},{5,4},{7,6},{9,8},{11,10},{13,12},{15,14},{17,16},{19,... | collective-permute-start | bytes 728 | tf_op jit(solution)/shard_map/ppermute | solution.py:21
  205.6 12.8 %collective-permute-start.38 = (f32[4,1,32]{2,1,0:T(1,128)S(1)}, f32[4,1,32]{2,1,0:T(1,128)S(1)}, u32[]{:S(2)}, u32[]{:S(2)}) collective-permute-start(f32[4,1,32]{2,1,0:T(1,128)S(1)} %get-tuple-element.231), channel_id=1, source_target_pairs={{0,2},{2,4},{4,6},{6,8},{8,10},{10,12},{12,14},{1,3},{3,5},{5,7},{... | collective-permute-start | bytes 1544 | tf_op jit(solution)/shard_map/ppermute | solution.py:18
  246.6 11.8 %collective-permute-start.44 = (f32[4,1,32]{2,1,0:T(1,128)S(1)}, f32[4,1,32]{2,1,0:T(1,128)S(1)}, u32[]{:S(2)}, u32[]{:S(2)}) collective-permute-start(f32[4,1,32]{2,1,0:T(1,128)S(1)} %get-tuple-element.228), channel_id=1, source_target_pairs={{0,2},{2,4},{4,6},{6,8},{8,10},{10,12},{12,14},{1,3},{3,5},{5,7},{... | collective-permute-start | bytes 1544 | tf_op jit(solution)/shard_map/ppermute | solution.py:18
  248.5 9.9 %collective-permute-start.45 = (f32[4,1,32]{2,1,0:T(1,128)S(1)}, f32[4,1,32]{2,1,0:T(1,128)S(1)}, u32[]{:S(2)}, u32[]{:S(2)}) collective-permute-start(f32[4,1,32]{2,1,0:T(1,128)S(1)} %get-tuple-element.229), channel_id=1, source_target_pairs={{2,0},{4,2},{6,4},{8,6},{10,8},{12,10},{14,12},{3,1},{5,3},{7,5},{... | collective-permute-start | bytes 1544 | tf_op jit(solution)/shard_map/ppermute | solution.py:21
  251.9 22.1 %collective-permute-start.57 = (f32[3,1,16]{2,1,0:T(1,128)S(1)}, f32[3,1,16]{2,1,0:T(1,128)S(1)}, u32[]{:S(2)}, u32[]{:S(2)}) collective-permute-start(f32[3,1,16]{2,1,0:T(1,128)S(1)} %get-tuple-element.246), channel_id=1, source_target_pairs={{2,0},{4,2},{6,4},{8,6},{10,8},{12,10},{14,12},{3,1},{5,3},{7,5},{... | collective-permute-start | bytes 584 | tf_op jit(solution)/shard_map/ppermute | solution.py:21
  254.3 19.6 %collective-permute-start.56 = (f32[3,1,16]{2,1,0:T(1,128)S(1)}, f32[3,1,16]{2,1,0:T(1,128)S(1)}, u32[]{:S(2)}, u32[]{:S(2)}) collective-permute-start(f32[3,1,16]{2,1,0:T(1,128)S(1)} %get-tuple-element.247), channel_id=1, source_target_pairs={{0,2},{2,4},{4,6},{6,8},{8,10},{10,12},{12,14},{1,3},{3,5},{5,7},{... | collective-permute-start | bytes 584 | tf_op jit(solution)/shard_map/ppermute | solution.py:18
  274.7 10.3 %collective-permute-start.50 = (f32[4,1,32]{2,1,0:T(1,128)S(1)}, f32[4,1,32]{2,1,0:T(1,128)S(1)}, u32[]{:S(2)}, u32[]{:S(2)}) collective-permute-start(f32[4,1,32]{2,1,0:T(1,128)S(1)} %get-tuple-element.226), channel_id=1, source_target_pairs={{0,2},{2,4},{4,6},{6,8},{8,10},{10,12},{12,14},{1,3},{3,5},{5,7},{... | collective-permute-start | bytes 1544 | tf_op jit(solution)/shard_map/ppermute | solution.py:18
  280.0 10.5 %collective-permute-start.59 = (f32[3,4,1]{2,1,0:T(4,128)S(1)}, f32[3,4,1]{2,1,0:T(4,128)S(1)}, u32[]{:S(2)}, u32[]{:S(2)}) collective-permute-start(f32[3,4,1]{2,1,0:T(4,128)S(1)} %get-tuple-element.234), channel_id=1, source_target_pairs={{1,0},{3,2},{5,4},{7,6},{9,8},{11,10},{13,12},{15,14},{17,16},{19,... | collective-permute-start | bytes 152 | tf_op jit(solution)/shard_map/ppermute | solution.py:21
  (47 other events, 427.4 us)
where the time goes:
time: 324 us; the launch traced here: 322 us
  starting transfers between devices  210 us (65%)
  blocking collectives  45.4 us (14%)
  local copies, waits for them, and re-layouts  25.3 us (8%)
  waiting for transfers between devices  24.9 us (8%)
  other arithmetic  12.2 us (4%)
  between operations  3.27 us (1%)
    ppermute x33, starting transfers between devices, padded_2(): lax.ppermute(lax.slice_in_dim(block, 0, width, axis=dim), axis, backward)  137 us
    ppermute x33, starting transfers between devices, padded_2(): lax.ppermute(lax.slice_in_dim(block, block.shape[dim] - width, None, axis...  72.7 us
    unnamed x1, blocking collectives  23.6 us
    all_gather x1, blocking collectives, per_device(): lax.all_gather(restricted, ('gy', 'gz'), axis=0, tiled=True)  21.8 us
    ppermute x33, waiting for transfers between devices, padded_2(): lax.ppermute(lax.slice_in_dim(block, 0, width, axis=dim), axis, backward)  18.1 us
    ppermute x33, waiting for transfers between devices, padded_2(): lax.ppermute(lax.slice_in_dim(block, block.shape[dim] - width, None, axis...  6.77 us
  transfers between devices with their start and end apart: 66, of which 14 were waited for; matrix products, arithmetic and copies ran while one was open for 11% of the time, Pallas kernels for 0%

commit v1 on v0

v1 whole, which is shorter than its diff:
```python
import functools

import jax
import jax.numpy as jnp
from jax import lax
from jax.experimental import pallas as pl
from jax.experimental.pallas import tpu as pltpu
from jax.sharding import PartitionSpec as P

DAMPING = 6.0 / 7.0
REST = 1.0 - DAMPING
PRECISE = lax.Precision.HIGHEST
F32 = jnp.float32
CORES = 2
VMEM_BYTES = 40 * 1024 * 1024


def iota(shape, dim):
    return lax.broadcasted_iota(jnp.int32, shape, dim)


def dot(a, b):
    return jnp.dot(a, b, precision=PRECISE, preferred_element_type=F32)


def after(values, axis):
    return pltpu.roll(values, values.shape[axis] - 1, axis)


def before(values, axis):
    return pltpu.roll(values, 1, axis)


def fine_kernel(count_ref, target_ref, rhs_ref, coef_ref, solved_ref, send_ref):
    live = count_ref[0]
    half = rhs_ref.shape[0] // 2
    source = jnp.concatenate([rhs_ref[:half], rhs_ref[half:]], axis=2)
    k = coef_ref[...].astype(F32) * 0.5
    h = jnp.concatenate([k[:half], k[half:]], axis=2)
    shape = h.shape
    x, lane = iota(shape, 1), iota(shape, 2)
    y, z = (lane >> 3) & 7, lane & 7

    def wrapped(values, amount):
        return pltpu.roll(values, amount % 128, 2)

    hx = jnp.where(x < 7, after(h, 1), 0.0)
    hy = jnp.where(y < 7, wrapped(h, -8), 0.0)
    hz = jnp.where(z < 7, wrapped(h, -1), 0.0)
    diagonal = 6.0 * h + hx + hy + hz
    diagonal += jnp.where(x > 0, before(h, 1), 0.0)
    diagonal += jnp.where(y > 0, wrapped(h, 8), 0.0)
    diagonal += jnp.where(z > 0, wrapped(h, 1), 0.0)
    wx = jnp.where(x < 7, h + hx, 0.0)
    wy = jnp.where(y < 7, h + hy, 0.0)
    wz = jnp.where(z < 7, h + hz, 0.0)

    def sides(u):
        total = wx * after(u, 1) + before(wx * u, 1)
        total += wy * wrapped(u, -8) + wrapped(wy * u, 8)
        return total + wz * wrapped(u, -1) + wrapped(wz * u, 1)

    scale = DAMPING / diagonal
    first = source * scale
    second = first + scale * (REST * source + sides(first))
    residue = source - diagonal * second + sides(second)
    slot = iota((half, 8, 64), 0)
    solved_ref[:half] = jnp.where(slot < live, second[:, :, :64], 0.0)
    solved_ref[half:] = jnp.where(slot + half < live, second[:, :, 64:], 0.0)

    square = (128, 128)
    row, col = iota(square, 0), iota(square, 1)
    iz, ix, iy = col >> 4, (col >> 2) & 3, col & 3
    match = (((row >> 4) & 3) == iy) & (((row >> 1) & 3) == iz)
    keep = ((row >> 1) & 3) == ix
    cells = residue.reshape(square)
    parts = []
    for number in range(2):
        gather = jnp.where(match & ((row >> 6) == number), 0.5, 0.0)
        parts.append(jnp.where(keep, dot(cells, gather), 0.0))

    wide = (32, 256)
    spread = jnp.where(iota(wide, 0) == (iota(wide, 1) >> 3), 1.0, 0.0)
    names = jnp.broadcast_to(target_ref[...].astype(F32), (8, 32))
    name = (dot(names, spread)[:1] + 0.5).astype(jnp.int32)
    row, col = iota(wide, 0), iota(wide, 1)
    name = jnp.broadcast_to(name, wide)
    own = jnp.sum(jnp.where(col == row * 8, name, 0).astype(F32), axis=1, keepdims=True)
    own = own.astype(jnp.int32)
    earlier = ((own >> 8) == (name >> 8)) & (row < (col >> 3))
    rank = jnp.sum(jnp.where(earlier, 1.0, 0.0), axis=0, keepdims=True).astype(jnp.int32)
    place = (name >> 8) * 2 + rank
    chosen = (place == row) & ((col >> 3) < live)
    picked = jnp.where(chosen, 1.0, 0.0)
    tag = jnp.where(chosen & ((col & 7) == 0), (name & 255) + 1, 0).astype(F32)
    tag = jnp.sum(tag, axis=1, keepdims=True)
    packed = dot(picked[:, :128], parts[0]) + dot(picked[:, 128:], parts[1])
    send_ref[...] = jnp.where(iota(packed.shape, 1) < 64, packed, tag)


def place_kernel(got_ref, rhs_ref, coef_ref, out_ref):
    got = got_ref[...]
    four = jnp.concatenate([got, got, got, got], axis=0)
    square = (128, 128)
    row, col = iota(square, 0), iota(square, 1)
    slices = jnp.where((col >> 4) == (row >> 5), four, 0.0)
    cell = (((row >> 4) & 3) << 2) + (row & 3)
    select = jnp.where(((col & 15) == cell) & (col < 64), 1.0, 0.0)
    turned = (((1,), (1,)), ((), ()))
    left = lax.dot_general(select, slices, turned, precision=PRECISE, preferred_element_type=F32)
    only = jnp.where(iota((8, 128), 1) == 64, 1.0, 0.0)
    tags = lax.dot_general(only, four, turned, precision=PRECISE, preferred_element_type=F32)
    tags = (tags[:1] + 0.5).astype(jnp.int32) - 1
    tags = jnp.broadcast_to(tags, square)
    here = ((tags >> 7) == (row >> 6)) & (((tags >> 5) & 3) == ((row >> 2) & 3))
    down = (four[:, 64:65] + 0.5).astype(jnp.int32) - 1
    right = jnp.where(((down & 31) == (col >> 2)) & ((col & 3) == (row >> 5)), 1.0, 0.0)
    placed = dot(jnp.where(here, left, 0.0), right)
    covered = jnp.dot(
        jnp.where(here, 1.0, 0.0).astype(jnp.bfloat16),
        right.astype(jnp.bfloat16),
        preferred_element_type=F32,
    )
    shape = rhs_ref.shape
    out_ref[0] = jnp.where(covered.reshape(shape) > 0.5, placed.reshape(shape), rhs_ref[...])
    out_ref[1] = coef_ref[...].astype(F32) * 0.5


def pair_matrix(size):
    shape = (size, 128)
    return jnp.where((iota(shape, 0) >> 1) == iota(shape, 1), 1.0, 0.0)


def prepare(h, inside, depth):
    mid = h[1:-1]
    lane = iota(mid.shape, 2)
    hy = after(mid, 1)
    hz = jnp.where(lane < depth - 1, after(mid, 2), 0.0)
    diagonal = 6.0 * mid + h[:-2] + h[2:] + hy + before(mid, 1) + hz
    diagonal += jnp.where(lane > 0, before(mid, 2), 0.0)
    scale = jnp.where(inside & (lane < depth), DAMPING / diagonal, 0.0)
    wx = h[:-1] + h[1:]
    wy = mid + hy
    wz = jnp.where(lane < depth - 1, mid + hz, 0.0)
    return diagonal, scale, wx, wy, wz


def neighbours(u, wx, wy, wz):
    mid = u[1:-1]
    total = wx[1:] * u[2:] + wx[:-1] * u[:-2]
    total += wy * after(mid, 1) + before(wy * mid, 1)
    return total + wz * after(mid, 2) + before(wz * mid, 2)


def within(shape, start, first_layer, first_row, sizes):
    x = iota(shape, 0) + (start[0] + first_layer)
    y = iota(shape, 1) + (start[1] + first_row)
    return (x >= 0) & (x < sizes[0]) & (y >= 0) & (y < sizes[1])


def coarser(values, matrix, scale, rows_ref):
    layers, rows, depth = values.shape
    values = values.reshape(layers // 2, 2, rows, depth)
    values = values[:, 0] + values[:, 1]
    flat = dot(values.reshape(layers // 2 * rows, depth), matrix) * scale
    count = flat.shape[0]
    rows_ref[:count] = flat
    total = rows_ref[pl.ds(0, count // 2, stride=2), :] + rows_ref[pl.ds(1, count // 2, stride=2), :]
    return total.reshape(layers // 2, rows // 2, 128)


def base_kernel(
    sizes, pos_ref, full_ref, side_ref, out_ref, pay_ref,
    s_ref, h_ref, wx_ref, wy_ref, wz_ref, diag_ref, scale_ref, first_ref, second_ref,
    res_ref, rows_ref,
):
    gx, gy, core = pos_ref[0], pos_ref[1], pos_ref[2]
    for number in range(2):
        lanes = slice(128 * number, 128 * number + 128)
        s_ref[0:6, :, lanes] = side_ref[0, number, 0:6]
        s_ref[6:14, :, lanes] = full_ref[number, 0]
        s_ref[14:20, :, lanes] = side_ref[1, number, 0:6]
        h_ref[0:7, :, lanes] = side_ref[0, number, 6:13]
        h_ref[7:15, :, lanes] = full_ref[number, 1]
        h_ref[15:22, :, lanes] = side_ref[1, number, 6:13]
    shape = (32, 256)
    lane = iota(shape, 1)
    y = iota(shape, 0) + (gy * 16 - 8)
    rows_in = (y >= 0) & (y < sizes[1])

    def weigh(layer, _):
        h = h_ref[layer + 1]
        below, above = h_ref[layer], h_ref[layer + 2]
        hy = after(h, 0)
        hz = jnp.where(lane < 255, after(h, 1), 0.0)
        diagonal = 6.0 * h + below + above + hy + before(h, 0) + hz
        diagonal += jnp.where(lane > 0, before(h, 1), 0.0)
        x = gx * 8 + layer - 6
        inside = rows_in & (x >= 0) & (x < sizes[0])
        scale = jnp.where(inside, DAMPING / diagonal, 0.0)
        diag_ref[layer] = diagonal
        scale_ref[layer] = scale
        wx_ref[layer] = h + above
        wy_ref[layer] = h + hy
        wz_ref[layer] = jnp.where(lane < 255, h + hz, 0.0)
        first_ref[layer] = s_ref[layer] * scale
        return 0

    lax.fori_loop(0, 20, weigh, 0)

    def sides(ref, layer):
        u, wy, wz = ref[layer], wy_ref[layer], wz_ref[layer]
        total = wx_ref[layer] * ref[layer + 1] + wx_ref[layer - 1] * ref[layer - 1]
        total += wy * after(u, 0) + before(wy * u, 0)
        return u, total + wz * after(u, 1) + before(wz * u, 1)

    def correct(layer, _):
        u, total = sides(first_ref, layer)
        second_ref[layer] = u + scale_ref[layer] * (REST * s_ref[layer] + total)
        return 0

    lax.fori_loop(1, 19, correct, 0)

    def leave(layer, _):
        u, total = sides(second_ref, layer)
        res_ref[layer - 2] = s_ref[layer] - diag_ref[layer] * u + total
        return 0

    lax.fori_loop(2, 18, leave, 0)
    own = second_ref[6:14, 8:24, :]
    out_ref[...] = jnp.where(core == 0, own[:, :, :128], own[:, :, 128:])

    zoom = pair_matrix(256)
    source = coarser(res_ref[...], zoom, 0.5, rows_ref)
    h = coarser(h_ref[1:21], zoom, 0.125, rows_ref)
    inside = within(source.shape, (gx * 4, gy * 8), -2, -4, (sizes[0] // 2, sizes[1] // 2))
    diagonal, scale, wx, wy, wz = prepare(h, inside, 128)
    first = source * scale
    total = neighbours(first, wx[1:-1], wy[1:-1], wz[1:-1])
    second = first[1:-1] + scale[1:-1] * (REST * source[1:-1] + total)
    total = neighbours(second, wx[2:-2], wy[2:-2], wz[2:-2])
    residue = source[2:-2] - diagonal[2:-2] * second[1:-1] + total

    zoom = pair_matrix(128)
    source = coarser(residue, zoom, 0.5, rows_ref)
    h = coarser(h[1:-1], zoom, 0.125, rows_ref)
    _, scale, _, _, _ = prepare(h, jnp.full(source.shape, True), 64)
    pay_ref[0:2] = source[:, 2:6]
    pay_ref[2:4] = (source * scale)[:, 2:6]
    pay_ref[4:6] = h[1:3, 2:6]


def deep_kernel(sizes, pos_ref, mid_ref, side_ref, out_ref, win_ref, rows_ref):
    gx, gy, core = pos_ref[0], pos_ref[1], pos_ref[2]
    win_ref[...] = jnp.zeros(win_ref.shape, F32)
    for number in range(3):
        for part in range(3):
            blocks = [
                side_ref[0, 1, part], side_ref[0, 0, part], mid_ref[part],
                side_ref[1, 0, part], side_ref[1, 1, part],
            ]
            for place, block in enumerate(blocks):
                win_ref[number, 2 * place : 2 * place + 2, 4 * part : 4 * part + 4] = block[
                    2 * number : 2 * number + 2
                ]
    source, first, h = win_ref[0], win_ref[1], win_ref[2]
    shape = (8, 16, 128)
    inside = within(shape, (gx * 2, gy * 4), -3, -4, (sizes[0] // 4, sizes[1] // 4))
    inside &= iota(shape, 1) < 12
    diagonal, scale, wx, wy, wz = prepare(h, inside, 64)
    total = neighbours(first, wx, wy, wz)
    second = first[1:-1] + scale * (REST * source[1:-1] + total)
    total = neighbours(second, wx[1:-1], wy[1:-1], wz[1:-1])
    residue = source[2:-2] - diagonal[1:-1] * second[1:-1] + total

    zoom = pair_matrix(128)
    source = coarser(residue, zoom, 0.5, rows_ref)
    h = coarser(h, zoom, 0.125, rows_ref)
    inside = within(source.shape, (gx, gy * 2), -1, -2, (sizes[0] // 8, sizes[1] // 8))
    inside &= iota(source.shape, 1) < 6
    _, scale, wx, wy, wz = prepare(h, inside, 32)
    first = source * scale
    total = neighbours(first, wx[1:-1], wy[1:-1], wz[1:-1])
    second = first[1:-1] + scale[1:-1] * (REST * source[1:-1] + total)
    second = second[:, 2:4]
    out_ref[...] = jnp.where(core == 0, second[:, :, :16], second[:, :, 16:32])


def call(kernel, out_shape, in_specs=None, scratch=(), flops=100_000):
    specs = {} if in_specs is None else {"in_specs": in_specs}
    return pl.pallas_call(
        kernel,
        out_shape=out_shape,
        scratch_shapes=list(scratch),
        compiler_params=pltpu.CompilerParams(vmem_limit_bytes=VMEM_BYTES),
        cost_estimate=pl.CostEstimate(flops=flops, bytes_accessed=flops, transcendentals=0),
        **specs,
    )


def split_send(values, axis, step):
    count = lax.axis_size(axis)
    pairs = []
    for place in range(count):
        if place + step < count:
            pairs.append((place * CORES, (place + step) * CORES))
        if place - step >= 0:
            pairs.append((place * CORES + 1, (place - step) * CORES + 1))
    return lax.ppermute(values, (axis, "gz"), pairs)


def shared(values):
    return lax.all_gather(values, "gz")


def per_device(fine_rhs, fine_coef, coarse_rhs, coarse_coef, patch_count, patch_target):
    core = lax.axis_index("gz")
    pos = jnp.stack([lax.axis_index("gx"), lax.axis_index("gy"), core])
    sizes = (
        lax.axis_size("gx") * coarse_rhs.shape[0],
        lax.axis_size("gy") * coarse_rhs.shape[1],
    )
    vmem = pl.BlockSpec(memory_space=pltpu.VMEM)
    smem = pl.BlockSpec(memory_space=pltpu.SMEM)
    struct = jax.ShapeDtypeStruct
    fine_solution, send = call(
        fine_kernel,
        (struct(fine_rhs.shape, F32), struct((32, 128), F32)),
        [smem, vmem, vmem, vmem],
    )(patch_count, patch_target.reshape(1, 32), fine_rhs, fine_coef)
    got = lax.all_to_all(send.reshape(16, 2, 128), ("gy", "gz"), 0, 0).reshape(32, 128)
    both = call(place_kernel, struct((2, 8, 16, 128), F32), [vmem, vmem, vmem])(
        got, coarse_rhs, coarse_coef
    )
    chip = shared(both)
    rows = jnp.where(core == 0, chip[:, :, :, 8:], chip[:, :, :, :8])
    halo = shared(split_send(rows, "gy", 1))
    full = jnp.concatenate([halo[0], chip, halo[1]], axis=3)
    high = jnp.concatenate([full[:, 0, 2:], full[:, 1, 1:]], axis=1)
    low = jnp.concatenate([full[:, 0, :6], full[:, 1, :7]], axis=1)
    side = shared(split_send(jnp.where(core == 0, high, low), "gx", 1))
    grid = (32, 256)
    coarse_solution, pay = call(
        functools.partial(base_kernel, sizes),
        (struct((8, 16, 128), F32), struct((6, 4, 128), F32)),
        [smem, vmem, vmem],
        [pltpu.VMEM((20, *grid), F32), pltpu.VMEM((22, *grid), F32)]
        + [pltpu.VMEM((20, *grid), F32)] * 7
        + [pltpu.VMEM((16, *grid), F32), pltpu.VMEM((320, 128), F32)],
        flops=5_000_000,
    )(pos, full, side)
    halo = shared(split_send(pay, "gy", 1))
    mid = jnp.stack([halo[0], pay, halo[1]])
    sides = shared(jnp.stack([split_send(mid, "gx", 1), split_send(mid, "gx", 2)]))
    deep_solution = call(
        functools.partial(deep_kernel, sizes),
        struct((1, 2, 16), F32),
        [smem, vmem, vmem],
        [pltpu.VMEM((3, 10, 16, 128), F32), pltpu.VMEM((320, 128), F32)],
    )(pos, mid, sides)
    return (fine_solution, coarse_solution, deep_solution)


def solution(mesh):
    return jax.shard_map(
        per_device,
        mesh=mesh,
        in_specs=(
            P(("gx", "gy", "gz"), None, None),
            P(("gx", "gy", "gz"), None, None),
            P("gx", "gy", "gz"),
            P("gx", "gy", "gz"),
            P(("gx", "gy", "gz")),
            P(("gx", "gy", "gz")),
        ),
        out_specs=(P(("gx", "gy", "gz"), None, None), P("gx", "gy", "gz"), P("gx", "gy", "gz")),
        check_vma=False,
    )
```

time: 324 us -> 77.3 us (0.24)
  the two profiles are of different devices: /device:TPU:519 before, /device:TPU:51 now
where the time goes in v1:
time: 77.3 us; the launch traced here: 76.9 us
  starting transfers between devices  25.8 us (33%)
  waiting for transfers between devices  22.7 us (29%)
  blocking collectives  12.5 us (16%)
  Pallas kernels  11.7 us (15%)
  local copies, waits for them, and re-layouts  2.5 us (3%)
  between operations  1.4 us (2%)
    ppermute x5, starting transfers between devices, split_send(): return lax.ppermute(values, (axis, 'gz'), pairs)  18.1 us
    ppermute x5, waiting for transfers between devices, split_send(): return lax.ppermute(values, (axis, 'gz'), pairs)  16.4 us
    all_gather x5, blocking collectives, shared(): return lax.all_gather(values, 'gz')  12.5 us
    all_to_all x1, starting transfers between devices, per_device(): lax.all_to_all(send.reshape(16, 2, 128), ('gy', 'gz'), 0, 0)  7.75 us
    pallas_call x1, Pallas kernels, per_device(): call(functools.partial(base_kernel, sizes), (struct((8, 16, 128), F32), s...  7.53 us
    all_to_all x1, waiting for transfers between devices, per_device(): lax.all_to_all(send.reshape(16, 2, 128), ('gy', 'gz'), 0, 0)  6.22 us
    unnamed x10, local copies, waits for them, and re-layouts  2.4 us
    pallas_call x1, Pallas kernels, per_device(): call(functools.partial(deep_kernel, sizes), struct((1, 2, 16), F32), [sme...  1.82 us
  transfers between devices with their start and end apart: 6, of which 5 were waited for; matrix products, arithmetic and copies ran while one was open for 0% of the time, Pallas kernels for 0%

profile of v1, /device:TPU:51, one launch (start us, length us, event | category | flops | bytes accessed | tf_op | source)
XLA Modules:
  0.0 76.9 jit_solution(11661552921527610992)
XLA Ops:
  1.3 0.6 copy-done.4
  1.9 0.9 %copy-done = f32[32,8,64]{2,1,0:T(8,128)S(1)} copy-done((f32[32,8,64]{2,1,0:T(8,128)S(1)}, f32[32,8,64]{2,1,0:T(8,128)}, u32[]{:S(2)}) %copy-start) | copy-done | bytes 65560
  2.8 0.8 %copy-done.1 = bf16[32,8,64]{2,1,0:T(8,128)(2,1)S(1)} copy-done((bf16[32,8,64]{2,1,0:T(8,128)(2,1)S(1)}, bf16[32,8,64]{2,1,0:T(8,128)(2,1)}, u32[]{:S(2)}) %copy-start.1) | copy-done | bytes 32792
  3.7 1.8 %shard_map.85 = (f32[32,8,64]{2,1,0:T(8,128)}, f32[32,128]{1,0:T(8,128)}) custom-call(s32[1]{0:T(128)S(6)} %copy.18.count_ref, s32[1,32]{1,0:T(1,128)S(1)} %bitcast.34, f32[32,8,64]{2,1,0:T(8,128)S(1)} %copy-done, bf16[32,8,64]{2,1,0:T(8,128)(2,1)S(1)} %copy-done.1), custom_call_target="tpu_custom_call" | custom-call | flops 100000 | bytes 100000 | tf_op jit(solution)/shard_map/pallas_call | solution.py:326
  5.5 7.8 %all-to-all-start = ((f32[16,2,128]{2,1,0:T(2,128)}), f32[16,2,128]{2,1,0:T(2,128)S(1)}, u32[]{:S(2)}, u32[]{:S(2)}) async-start(f32[16,2,128]{2,1,0:T(2,128)} %bitcast.4), calls=%async_computation | async-start | bytes 32768 | tf_op jit(solution)/shard_map/all_to_all | solution.py:331
  13.2 6.2 %all-to-all-done = f32[16,2,128]{2,1,0:T(2,128)S(1)} async-done(((f32[16,2,128]{2,1,0:T(2,128)}), f32[16,2,128]{2,1,0:T(2,128)S(1)}, u32[]{:S(2)}, u32[]{:S(2)}) %all-to-all-start) | async-done | bytes 16416 | tf_op jit(solution)/shard_map/all_to_all | solution.py:331
  19.4 0.6 shard_map.86
  20.0 2.0 %all-gather = f32[4,8,16,128]{3,2,1,0:T(8,128)S(1)} all-gather(f32[2,8,16,128]{3,2,1,0:T(8,128)S(1)} %shard_map.86), channel_id=2, replica_groups=mesh['gx'=64,'gy'=8,'gz'=2] {'gz'}, dimensions={0}, use_global_device_ids=true | all-gather | bytes 393216 | tf_op jit(solution)/shard_map/all_gather | solution.py:313
  22.1 3.1 %collective-permute-start = (f32[2,2,8,8,128]{4,3,2,1,0:T(8,128)S(1)}, f32[2,2,8,8,128]{4,3,2,1,0:T(8,128)S(1)}, u32[]{:S(2)}, u32[]{:S(2)}) collective-permute-start(f32[2,2,8,8,128]{4,3,2,1,0:T(8,128)S(1)} %slice_select_fusion), channel_id=1, source_target_pairs={{0,2},{2,4},{3,1},{4,6},{5,3},{6,8},{7,5},{8,10},{9,7},{10,12},{11... | collective-permute-start | bytes 393224 | tf_op jit(solution)/shard_map/ppermute | solution.py:309
  25.2 2.9 %collective-permute-done = f32[2,2,8,8,128]{4,3,2,1,0:T(8,128)S(1)} collective-permute-done((f32[2,2,8,8,128]{4,3,2,1,0:T(8,128)S(1)}, f32[2,2,8,8,128]{4,3,2,1,0:T(8,128)S(1)}, u32[]{:S(2)}, u32[]{:S(2)}) %collective-permute-start) | collective-permute-done | bytes 131104 | tf_op jit(solution)/shard_map/ppermute | solution.py:309
  28.1 2.8 %all-gather.1 = f32[4,2,8,8,128]{4,3,2,1,0:T(8,128)S(1)} all-gather(f32[2,2,8,8,128]{4,3,2,1,0:T(8,128)S(1)} %collective-permute-done), channel_id=3, replica_groups=mesh['gx'=64,'gy'=8,'gz'=2] {'gz'}, dimensions={0}, use_global_device_ids=true | all-gather | bytes 393216 | tf_op jit(solution)/shard_map/all_gather | solution.py:313
  31.2 2.0 %collective-permute-start.1 = (f32[2,13,32,128]{3,2,1,0:T(8,128)S(1)}, f32[2,13,32,128]{3,2,1,0:T(8,128)S(1)}, u32[]{:S(2)}, u32[]{:S(2)}) collective-permute-start(f32[2,13,32,128]{3,2,1,0:T(8,128)S(1)} %maximum_select_fusion), channel_id=1, source_target_pairs={{0,16},{16,32},{17,1},{32,48},{33,17},{48,64},{49,33},{64,80},{65,... | collective-permute-start | bytes 1277960 | tf_op jit(solution)/shard_map/ppermute | solution.py:309
  33.2 0.1 pad_add_fusion.pos_ref
  33.2 8.0 %collective-permute-done.1 = f32[2,13,32,128]{3,2,1,0:T(8,128)S(1)} collective-permute-done((f32[2,13,32,128]{3,2,1,0:T(8,128)S(1)}, f32[2,13,32,128]{3,2,1,0:T(8,128)S(1)}, u32[]{:S(2)}, u32[]{:S(2)}) %collective-permute-start.1) | collective-permute-done | bytes 426016 | tf_op jit(solution)/shard_map/ppermute | solution.py:309
  41.3 2.7 %all-gather.2 = f32[4,13,32,128]{3,2,1,0:T(8,128)S(1)} all-gather(f32[2,13,32,128]{3,2,1,0:T(8,128)S(1)} %collective-permute-done.1), channel_id=4, replica_groups=mesh['gx'=64,'gy'=8,'gz'=2] {'gz'}, dimensions={0}, use_global_device_ids=true | all-gather | bytes 1277952 | tf_op jit(solution)/shard_map/all_gather | solution.py:313
  44.0 7.5 %shard_map.87 = (f32[8,16,128]{2,1,0:T(8,128)}, f32[6,4,128]{2,1,0:T(4,128)S(1)}) custom-call(s32[3]{0:T(128)S(1)} %pad_add_fusion.pos_ref, f32[2,2,8,32,128]{4,3,2,1,0:T(8,128)S(1)} %pad_maximum_fusion.full_ref, f32[2,2,13,32,128]{4,3,2,1,0:T(8,128)S(1)} %bitcast.30), custom_call_target="tpu_custom_call" | custom-call | flops 5000000 | bytes 5000000 | tf_op jit(solution)/shard_map/pallas_call | solution.py:343
  51.5 1.9 %collective-permute-start.2 = (f32[6,4,128]{2,1,0:T(4,128)S(1)}, f32[6,4,128]{2,1,0:T(4,128)S(1)}, u32[]{:S(2)}, u32[]{:S(2)}) collective-permute-start(f32[6,4,128]{2,1,0:T(4,128)S(1)} %get-tuple-element.10), channel_id=1, source_target_pairs={{0,2},{2,4},{3,1},{4,6},{5,3},{6,8},{7,5},{8,10},{9,7},{10,12},{11... | collective-permute-start | bytes 36872 | tf_op jit(solution)/shard_map/ppermute | solution.py:309
  53.5 2.5 %collective-permute-done.2 = f32[6,4,128]{2,1,0:T(4,128)S(1)} collective-permute-done((f32[6,4,128]{2,1,0:T(4,128)S(1)}, f32[6,4,128]{2,1,0:T(4,128)S(1)}, u32[]{:S(2)}, u32[]{:S(2)}) %collective-permute-start.2) | collective-permute-done | bytes 12320 | tf_op jit(solution)/shard_map/ppermute | solution.py:309
  56.0 3.0 %all-gather.3 = f32[12,4,128]{2,1,0:T(4,128)S(1)} all-gather(f32[6,4,128]{2,1,0:T(4,128)S(1)} %collective-permute-done.2), channel_id=5, replica_groups=mesh['gx'=64,'gy'=8,'gz'=2] {'gz'}, dimensions={0}, use_global_device_ids=true | all-gather | bytes 36864 | tf_op jit(solution)/shard_map/all_gather | solution.py:313
  59.0 8.2 %collective-permute-start.4 = (f32[3,6,4,128]{3,2,1,0:T(4,128)S(1)}, f32[3,6,4,128]{3,2,1,0:T(4,128)S(1)}, u32[]{:S(2)}, u32[]{:S(2)}) collective-permute-start(f32[3,6,4,128]{3,2,1,0:T(4,128)S(1)} %pad_maximum_fusion.2.mid_ref), channel_id=1, source_target_pairs={{0,32},{16,48},{32,64},{33,1},{48,80},{49,17},{64,96},{65,33},{80,... | collective-permute-start | bytes 110600 | tf_op jit(solution)/shard_map/ppermute | solution.py:309
  67.2 2.9 %collective-permute-start.3 = (f32[3,6,4,128]{3,2,1,0:T(4,128)S(1)}, f32[3,6,4,128]{3,2,1,0:T(4,128)S(1)}, u32[]{:S(2)}, u32[]{:S(2)}) collective-permute-start(f32[3,6,4,128]{3,2,1,0:T(4,128)S(1)} %pad_maximum_fusion.2.mid_ref), channel_id=1, source_target_pairs={{0,16},{16,32},{17,1},{32,48},{33,17},{48,64},{49,33},{64,80},{65,... | collective-permute-start | bytes 110600 | tf_op jit(solution)/shard_map/ppermute | solution.py:309
  70.1 3.0 %collective-permute-done.3 = f32[3,6,4,128]{3,2,1,0:T(4,128)S(1)} collective-permute-done((f32[3,6,4,128]{3,2,1,0:T(4,128)S(1)}, f32[3,6,4,128]{3,2,1,0:T(4,128)S(1)}, u32[]{:S(2)}, u32[]{:S(2)}) %collective-permute-start.3) | collective-permute-done | bytes 36896 | tf_op jit(solution)/shard_map/ppermute | solution.py:309
  73.1 1.9 %all-gather.4 = f32[4,3,6,4,128]{4,3,2,1,0:T(4,128)S(1)} all-gather(f32[2,3,6,4,128]{4,3,2,1,0:T(4,128)S(1)} %pad_maximum_fusion.1), channel_id=6, replica_groups=mesh['gx'=64,'gy'=8,'gz'=2] {'gz'}, dimensions={0}, use_global_device_ids=true | all-gather | bytes 221184 | tf_op jit(solution)/shard_map/all_gather | solution.py:313
  75.1 1.8 %shard_map.88 = f32[1,2,16]{2,1,0:T(2,128)} custom-call(s32[3]{0:T(128)S(1)} %pad_add_fusion.pos_ref, f32[3,6,4,128]{3,2,1,0:T(4,128)S(1)} %pad_maximum_fusion.2.mid_ref, f32[2,2,3,6,4,128]{5,4,3,2,1,0:T(4,128)S(1)} %bitcast.31), custom_call_target="tpu_custom_call" | custom-call | flops 100000 | bytes 100000 | tf_op jit(solution)/shard_map/pallas_call | solution.py:355
  (17 shorter events, 0.3 us)
Async XLA Ops:
  1.3 0.7 copy-start.4
  1.9 0.9 %copy-start = (f32[32,8,64]{2,1,0:T(8,128)S(1)}, f32[32,8,64]{2,1,0:T(8,128)}, u32[]{:S(2)}) copy-start(f32[32,8,64]{2,1,0:T(8,128)} %rhs_ref.2) | copy-start | bytes 196612
  2.8 0.8 %copy-start.1 = (bf16[32,8,64]{2,1,0:T(8,128)(2,1)S(1)}, bf16[32,8,64]{2,1,0:T(8,128)(2,1)}, u32[]{:S(2)}) copy-start(bf16[32,8,64]{2,1,0:T(8,128)(2,1)} %coef_ref.2) | copy-start | bytes 98308
  3.7 15.8 %copy-start.2 = (f32[8,16,128]{2,1,0:T(8,128)S(1)}, f32[8,16,128]{2,1,0:T(8,128)}, u32[]{:S(2)}) copy-start(f32[8,16,128]{2,1,0:T(8,128)} %rhs_ref.3) | copy-start | bytes 196612
  5.5 14.0 %copy-start.3 = (bf16[8,16,128]{2,1,0:T(8,128)(2,1)S(1)}, bf16[8,16,128]{2,1,0:T(8,128)(2,1)}, u32[]{:S(2)}) copy-start(bf16[8,16,128]{2,1,0:T(8,128)(2,1)} %coef_ref.3) | copy-start | bytes 98308
  5.5 14.0 %all-to-all-start = ((f32[16,2,128]{2,1,0:T(2,128)}), f32[16,2,128]{2,1,0:T(2,128)S(1)}, u32[]{:S(2)}, u32[]{:S(2)}) async-start(f32[16,2,128]{2,1,0:T(2,128)} %bitcast.4), calls=%async_computation | async-start | bytes 32768 | tf_op jit(solution)/shard_map/all_to_all | solution.py:331
  22.1 6.0 %collective-permute-start = (f32[2,2,8,8,128]{4,3,2,1,0:T(8,128)S(1)}, f32[2,2,8,8,128]{4,3,2,1,0:T(8,128)S(1)}, u32[]{:S(2)}, u32[]{:S(2)}) collective-permute-start(f32[2,2,8,8,128]{4,3,2,1,0:T(8,128)S(1)} %slice_select_fusion), channel_id=1, source_target_pairs={{0,2},{2,4},{3,1},{4,6},{5,3},{6,8},{7,5},{8,10},{9,7},{10,12},{11... | collective-permute-start | bytes 393224 | tf_op jit(solution)/shard_map/ppermute | solution.py:309
  31.2 10.1 %collective-permute-start.1 = (f32[2,13,32,128]{3,2,1,0:T(8,128)S(1)}, f32[2,13,32,128]{3,2,1,0:T(8,128)S(1)}, u32[]{:S(2)}, u32[]{:S(2)}) collective-permute-start(f32[2,13,32,128]{3,2,1,0:T(8,128)S(1)} %maximum_select_fusion), channel_id=1, source_target_pairs={{0,16},{16,32},{17,1},{32,48},{33,17},{48,64},{49,33},{64,80},{65,... | collective-permute-start | bytes 1277960 | tf_op jit(solution)/shard_map/ppermute | solution.py:309
  51.5 4.4 %collective-permute-start.2 = (f32[6,4,128]{2,1,0:T(4,128)S(1)}, f32[6,4,128]{2,1,0:T(4,128)S(1)}, u32[]{:S(2)}, u32[]{:S(2)}) collective-permute-start(f32[6,4,128]{2,1,0:T(4,128)S(1)} %get-tuple-element.10), channel_id=1, source_target_pairs={{0,2},{2,4},{3,1},{4,6},{5,3},{6,8},{7,5},{8,10},{9,7},{10,12},{11... | collective-permute-start | bytes 36872 | tf_op jit(solution)/shard_map/ppermute | solution.py:309
  59.0 11.1 %collective-permute-start.4 = (f32[3,6,4,128]{3,2,1,0:T(4,128)S(1)}, f32[3,6,4,128]{3,2,1,0:T(4,128)S(1)}, u32[]{:S(2)}, u32[]{:S(2)}) collective-permute-start(f32[3,6,4,128]{3,2,1,0:T(4,128)S(1)} %pad_maximum_fusion.2.mid_ref), channel_id=1, source_target_pairs={{0,32},{16,48},{32,64},{33,1},{48,80},{49,17},{64,96},{65,33},{80,... | collective-permute-start | bytes 110600 | tf_op jit(solution)/shard_map/ppermute | solution.py:309
  67.2 5.9 %collective-permute-start.3 = (f32[3,6,4,128]{3,2,1,0:T(4,128)S(1)}, f32[3,6,4,128]{3,2,1,0:T(4,128)S(1)}, u32[]{:S(2)}, u32[]{:S(2)}) collective-permute-start(f32[3,6,4,128]{3,2,1,0:T(4,128)S(1)} %pad_maximum_fusion.2.mid_ref), channel_id=1, source_target_pairs={{0,16},{16,32},{17,1},{32,48},{33,17},{48,64},{49,33},{64,80},{65,... | collective-permute-start | bytes 110600 | tf_op jit(solution)/shard_map/ppermute | solution.py:309

commit v2 on v1

--- a/solution.py
+++ b/solution.py
@@ -31,10 +31,24 @@
     return pltpu.roll(values, 1, axis)
 
 
-def fine_kernel(count_ref, target_ref, rhs_ref, coef_ref, solved_ref, send_ref):
+def inverse(values):
+    guess = pl.reciprocal(values, approx=True)
+    return guess * (2.0 - values * guess)
+
+
+def fine_kernel(
+    count_ref, target_hbm, rhs_hbm, coef_hbm, solved_ref, send_ref, target_ref, rhs_ref, coef_ref, sems
+):
     live = count_ref[0]
+    loads = [
+        pltpu.make_async_copy(coef_hbm, coef_ref, sems.at[0]),
+        pltpu.make_async_copy(rhs_hbm, rhs_ref, sems.at[1]),
+        pltpu.make_async_copy(target_hbm, target_ref, sems.at[2]),
+    ]
+    for load in loads:
+        load.start()
     half = rhs_ref.shape[0] // 2
-    source = jnp.concatenate([rhs_ref[:half], rhs_ref[half:]], axis=2)
+    loads[0].wait()
     k = coef_ref[...].astype(F32) * 0.5
     h = jnp.concatenate([k[:half], k[half:]], axis=2)
     shape = h.shape
@@ -60,17 +74,18 @@
         total += wy * wrapped(u, -8) + wrapped(wy * u, 8)
         return total + wz * wrapped(u, -1) + wrapped(wz * u, 1)
 
-    scale = DAMPING / diagonal
+    scale = DAMPING * inverse(diagonal)
+    loads[1].wait()
+    source = jnp.concatenate([rhs_ref[:half], rhs_ref[half:]], axis=2)
     first = source * scale
     second = first + scale * (REST * source + sides(first))
     residue = source - diagonal * second + sides(second)
-    slot = iota((half, 8, 64), 0)
-    solved_ref[:half] = jnp.where(slot < live, second[:, :, :64], 0.0)
-    solved_ref[half:] = jnp.where(slot + half < live, second[:, :, 64:], 0.0)
-
+    solved_ref[...] = second
+
+    loads[2].wait()
     square = (128, 128)
     row, col = iota(square, 0), iota(square, 1)
-    iz, ix, iy = col >> 4, (col >> 2) & 3, col & 3
+    iz, ix, iy = (col >> 4) & 3, (col >> 2) & 3, col & 3
     match = (((row >> 4) & 3) == iy) & (((row >> 1) & 3) == iz)
     keep = ((row >> 1) & 3) == ix
     cells = residue.reshape(square)
@@ -83,47 +98,97 @@
     spread = jnp.where(iota(wide, 0) == (iota(wide, 1) >> 3), 1.0, 0.0)
     names = jnp.broadcast_to(target_ref[...].astype(F32), (8, 32))
     name = (dot(names, spread)[:1] + 0.5).astype(jnp.int32)
+    names = jnp.broadcast_to(name, wide)
     row, col = iota(wide, 0), iota(wide, 1)
-    name = jnp.broadcast_to(name, wide)
-    own = jnp.sum(jnp.where(col == row * 8, name, 0).astype(F32), axis=1, keepdims=True)
+    own = jnp.sum(jnp.where(col == row * 8, names, 0).astype(F32), axis=1, keepdims=True)
     own = own.astype(jnp.int32)
-    earlier = ((own >> 8) == (name >> 8)) & (row < (col >> 3))
+    earlier = ((own >> 8) == (names >> 8)) & (row < (col >> 3))
     rank = jnp.sum(jnp.where(earlier, 1.0, 0.0), axis=0, keepdims=True).astype(jnp.int32)
-    place = (name >> 8) * 2 + rank
-    chosen = (place == row) & ((col >> 3) < live)
-    picked = jnp.where(chosen, 1.0, 0.0)
-    tag = jnp.where(chosen & ((col & 7) == 0), (name & 255) + 1, 0).astype(F32)
-    tag = jnp.sum(tag, axis=1, keepdims=True)
-    packed = dot(picked[:, :128], parts[0]) + dot(picked[:, 128:], parts[1])
-    send_ref[...] = jnp.where(iota(packed.shape, 1) < 64, packed, tag)
-
-
-def place_kernel(got_ref, rhs_ref, coef_ref, out_ref):
-    got = got_ref[...]
-    four = jnp.concatenate([got, got, got, got], axis=0)
+    wide = (128, 256)
+    row, col = iota(wide, 0), iota(wide, 1)
+    chip = (row >> 4) + ((row >> 1) & 3) - 1
+    owner = chip * 2 + (row & 1)
+    wanted = ((row & 7) < 6) & (chip >= 0) & (chip < 8) & ((col >> 3) < live)
+    chosen = wanted & (owner == (name >> 8))
+    packed, tags = [], []
+    for number in range(2):
+        mine = chosen & (rank == number)
+        picked = jnp.where(mine, 1.0, 0.0)
+        packed.append(dot(picked[:, :128], parts[0]) + dot(picked[:, 128:], parts[1]))
+        tag = jnp.where(mine & ((col & 7) == 0), (name & 255) + 1, 0).astype(F32)
+        tags.append(jnp.sum(tag, axis=1, keepdims=True))
+    row, col = iota(square, 0), iota(square, 1)
+    place = (row & 7) * 2
+    tags = jnp.where(col == place, tags[0], 0.0) + jnp.where(col == place + 1, tags[1], 0.0)
+    lift = jnp.where(((row & 7) == 6) & ((row >> 3) == (col >> 3)), 1.0, 0.0)
+    send_ref[...] = jnp.where(col < 64, packed[0], packed[1]) + dot(lift, tags)
+
+
+def store_kernel(count_ref, second_ref, solved_ref):
+    live = count_ref[0]
+    second = second_ref[...]
+    half = second.shape[0]
+    slot = iota((half, 8, 64), 0)
+    solved_ref[:half] = jnp.where(slot < live, second[:, :, :64], 0.0)
+    solved_ref[half:] = jnp.where(slot + half < live, second[:, :, 64:], 0.0)
+
+
+def place_kernel(pos_ref, got_ref, chip_ref, full_ref, pay_ref):
+    tags = got_ref[pl.ds(6, 16, stride=8), :]
     square = (128, 128)
     row, col = iota(square, 0), iota(square, 1)
-    slices = jnp.where((col >> 4) == (row >> 5), four, 0.0)
-    cell = (((row >> 4) & 3) << 2) + (row & 3)
-    select = jnp.where(((col & 15) == cell) & (col < 64), 1.0, 0.0)
+    rank = (row >> 4) & 1
+    mask = (col >> 4) == rank * 4 + (row >> 5)
     turned = (((1,), (1,)), ((), ()))
-    left = lax.dot_general(select, slices, turned, precision=PRECISE, preferred_element_type=F32)
-    only = jnp.where(iota((8, 128), 1) == 64, 1.0, 0.0)
-    tags = lax.dot_general(only, four, turned, precision=PRECISE, preferred_element_type=F32)
-    tags = (tags[:1] + 0.5).astype(jnp.int32) - 1
-    tags = jnp.broadcast_to(tags, square)
-    here = ((tags >> 7) == (row >> 6)) & (((tags >> 5) & 3) == ((row >> 2) & 3))
-    down = (four[:, 64:65] + 0.5).astype(jnp.int32) - 1
-    right = jnp.where(((down & 31) == (col >> 2)) & ((col & 3) == (row >> 5)), 1.0, 0.0)
-    placed = dot(jnp.where(here, left, 0.0), right)
-    covered = jnp.dot(
-        jnp.where(here, 1.0, 0.0).astype(jnp.bfloat16),
-        right.astype(jnp.bfloat16),
-        preferred_element_type=F32,
-    )
-    shape = rhs_ref.shape
-    out_ref[0] = jnp.where(covered.reshape(shape) > 0.5, placed.reshape(shape), rhs_ref[...])
-    out_ref[1] = coef_ref[...].astype(F32) * 0.5
+    tall = jnp.concatenate([tags] * 8, axis=0)
+    ones = jnp.ones((8, 128), F32)
+
+    def place(number, first_row, rows):
+        got = got_ref[pl.ds(number, 16, stride=8), :]
+        slices = jnp.where(mask, jnp.concatenate([got] * 8, axis=0), 0.0)
+        shape = (8 * rows, 128)
+        shift = rows.bit_length() - 1
+        r, c = iota(shape, 0), iota(shape, 1)
+        x, y = r >> shift, (r & (rows - 1)) + first_row
+        select = jnp.where((c & 15) == (x & 3) * 4 + (y & 3), 1.0, 0.0)
+        left = lax.dot_general(
+            select, slices, turned, precision=PRECISE, preferred_element_type=F32
+        )
+        named = jnp.where(col == 2 * number + rank, tall, 0.0)
+        across = lax.dot_general(
+            ones, named, turned, precision=PRECISE, preferred_element_type=F32
+        )
+        across = (across[:1] + 0.5).astype(jnp.int32) - 1
+        here = ((across >> 7) == (x >> 2)) & (((across >> 5) & 3) == (y >> 2))
+        down = (jnp.sum(named, axis=1, keepdims=True) + 0.5).astype(jnp.int32) - 1
+        right = jnp.where(((down & 31) == (col >> 2)) & ((col & 3) == (row >> 5)), 1.0, 0.0)
+        placed = dot(jnp.where(here, left, 0.0), right)
+        covered = jnp.dot(
+            jnp.where(here, 1.0, 0.0).astype(jnp.bfloat16),
+            right.astype(jnp.bfloat16),
+            preferred_element_type=F32,
+        )
+        return placed.reshape(8, rows, 128), covered.reshape(8, rows, 128) > 0.5
+
+    core = pos_ref[2]
+    for number in range(2):
+        for part, (first_row, rows, start) in enumerate(((8, 8, 0), (0, 16, 8), (0, 8, 24))):
+            placed, covered = place(2 * part + number, first_row, rows)
+            lines = slice(start, start + rows)
+            full_ref[number, 0, :, lines] = jnp.where(covered, placed, chip_ref[number, 0, :, lines])
+        full_ref[number, 1] = chip_ref[number, 1]
+
+    @pl.when(core == 0)
+    def _():
+        for number in range(2):
+            pay_ref[number, 0:6] = full_ref[number, 0, 2:8]
+            pay_ref[number, 6:13] = full_ref[number, 1, 1:8]
+
+    @pl.when(core != 0)
+    def _():
+        for number in range(2):
+            pay_ref[number, 0:6] = full_ref[number, 0, 0:6]
+            pay_ref[number, 6:13] = full_ref[number, 1, 0:7]
 
 
 def pair_matrix(size):
@@ -138,7 +203,7 @@
     hz = jnp.where(lane < depth - 1, after(mid, 2), 0.0)
     diagonal = 6.0 * mid + h[:-2] + h[2:] + hy + before(mid, 1) + hz
     diagonal += jnp.where(lane > 0, before(mid, 2), 0.0)
-    scale = jnp.where(inside & (lane < depth), DAMPING / diagonal, 0.0)
+    scale = jnp.where(inside & (lane < depth), DAMPING * inverse(diagonal), 0.0)
     wx = h[:-1] + h[1:]
     wy = mid + hy
     wz = jnp.where(lane < depth - 1, mid + hz, 0.0)
@@ -197,7 +262,7 @@
         diagonal += jnp.where(lane > 0, before(h, 1), 0.0)
         x = gx * 8 + layer - 6
         inside = rows_in & (x >= 0) & (x < sizes[0])
-        scale = jnp.where(inside, DAMPING / diagonal, 0.0)
+        scale = jnp.where(inside, DAMPING * inverse(diagonal), 0.0)
         diag_ref[layer] = diagonal
         scale_ref[layer] = scale
         wx_ref[layer] = h + above
@@ -309,6 +374,13 @@
     return lax.ppermute(values, (axis, "gz"), pairs)
 
 
+def exchanged(up, down, axis):
+    count = lax.axis_size(axis)
+    pairs = [(place, place + 1) for place in range(count - 1)]
+    back = [(target, source) for source, target in pairs]
+    return lax.ppermute(up, axis, pairs), lax.ppermute(down, axis, back)
+
+
 def shared(values):
     return lax.all_gather(values, "gz")
 
@@ -323,22 +395,31 @@
     vmem = pl.BlockSpec(memory_space=pltpu.VMEM)
     smem = pl.BlockSpec(memory_space=pltpu.SMEM)
     struct = jax.ShapeDtypeStruct
-    fine_solution, send = call(
+    anywhere = pl.BlockSpec(memory_space=pl.ANY)
+    second, send = call(
         fine_kernel,
-        (struct(fine_rhs.shape, F32), struct((32, 128), F32)),
-        [smem, vmem, vmem, vmem],
+        (struct((16, 8, 128), F32), struct((128, 128), F32)),
+        [smem, anywhere, anywhere, anywhere],
+        [
+            pltpu.VMEM((1, 32), jnp.int32),
+            pltpu.VMEM(fine_rhs.shape, F32),
+            pltpu.VMEM(fine_coef.shape, fine_coef.dtype),
+            pltpu.SemaphoreType.DMA((3,)),
+        ],
     )(patch_count, patch_target.reshape(1, 32), fine_rhs, fine_coef)
-    got = lax.all_to_all(send.reshape(16, 2, 128), ("gy", "gz"), 0, 0).reshape(32, 128)
-    both = call(place_kernel, struct((2, 8, 16, 128), F32), [vmem, vmem, vmem])(
-        got, coarse_rhs, coarse_coef
+    got = lax.all_to_all(send.reshape(16, 8, 128), ("gy", "gz"), 0, 0).reshape(128, 128)
+    fine_solution = call(store_kernel, struct(fine_rhs.shape, F32), [smem, vmem])(
+        patch_count, second
     )
-    chip = shared(both)
-    rows = jnp.where(core == 0, chip[:, :, :, 8:], chip[:, :, :, :8])
-    halo = shared(split_send(rows, "gy", 1))
-    full = jnp.concatenate([halo[0], chip, halo[1]], axis=3)
-    high = jnp.concatenate([full[:, 0, 2:], full[:, 1, 1:]], axis=1)
-    low = jnp.concatenate([full[:, 0, :6], full[:, 1, :7]], axis=1)
-    side = shared(split_send(jnp.where(core == 0, high, low), "gx", 1))
+    own = jnp.stack([coarse_rhs, coarse_coef.astype(F32) * 0.5])
+    below, above = exchanged(own[:, :, 8:], own[:, :, :8], "gy")
+    chip = shared(jnp.concatenate([below, own, above], axis=2))
+    full, pay = call(
+        place_kernel,
+        (struct((2, 2, 8, 32, 128), F32), struct((2, 13, 32, 128), F32)),
+        [smem, vmem, vmem],
+    )(pos, got, chip)
+    side = shared(split_send(pay, "gx", 1))
     grid = (32, 256)
     coarse_solution, pay = call(
         functools.partial(base_kernel, sizes),

time: 77.3 us -> 76.6 us (level)
  the two profiles are of different devices: /device:TPU:51 before, /device:TPU:515 now
where the time goes in v2:
time: 76.6 us; the launch traced here: 76.2 us
  starting transfers between devices  26.7 us (35%)
  blocking collectives  16.4 us (21%)
  Pallas kernels  15.6 us (20%)
  waiting for transfers between devices  14.4 us (19%)
  between operations  1.4 us (2%)
  other arithmetic  0.93 us (1%)
    all_gather x4, blocking collectives, shared(): return lax.all_gather(values, 'gz')  16.4 us
    ppermute x4, starting transfers between devices, split_send(): return lax.ppermute(values, (axis, 'gz'), pairs)  11.9 us
    ppermute x4, waiting for transfers between devices, split_send(): return lax.ppermute(values, (axis, 'gz'), pairs)  10.1 us
    all_to_all x1, starting transfers between devices, per_device(): lax.all_to_all(send.reshape(16, 8, 128), ('gy', 'gz'), 0, 0)  9.41 us
    pallas_call x1, Pallas kernels, per_device(): call(functools.partial(base_kernel, sizes), (struct((8, 16, 128), F32), s...  7.61 us
    ppermute x2, starting transfers between devices, exchanged(): return (lax.ppermute(up, axis, pairs), lax.ppermute(down, axis, back))  5.41 us
    all_to_all x1, waiting for transfers between devices, per_device(): lax.all_to_all(send.reshape(16, 8, 128), ('gy', 'gz'), 0, 0)  4.33 us
    pallas_call x1, Pallas kernels, per_device(): call(place_kernel, (struct((2, 2, 8, 32, 128), F32), struct((2, 13, 32, 1...  3.14 us
  transfers between devices with their start and end apart: 7, of which 4 were waited for; matrix products, arithmetic and copies ran while one was open for 0% of the time, Pallas kernels for 4%

profile of v2, /device:TPU:515, one launch (start us, length us, event | category | flops | bytes accessed | tf_op | source)
XLA Modules:
  0.0 76.2 jit_solution(14805469770149117931)
XLA Ops:
  0.6 0.8 %multiply_bitcast_fusion = f32[1,8,16,128]{3,2,1,0:T(8,128)S(1)} fusion(bf16[8,16,128]{2,1,0:T(8,128)(2,1)} %param.9), kind=kLoop, calls=%fused_computation.6 | loop fusion | flops 32768 | bytes 98304 | tf_op jit(solution)/shard_map/stack | solution.py:414
  1.4 0.0 copy-done.3
  1.5 3.3 %collective-permute-start = (f32[2,8,8,128]{3,2,1,0:T(8,128)S(1)}, f32[2,8,8,128]{3,2,1,0:T(8,128)S(1)}, u32[]{:S(2)}, u32[]{:S(2)}) collective-permute-start(f32[2,8,8,128]{3,2,1,0:T(8,128)S(1)} %get-tuple-element.15), channel_id=1, source_target_pairs={{0,2},{2,4},{4,6},{6,8},{8,10},{10,12},{12,14},{1,3},{3,5},{5,7},{... | collective-permute-start | bytes 196616 | tf_op jit(solution)/shard_map/ppermute | solution.py:381
  4.7 2.2 %collective-permute-start.1 = (f32[2,8,8,128]{3,2,1,0:T(8,128)S(1)}, f32[2,8,8,128]{3,2,1,0:T(8,128)S(1)}, u32[]{:S(2)}, u32[]{:S(2)}) collective-permute-start(f32[2,8,8,128]{3,2,1,0:T(8,128)S(1)} %get-tuple-element.16), channel_id=1, source_target_pairs={{2,0},{4,2},{6,4},{8,6},{10,8},{12,10},{14,12},{3,1},{5,3},{7,5},{... | collective-permute-start | bytes 196616 | tf_op jit(solution)/shard_map/ppermute | solution.py:381
  7.6 0.6 copy-done.2
  8.2 2.3 %shard_map.85 = (f32[16,8,128]{2,1,0:T(8,128)S(1)}, f32[128,128]{1,0:T(8,128)}) custom-call(s32[1]{0:T(128)S(6)} %copy.9.count_ref, s32[1,32]{1,0:T(1,128)S(1)} %bitcast.24, f32[32,8,64]{2,1,0:T(8,128)S(1)} %copy-done, bf16[32,8,64]{2,1,0:T(8,128)(2,1)S(1)} %copy-done.1), custom_call_target="tpu_custom_call" | custom-call | flops 100000 | bytes 100000 | tf_op jit(solution)/shard_map/pallas_call | solution.py:399
  10.6 9.4 %all-to-all-start = ((f32[16,8,128]{2,1,0:T(8,128)}), f32[16,8,128]{2,1,0:T(8,128)S(1)}, u32[]{:S(2)}, u32[]{:S(2)}) async-start(f32[16,8,128]{2,1,0:T(8,128)} %bitcast.4), calls=%async_computation | async-start | bytes 131072 | tf_op jit(solution)/shard_map/all_to_all | solution.py:410
  20.0 0.1 pad_add_fusion.pos_ref
  20.1 2.2 %all-gather = f32[4,8,32,128]{3,2,1,0:T(8,128)S(1)} all-gather(f32[2,8,32,128]{3,2,1,0:T(8,128)S(1)} %pad_maximum_fusion), channel_id=2, replica_groups=mesh['gx'=64,'gy'=8,'gz'=2] {'gz'}, dimensions={0}, use_global_device_ids=true | all-gather | bytes 786432 | tf_op jit(solution)/shard_map/all_gather | solution.py:385
  22.3 4.3 %all-to-all-done = f32[16,8,128]{2,1,0:T(8,128)S(1)} async-done(((f32[16,8,128]{2,1,0:T(8,128)}), f32[16,8,128]{2,1,0:T(8,128)S(1)}, u32[]{:S(2)}, u32[]{:S(2)}) %all-to-all-start) | async-done | bytes 65568 | tf_op jit(solution)/shard_map/all_to_all | solution.py:410
  26.6 3.1 %shard_map.87 = (f32[2,2,8,32,128]{4,3,2,1,0:T(8,128)S(1)}, f32[2,13,32,128]{3,2,1,0:T(8,128)S(1)}) custom-call(s32[3]{0:T(128)S(1)} %pad_add_fusion.pos_ref, f32[128,128]{1,0:T(8,128)S(1)} %bitcast.22, f32[2,2,8,32,128]{4,3,2,1,0:T(8,128)S(1)} %bitcast.20), custom_call_target="tpu_custom_call" | custom-call | flops 100000 | bytes 100000 | tf_op jit(solution)/shard_map/pallas_call | solution.py:417
  29.8 4.1 %collective-permute-start.2 = (f32[2,13,32,128]{3,2,1,0:T(8,128)S(1)}, f32[2,13,32,128]{3,2,1,0:T(8,128)S(1)}, u32[]{:S(2)}, u32[]{:S(2)}) collective-permute-start(f32[2,13,32,128]{3,2,1,0:T(8,128)S(1)} %get-tuple-element.12), channel_id=1, source_target_pairs={{0,16},{16,32},{17,1},{32,48},{33,17},{48,64},{49,33},{64,80},{65,... | collective-permute-start | bytes 1277960 | tf_op jit(solution)/shard_map/ppermute | solution.py:374
  33.8 5.1 %collective-permute-done.2 = f32[2,13,32,128]{3,2,1,0:T(8,128)S(1)} collective-permute-done((f32[2,13,32,128]{3,2,1,0:T(8,128)S(1)}, f32[2,13,32,128]{3,2,1,0:T(8,128)S(1)}, u32[]{:S(2)}, u32[]{:S(2)}) %collective-permute-start.2) | collective-permute-done | bytes 426016 | tf_op jit(solution)/shard_map/ppermute | solution.py:374
  38.9 6.5 %all-gather.1 = f32[4,13,32,128]{3,2,1,0:T(8,128)S(1)} all-gather(f32[2,13,32,128]{3,2,1,0:T(8,128)S(1)} %collective-permute-done.2), channel_id=3, replica_groups=mesh['gx'=64,'gy'=8,'gz'=2] {'gz'}, dimensions={0}, use_global_device_ids=true | all-gather | bytes 1277952 | tf_op jit(solution)/shard_map/all_gather | solution.py:385
  45.4 7.6 %shard_map.88 = (f32[8,16,128]{2,1,0:T(8,128)}, f32[6,4,128]{2,1,0:T(4,128)S(1)}) custom-call(s32[3]{0:T(128)S(1)} %pad_add_fusion.pos_ref, f32[2,2,8,32,128]{4,3,2,1,0:T(8,128)S(1)} %get-tuple-element.11.full_ref, f32[2,2,13,32,128]{4,3,2,1,0:T(8,128)S(1)} %bitcast.19), custom_call_target="tpu_custom_call" | custom-call | flops 5000000 | bytes 5000000 | tf_op jit(solution)/shard_map/pallas_call | solution.py:424
  53.0 3.1 %collective-permute-start.3 = (f32[6,4,128]{2,1,0:T(4,128)S(1)}, f32[6,4,128]{2,1,0:T(4,128)S(1)}, u32[]{:S(2)}, u32[]{:S(2)}) collective-permute-start(f32[6,4,128]{2,1,0:T(4,128)S(1)} %get-tuple-element.14), channel_id=1, source_target_pairs={{0,2},{2,4},{3,1},{4,6},{5,3},{6,8},{7,5},{8,10},{9,7},{10,12},{11... | collective-permute-start | bytes 36872 | tf_op jit(solution)/shard_map/ppermute | solution.py:374
  56.1 1.4 %collective-permute-done.3 = f32[6,4,128]{2,1,0:T(4,128)S(1)} collective-permute-done((f32[6,4,128]{2,1,0:T(4,128)S(1)}, f32[6,4,128]{2,1,0:T(4,128)S(1)}, u32[]{:S(2)}, u32[]{:S(2)}) %collective-permute-start.3) | collective-permute-done | bytes 12320 | tf_op jit(solution)/shard_map/ppermute | solution.py:374
  57.4 3.0 %all-gather.2 = f32[12,4,128]{2,1,0:T(4,128)S(1)} all-gather(f32[6,4,128]{2,1,0:T(4,128)S(1)} %collective-permute-done.3), channel_id=4, replica_groups=mesh['gx'=64,'gy'=8,'gz'=2] {'gz'}, dimensions={0}, use_global_device_ids=true | all-gather | bytes 36864 | tf_op jit(solution)/shard_map/all_gather | solution.py:385
  60.4 2.8 %collective-permute-start.4 = (f32[3,6,4,128]{3,2,1,0:T(4,128)S(1)}, f32[3,6,4,128]{3,2,1,0:T(4,128)S(1)}, u32[]{:S(2)}, u32[]{:S(2)}) collective-permute-start(f32[3,6,4,128]{3,2,1,0:T(4,128)S(1)} %pad_maximum_fusion.3.mid_ref), channel_id=1, source_target_pairs={{0,16},{16,32},{17,1},{32,48},{33,17},{48,64},{49,33},{64,80},{65,... | collective-permute-start | bytes 110600 | tf_op jit(solution)/shard_map/ppermute | solution.py:374
  63.2 1.9 %collective-permute-start.5 = (f32[3,6,4,128]{3,2,1,0:T(4,128)S(1)}, f32[3,6,4,128]{3,2,1,0:T(4,128)S(1)}, u32[]{:S(2)}, u32[]{:S(2)}) collective-permute-start(f32[3,6,4,128]{3,2,1,0:T(4,128)S(1)} %pad_maximum_fusion.3.mid_ref), channel_id=1, source_target_pairs={{0,32},{16,48},{32,64},{33,1},{48,80},{49,17},{64,96},{65,33},{80,... | collective-permute-start | bytes 110600 | tf_op jit(solution)/shard_map/ppermute | solution.py:374
  65.2 0.7 shard_map.86
  65.9 3.6 %collective-permute-done.5 = f32[3,6,4,128]{3,2,1,0:T(4,128)S(1)} collective-permute-done((f32[3,6,4,128]{3,2,1,0:T(4,128)S(1)}, f32[3,6,4,128]{3,2,1,0:T(4,128)S(1)}, u32[]{:S(2)}, u32[]{:S(2)}) %collective-permute-start.5) | collective-permute-done | bytes 36896 | tf_op jit(solution)/shard_map/ppermute | solution.py:374
  69.6 4.8 %all-gather.3 = f32[4,3,6,4,128]{4,3,2,1,0:T(4,128)S(1)} all-gather(f32[2,3,6,4,128]{4,3,2,1,0:T(4,128)S(1)} %pad_maximum_fusion.1), channel_id=5, replica_groups=mesh['gx'=64,'gy'=8,'gz'=2] {'gz'}, dimensions={0}, use_global_device_ids=true | all-gather | bytes 221184 | tf_op jit(solution)/shard_map/all_gather | solution.py:385
  74.3 1.8 %shard_map.89 = f32[1,2,16]{2,1,0:T(2,128)} custom-call(s32[3]{0:T(128)S(1)} %pad_add_fusion.pos_ref, f32[3,6,4,128]{3,2,1,0:T(4,128)S(1)} %pad_maximum_fusion.3.mid_ref, f32[2,2,3,6,4,128]{5,4,3,2,1,0:T(4,128)S(1)} %bitcast.21), custom_call_target="tpu_custom_call" | custom-call | flops 100000 | bytes 100000 | tf_op jit(solution)/shard_map/pallas_call | solution.py:436
  (14 shorter events, 0.1 us)
Async XLA Ops:
  0.6 0.8 %copy-start.3 = (f32[8,16,128]{2,1,0:T(8,128)S(1)}, f32[8,16,128]{2,1,0:T(8,128)}, u32[]{:S(2)}) copy-start(f32[8,16,128]{2,1,0:T(8,128)} %param.8) | copy-start | bytes 196612
  1.5 6.1 %copy-start = (f32[32,8,64]{2,1,0:T(8,128)S(1)}, f32[32,8,64]{2,1,0:T(8,128)}, u32[]{:S(2)}) copy-start(f32[32,8,64]{2,1,0:T(8,128)} %rhs_hbm.1) | copy-start | bytes 196612
  1.5 6.1 %copy-start.1 = (bf16[32,8,64]{2,1,0:T(8,128)(2,1)S(1)}, bf16[32,8,64]{2,1,0:T(8,128)(2,1)}, u32[]{:S(2)}) copy-start(bf16[32,8,64]{2,1,0:T(8,128)(2,1)} %coef_hbm.1) | copy-start | bytes 98308
  1.5 18.6 %collective-permute-start = (f32[2,8,8,128]{3,2,1,0:T(8,128)S(1)}, f32[2,8,8,128]{3,2,1,0:T(8,128)S(1)}, u32[]{:S(2)}, u32[]{:S(2)}) collective-permute-start(f32[2,8,8,128]{3,2,1,0:T(8,128)S(1)} %get-tuple-element.15), channel_id=1, source_target_pairs={{0,2},{2,4},{4,6},{6,8},{8,10},{10,12},{12,14},{1,3},{3,5},{5,7},{... | collective-permute-start | bytes 196616 | tf_op jit(solution)/shard_map/ppermute | solution.py:381
  4.7 15.3 %collective-permute-start.1 = (f32[2,8,8,128]{3,2,1,0:T(8,128)S(1)}, f32[2,8,8,128]{3,2,1,0:T(8,128)S(1)}, u32[]{:S(2)}, u32[]{:S(2)}) collective-permute-start(f32[2,8,8,128]{3,2,1,0:T(8,128)S(1)} %get-tuple-element.16), channel_id=1, source_target_pairs={{2,0},{4,2},{6,4},{8,6},{10,8},{12,10},{14,12},{3,1},{5,3},{7,5},{... | collective-permute-start | bytes 196616 | tf_op jit(solution)/shard_map/ppermute | solution.py:381
  7.6 0.7 copy-start.2
  10.6 16.0 %all-to-all-start = ((f32[16,8,128]{2,1,0:T(8,128)}), f32[16,8,128]{2,1,0:T(8,128)S(1)}, u32[]{:S(2)}, u32[]{:S(2)}) async-start(f32[16,8,128]{2,1,0:T(8,128)} %bitcast.4), calls=%async_computation | async-start | bytes 131072 | tf_op jit(solution)/shard_map/all_to_all | solution.py:410
  29.8 9.2 %collective-permute-start.2 = (f32[2,13,32,128]{3,2,1,0:T(8,128)S(1)}, f32[2,13,32,128]{3,2,1,0:T(8,128)S(1)}, u32[]{:S(2)}, u32[]{:S(2)}) collective-permute-start(f32[2,13,32,128]{3,2,1,0:T(8,128)S(1)} %get-tuple-element.12), channel_id=1, source_target_pairs={{0,16},{16,32},{17,1},{32,48},{33,17},{48,64},{49,33},{64,80},{65,... | collective-permute-start | bytes 1277960 | tf_op jit(solution)/shard_map/ppermute | solution.py:374
  53.0 4.4 %collective-permute-start.3 = (f32[6,4,128]{2,1,0:T(4,128)S(1)}, f32[6,4,128]{2,1,0:T(4,128)S(1)}, u32[]{:S(2)}, u32[]{:S(2)}) collective-permute-start(f32[6,4,128]{2,1,0:T(4,128)S(1)} %get-tuple-element.14), channel_id=1, source_target_pairs={{0,2},{2,4},{3,1},{4,6},{5,3},{6,8},{7,5},{8,10},{9,7},{10,12},{11... | collective-permute-start | bytes 36872 | tf_op jit(solution)/shard_map/ppermute | solution.py:374
  60.4 5.5 %collective-permute-start.4 = (f32[3,6,4,128]{3,2,1,0:T(4,128)S(1)}, f32[3,6,4,128]{3,2,1,0:T(4,128)S(1)}, u32[]{:S(2)}, u32[]{:S(2)}) collective-permute-start(f32[3,6,4,128]{3,2,1,0:T(4,128)S(1)} %pad_maximum_fusion.3.mid_ref), channel_id=1, source_target_pairs={{0,16},{16,32},{17,1},{32,48},{33,17},{48,64},{49,33},{64,80},{65,... | collective-permute-start | bytes 110600 | tf_op jit(solution)/shard_map/ppermute | solution.py:374
  63.2 6.3 %collective-permute-start.5 = (f32[3,6,4,128]{3,2,1,0:T(4,128)S(1)}, f32[3,6,4,128]{3,2,1,0:T(4,128)S(1)}, u32[]{:S(2)}, u32[]{:S(2)}) collective-permute-start(f32[3,6,4,128]{3,2,1,0:T(4,128)S(1)} %pad_maximum_fusion.3.mid_ref), channel_id=1, source_target_pairs={{0,32},{16,48},{32,64},{33,1},{48,80},{49,17},{64,96},{65,33},{80,... | collective-permute-start | bytes 110600 | tf_op jit(solution)/shard_map/ppermute | solution.py:374

commit v3 on v2

--- a/solution.py
+++ b/solution.py
@@ -9,18 +9,40 @@
 
 DAMPING = 6.0 / 7.0
 REST = 1.0 - DAMPING
-PRECISE = lax.Precision.HIGHEST
 F32 = jnp.float32
+BF16 = jnp.bfloat16
 CORES = 2
 VMEM_BYTES = 40 * 1024 * 1024
+MOST_VMEM = 60 * 1024 * 1024
 
 
 def iota(shape, dim):
     return lax.broadcasted_iota(jnp.int32, shape, dim)
 
 
-def dot(a, b):
-    return jnp.dot(a, b, precision=PRECISE, preferred_element_type=F32)
+def split(values):
+    high = values.astype(BF16)
+    return high, (values - high.astype(F32)).astype(BF16)
+
+
+def small(a, b):
+    return jnp.dot(a.astype(BF16), b.astype(BF16), preferred_element_type=F32)
+
+
+def dot(a, picks):
+    high, low = split(a)
+    return small(high, picks) + small(low, picks)
+
+
+def pick(picks, a):
+    high, low = split(a)
+    return small(picks, high) + small(picks, low)
+
+
+def turned(a, b):
+    return lax.dot_general(
+        a.astype(BF16), b, (((1,), (1,)), ((), ())), preferred_element_type=F32
+    )
 
 
 def after(values, axis):
@@ -37,13 +59,16 @@
 
 
 def fine_kernel(
-    count_ref, target_hbm, rhs_hbm, coef_hbm, solved_ref, send_ref, target_ref, rhs_ref, coef_ref, sems
+    count_ref, target_hbm, rhs_hbm, coef_hbm, grid_hbm, cond_hbm, solved_hbm, send_ref, low_ref, high_ref,
+    target_ref, rhs_ref, coef_ref, grid_ref, cond_ref, solved_ref, sems
 ):
     live = count_ref[0]
     loads = [
         pltpu.make_async_copy(coef_hbm, coef_ref, sems.at[0]),
         pltpu.make_async_copy(rhs_hbm, rhs_ref, sems.at[1]),
         pltpu.make_async_copy(target_hbm, target_ref, sems.at[2]),
+        pltpu.make_async_copy(grid_hbm, grid_ref, sems.at[3]),
+        pltpu.make_async_copy(cond_hbm, cond_ref, sems.at[4]),
     ]
     for load in loads:
         load.start()
@@ -80,7 +105,11 @@
     first = source * scale
     second = first + scale * (REST * source + sides(first))
     residue = source - diagonal * second + sides(second)
-    solved_ref[...] = second
+    slot = iota((half, 8, 64), 0)
+    solved_ref[:half] = jnp.where(slot < live, second[:, :, :64], 0.0)
+    solved_ref[half:] = jnp.where(slot + half < live, second[:, :, 64:], 0.0)
+    store = pltpu.make_async_copy(solved_ref, solved_hbm, sems.at[5])
+    store.start()
 
     loads[2].wait()
     square = (128, 128)
@@ -114,81 +143,90 @@
     for number in range(2):
         mine = chosen & (rank == number)
         picked = jnp.where(mine, 1.0, 0.0)
-        packed.append(dot(picked[:, :128], parts[0]) + dot(picked[:, 128:], parts[1]))
+        packed.append(pick(picked[:, :128], parts[0]) + pick(picked[:, 128:], parts[1]))
         tag = jnp.where(mine & ((col & 7) == 0), (name & 255) + 1, 0).astype(F32)
         tags.append(jnp.sum(tag, axis=1, keepdims=True))
     row, col = iota(square, 0), iota(square, 1)
     place = (row & 7) * 2
     tags = jnp.where(col == place, tags[0], 0.0) + jnp.where(col == place + 1, tags[1], 0.0)
     lift = jnp.where(((row & 7) == 6) & ((row >> 3) == (col >> 3)), 1.0, 0.0)
-    send_ref[...] = jnp.where(col < 64, packed[0], packed[1]) + dot(lift, tags)
-
-
-def store_kernel(count_ref, second_ref, solved_ref):
-    live = count_ref[0]
-    second = second_ref[...]
-    half = second.shape[0]
-    slot = iota((half, 8, 64), 0)
-    solved_ref[:half] = jnp.where(slot < live, second[:, :, :64], 0.0)
-    solved_ref[half:] = jnp.where(slot + half < live, second[:, :, 64:], 0.0)
-
-
-def place_kernel(pos_ref, got_ref, chip_ref, full_ref, pay_ref):
-    tags = got_ref[pl.ds(6, 16, stride=8), :]
+    send_ref[...] = jnp.where(col < 64, packed[0], packed[1]) + small(lift, tags)
+    loads[3].wait()
+    loads[4].wait()
+    k = cond_ref[...].astype(F32) * 0.5
+    low_ref[0] = grid_ref[:, 0:8]
+    low_ref[1] = k[:, 0:8]
+    high_ref[0] = grid_ref[:, 8:16]
+    high_ref[1] = k[:, 8:16]
+    store.wait()
+
+
+def place_kernel(pos_ref, got_ref, chip_ref, source_ref, pay_ref, sems):
+    first = jnp.where(pos_ref[2] == 0, 1, 0)
+    copies = [
+        pltpu.make_async_copy(
+            chip_ref.at[number, 1, pl.ds(first, 7)], pay_ref.at[number, pl.ds(6, 7)], sems.at[number]
+        )
+        for number in range(2)
+    ]
+    for copy in copies:
+        copy.start()
     square = (128, 128)
     row, col = iota(square, 0), iota(square, 1)
-    rank = (row >> 4) & 1
-    mask = (col >> 4) == rank * 4 + (row >> 5)
-    turned = (((1,), (1,)), ((), ()))
-    tall = jnp.concatenate([tags] * 8, axis=0)
-    ones = jnp.ones((8, 128), F32)
-
-    def place(number, first_row, rows):
-        got = got_ref[pl.ds(number, 16, stride=8), :]
+    slot = (row >> 4) & 1
+    tags = jnp.concatenate([got_ref[pl.ds(6, 16, stride=8), :]] * 8, axis=0)
+    tags = jnp.where((col & 1) == slot, tags, 0.0).astype(BF16)
+    some = (16, 128)
+    across = turned(jnp.where((iota(some, 1) >> 1) == iota(some, 0), 1.0, 0.0), tags)
+    across = (across + 0.5).astype(jnp.int32) - 1
+    wide = (128, 768)
+    spread = jnp.where((iota(wide, 0) >> 1) == (iota(wide, 1) >> 7), 1.0, 0.0)
+    down = (small(tags, spread) + 0.5).astype(jnp.int32) - 1
+    lane = iota(wide, 1)
+    right = ((down & 31) == ((lane & 127) >> 2)) & ((lane & 3) == (iota(wide, 0) >> 5))
+    right = jnp.where(right, 1.0, 0.0).astype(BF16)
+    mask = (col >> 4) == slot * 4 + (row >> 5)
+    some = (32, 128)
+    cell = (iota(some, 0) >> 3) * 4 + (iota(some, 0) & 3)
+    select = jnp.where((iota(some, 1) & 15) == cell, 1.0, 0.0)
+    half = iota((8, 128), 0) >> 2
+
+    def place(owner, tiles):
+        got = got_ref[pl.ds(owner, 16, stride=8), :]
         slices = jnp.where(mask, jnp.concatenate([got] * 8, axis=0), 0.0)
-        shape = (8 * rows, 128)
-        shift = rows.bit_length() - 1
-        r, c = iota(shape, 0), iota(shape, 1)
-        x, y = r >> shift, (r & (rows - 1)) + first_row
-        select = jnp.where((c & 15) == (x & 3) * 4 + (y & 3), 1.0, 0.0)
-        left = lax.dot_general(
-            select, slices, turned, precision=PRECISE, preferred_element_type=F32
+        high, low = split(slices)
+        left = turned(select, high) + turned(select, low)
+        name = jnp.broadcast_to(across[owner : owner + 1], (8, 128))
+        here = {
+            (x, t): ((name >> 7) == x) & (((name >> 5) & 3) == 2 * t + half)
+            for x in range(2)
+            for t in tiles
+        }
+        places = [(x, t) for x in range(8) for t in tiles]
+        values = jnp.concatenate(
+            [jnp.where(here[x >> 2, t], left[8 * (x & 3) : 8 * (x & 3) + 8], 0.0) for x, t in places],
+            axis=0,
         )
-        named = jnp.where(col == 2 * number + rank, tall, 0.0)
-        across = lax.dot_general(
-            ones, named, turned, precision=PRECISE, preferred_element_type=F32
+        marks = jnp.concatenate(
+            [jnp.where(here[x >> 2, t], 1.0, 0.0) for x, t in places if x % 4 == 0], axis=0
         )
-        across = (across[:1] + 0.5).astype(jnp.int32) - 1
-        here = ((across >> 7) == (x >> 2)) & (((across >> 5) & 3) == (y >> 2))
-        down = (jnp.sum(named, axis=1, keepdims=True) + 0.5).astype(jnp.int32) - 1
-        right = jnp.where(((down & 31) == (col >> 2)) & ((col & 3) == (row >> 5)), 1.0, 0.0)
-        placed = dot(jnp.where(here, left, 0.0), right)
-        covered = jnp.dot(
-            jnp.where(here, 1.0, 0.0).astype(jnp.bfloat16),
-            right.astype(jnp.bfloat16),
-            preferred_element_type=F32,
-        )
-        return placed.reshape(8, rows, 128), covered.reshape(8, rows, 128) > 0.5
-
-    core = pos_ref[2]
+        put = right[:, 128 * owner : 128 * owner + 128]
+        placed = dot(values, put).reshape(8, 8 * len(tiles), 128)
+        covered = small(marks, put).reshape(2, 8 * len(tiles), 128) > 0.5
+        return placed, covered
+
     for number in range(2):
-        for part, (first_row, rows, start) in enumerate(((8, 8, 0), (0, 16, 8), (0, 8, 24))):
-            placed, covered = place(2 * part + number, first_row, rows)
-            lines = slice(start, start + rows)
-            full_ref[number, 0, :, lines] = jnp.where(covered, placed, chip_ref[number, 0, :, lines])
-        full_ref[number, 1] = chip_ref[number, 1]
-
-    @pl.when(core == 0)
-    def _():
-        for number in range(2):
-            pay_ref[number, 0:6] = full_ref[number, 0, 2:8]
-            pay_ref[number, 6:13] = full_ref[number, 1, 1:8]
-
-    @pl.when(core != 0)
-    def _():
-        for number in range(2):
-            pay_ref[number, 0:6] = full_ref[number, 0, 0:6]
-            pay_ref[number, 6:13] = full_ref[number, 1, 0:7]
+        for part, (tiles, start) in enumerate((((1,), 0), ((0, 1), 8), ((0,), 24))):
+            placed, covered = place(2 * part + number, tiles)
+            lines = slice(start, start + 8 * len(tiles))
+            old = chip_ref[number, 0, :, lines]
+            for x in range(2):
+                four = slice(4 * x, 4 * x + 4)
+                source_ref[number, four, lines] = jnp.where(covered[x], placed[four], old[four])
+    for number in range(2):
+        pay_ref[number, 0:6] = source_ref[number, pl.ds(2 * first, 6)]
+    for copy in copies:
+        copy.wait()
 
 
 def pair_matrix(size):
@@ -235,7 +273,7 @@
 
 
 def base_kernel(
-    sizes, pos_ref, full_ref, side_ref, out_ref, pay_ref,
+    sizes, pos_ref, source_ref, chip_ref, side_ref, out_ref, pay_ref,
     s_ref, h_ref, wx_ref, wy_ref, wz_ref, diag_ref, scale_ref, first_ref, second_ref,
     res_ref, rows_ref,
 ):
@@ -243,10 +281,10 @@
     for number in range(2):
         lanes = slice(128 * number, 128 * number + 128)
         s_ref[0:6, :, lanes] = side_ref[0, number, 0:6]
-        s_ref[6:14, :, lanes] = full_ref[number, 0]
+        s_ref[6:14, :, lanes] = source_ref[number]
         s_ref[14:20, :, lanes] = side_ref[1, number, 0:6]
         h_ref[0:7, :, lanes] = side_ref[0, number, 6:13]
-        h_ref[7:15, :, lanes] = full_ref[number, 1]
+        h_ref[7:15, :, lanes] = chip_ref[number, 1]
         h_ref[15:22, :, lanes] = side_ref[1, number, 6:13]
     shape = (32, 256)
     lane = iota(shape, 1)
@@ -271,7 +309,7 @@
         first_ref[layer] = s_ref[layer] * scale
         return 0
 
-    lax.fori_loop(0, 20, weigh, 0)
+    lax.fori_loop(0, 20, weigh, 0, unroll=True)
 
     def sides(ref, layer):
         u, wy, wz = ref[layer], wy_ref[layer], wz_ref[layer]
@@ -284,14 +322,14 @@
         second_ref[layer] = u + scale_ref[layer] * (REST * s_ref[layer] + total)
         return 0
 
-    lax.fori_loop(1, 19, correct, 0)
+    lax.fori_loop(1, 19, correct, 0, unroll=True)
 
     def leave(layer, _):
         u, total = sides(second_ref, layer)
         res_ref[layer - 2] = s_ref[layer] - diag_ref[layer] * u + total
         return 0
 
-    lax.fori_loop(2, 18, leave, 0)
+    lax.fori_loop(2, 18, leave, 0, unroll=True)
     own = second_ref[6:14, 8:24, :]
     out_ref[...] = jnp.where(core == 0, own[:, :, :128], own[:, :, 128:])
 
@@ -351,14 +389,15 @@
     out_ref[...] = jnp.where(core == 0, second[:, :, :16], second[:, :, 16:32])
 
 
-def call(kernel, out_shape, in_specs=None, scratch=(), flops=100_000):
-    specs = {} if in_specs is None else {"in_specs": in_specs}
+def call(kernel, out_shape, in_specs, scratch=(), flops=100_000, outs=None, vmem=VMEM_BYTES):
+    specs = {} if outs is None else {"out_specs": outs}
     return pl.pallas_call(
         kernel,
         out_shape=out_shape,
         scratch_shapes=list(scratch),
-        compiler_params=pltpu.CompilerParams(vmem_limit_bytes=VMEM_BYTES),
+        compiler_params=pltpu.CompilerParams(vmem_limit_bytes=vmem),
         cost_estimate=pl.CostEstimate(flops=flops, bytes_accessed=flops, transcendentals=0),
+        in_specs=in_specs,
         **specs,
     )
 
@@ -395,41 +434,46 @@
     vmem = pl.BlockSpec(memory_space=pltpu.VMEM)
     smem = pl.BlockSpec(memory_space=pltpu.SMEM)
     struct = jax.ShapeDtypeStruct
-    anywhere = pl.BlockSpec(memory_space=pl.ANY)
-    second, send = call(
+    hbm = pl.BlockSpec(memory_space=pltpu.HBM)
+    edge = struct((2, 8, 8, 128), F32)
+    fine_solution, send, low, high = call(
         fine_kernel,
-        (struct((16, 8, 128), F32), struct((128, 128), F32)),
-        [smem, anywhere, anywhere, anywhere],
+        (struct(fine_rhs.shape, F32), struct((128, 128), F32), edge, edge),
+        [smem, hbm, hbm, hbm, hbm, hbm],
         [
             pltpu.VMEM((1, 32), jnp.int32),
             pltpu.VMEM(fine_rhs.shape, F32),
             pltpu.VMEM(fine_coef.shape, fine_coef.dtype),
-            pltpu.SemaphoreType.DMA((3,)),
+            pltpu.VMEM(coarse_rhs.shape, F32),
+            pltpu.VMEM(coarse_coef.shape, coarse_coef.dtype),
+            pltpu.VMEM(fine_rhs.shape, F32),
+            pltpu.SemaphoreType.DMA((6,)),
         ],
-    )(patch_count, patch_target.reshape(1, 32), fine_rhs, fine_coef)
+        outs=[hbm, vmem, vmem, vmem],
+        vmem=MOST_VMEM,
+    )(patch_count, patch_target.reshape(1, 32), fine_rhs, fine_coef, coarse_rhs, coarse_coef)
     got = lax.all_to_all(send.reshape(16, 8, 128), ("gy", "gz"), 0, 0).reshape(128, 128)
-    fine_solution = call(store_kernel, struct(fine_rhs.shape, F32), [smem, vmem])(
-        patch_count, second
-    )
-    own = jnp.stack([coarse_rhs, coarse_coef.astype(F32) * 0.5])
-    below, above = exchanged(own[:, :, 8:], own[:, :, :8], "gy")
-    chip = shared(jnp.concatenate([below, own, above], axis=2))
-    full, pay = call(
+    below, above = exchanged(high, low, "gy")
+    chip = shared(jnp.concatenate([below, low, high, above], axis=2))
+    source, pay = call(
         place_kernel,
-        (struct((2, 2, 8, 32, 128), F32), struct((2, 13, 32, 128), F32)),
+        (struct((2, 8, 32, 128), F32), struct((2, 13, 32, 128), F32)),
         [smem, vmem, vmem],
+        [pltpu.SemaphoreType.DMA((2,))],
+        outs=[vmem] * 2,
     )(pos, got, chip)
     side = shared(split_send(pay, "gx", 1))
     grid = (32, 256)
     coarse_solution, pay = call(
         functools.partial(base_kernel, sizes),
         (struct((8, 16, 128), F32), struct((6, 4, 128), F32)),
-        [smem, vmem, vmem],
+        [smem, vmem, vmem, vmem],
         [pltpu.VMEM((20, *grid), F32), pltpu.VMEM((22, *grid), F32)]
         + [pltpu.VMEM((20, *grid), F32)] * 7
         + [pltpu.VMEM((16, *grid), F32), pltpu.VMEM((320, 128), F32)],
         flops=5_000_000,
-    )(pos, full, side)
+        outs=[vmem] * 2,
+    )(pos, source, chip, side)
     halo = shared(split_send(pay, "gy", 1))
     mid = jnp.stack([halo[0], pay, halo[1]])
     sides = shared(jnp.stack([split_send(mid, "gx", 1), split_send(mid, "gx", 2)]))

time: 76.6 us -> 70.3 us (0.918)
  the two profiles are of different devices: /device:TPU:515 before, /device:TPU:55 now
where the time goes in v3:
time: 70.3 us; the launch traced here: 69.9 us
  starting transfers between devices  29.1 us (41%)
  waiting for transfers between devices  18.8 us (27%)
  Pallas kernels  10.3 us (15%)
  blocking collectives  10.1 us (14%)
  between operations  1.39 us (2%)
    ppermute x4, starting transfers between devices, split_send(): return lax.ppermute(values, (axis, 'gz'), pairs)  15.2 us
    ppermute x4, waiting for transfers between devices, split_send(): return lax.ppermute(values, (axis, 'gz'), pairs)  14.6 us
    all_gather x4, blocking collectives, shared(): return lax.all_gather(values, 'gz')  10.1 us
    all_to_all x1, starting transfers between devices, per_device(): lax.all_to_all(send.reshape(16, 8, 128), ('gy', 'gz'), 0, 0)  7.71 us
    ppermute x2, starting transfers between devices, exchanged(): return (lax.ppermute(up, axis, pairs), lax.ppermute(down, axis, back))  6.22 us
    ppermute x2, waiting for transfers between devices, exchanged(): return (lax.ppermute(up, axis, pairs), lax.ppermute(down, axis, back))  4.21 us
    pallas_call x1, Pallas kernels, per_device(): call(functools.partial(base_kernel, sizes), (struct((8, 16, 128), F32), s...  3.52 us
    pallas_call x1, Pallas kernels, per_device(): call(fine_kernel, (struct(fine_rhs.shape, F32), struct((128, 128), F32),...  2.78 us
  transfers between devices with their start and end apart: 7, of which 4 were waited for; matrix products, arithmetic and copies ran while one was open for 0% of the time, Pallas kernels for 0%

profile of v3, /device:TPU:55, one launch (start us, length us, event | category | flops | bytes accessed | tf_op | source)
XLA Modules:
  0.0 69.9 jit_solution(3109043989842634614)
XLA Ops:
  1.3 2.8 %shard_map.85 = (f32[32,8,64]{2,1,0:T(8,128)}, f32[128,128]{1,0:T(8,128)}, f32[2,8,8,128]{3,2,1,0:T(8,128)}, f32[2,8,8,128]{3,2,1,0:T(8,128)}) custom-call(s32[1]{0:T(128)S(6)} %copy.9.count_ref, s32[1,32]{1,0:T(1,128)} %bitcast.25, f32[32,8,64]{2,1,0:T(8,128)} %rhs_hbm.1, bf16[32,8,64]{2,1,0:T(8,128)(2,1)} %coef_hbm.1, f32[8,16,128]{2,1,0:T(8,128)} %grid_hbm.1, ...), custom_call_target="tpu_custom_call" | custom-call | flops 100000 | bytes 100000 | tf_op jit(solution)/shard_map/pallas_call | solution.py:439
  4.1 0.0 copy-start.1
  4.1 7.7 %all-to-all-start = ((f32[16,8,128]{2,1,0:T(8,128)}), f32[16,8,128]{2,1,0:T(8,128)S(1)}, u32[]{:S(2)}, u32[]{:S(2)}) async-start(f32[16,8,128]{2,1,0:T(8,128)} %bitcast.22), calls=%async_computation | async-start | bytes 131072 | tf_op jit(solution)/shard_map/all_to_all | solution.py:455
  11.8 4.3 %collective-permute-start = (f32[2,8,8,128]{3,2,1,0:T(8,128)S(1)}, f32[2,8,8,128]{3,2,1,0:T(8,128)S(1)}, u32[]{:S(2)}, u32[]{:S(2)}) collective-permute-start(f32[2,8,8,128]{3,2,1,0:T(8,128)S(1)} %copy-done.1), channel_id=1, source_target_pairs={{0,2},{2,4},{4,6},{6,8},{8,10},{10,12},{12,14},{1,3},{3,5},{5,7},{... | collective-permute-start | bytes 196616 | tf_op jit(solution)/shard_map/ppermute | solution.py:420
  16.1 1.9 %collective-permute-start.1 = (f32[2,8,8,128]{3,2,1,0:T(8,128)S(1)}, f32[2,8,8,128]{3,2,1,0:T(8,128)S(1)}, u32[]{:S(2)}, u32[]{:S(2)}) collective-permute-start(f32[2,8,8,128]{3,2,1,0:T(8,128)S(1)} %copy-done), channel_id=1, source_target_pairs={{2,0},{4,2},{6,4},{8,6},{10,8},{12,10},{14,12},{3,1},{5,3},{7,5},{... | collective-permute-start | bytes 196616 | tf_op jit(solution)/shard_map/ppermute | solution.py:420
  18.1 0.1 pad_add_fusion.pos_ref
  18.1 0.0 collective-permute-done
  18.1 4.2 %collective-permute-done.1 = f32[2,8,8,128]{3,2,1,0:T(8,128)S(1)} collective-permute-done((f32[2,8,8,128]{3,2,1,0:T(8,128)S(1)}, f32[2,8,8,128]{3,2,1,0:T(8,128)S(1)}, u32[]{:S(2)}, u32[]{:S(2)}) %collective-permute-start.1) | collective-permute-done | bytes 65568 | tf_op jit(solution)/shard_map/ppermute | solution.py:420
  22.4 3.6 %all-gather = f32[4,8,32,128]{3,2,1,0:T(8,128)S(1)} all-gather(f32[2,8,32,128]{3,2,1,0:T(8,128)S(1)} %pad_maximum_fusion), channel_id=2, replica_groups=mesh['gx'=64,'gy'=8,'gz'=2] {'gz'}, dimensions={0}, use_global_device_ids=true | all-gather | bytes 786432 | tf_op jit(solution)/shard_map/all_gather | solution.py:424
  26.0 0.0 all-to-all-done
  26.0 2.3 %shard_map.86 = (f32[2,8,32,128]{3,2,1,0:T(8,128)S(1)}, f32[2,13,32,128]{3,2,1,0:T(8,128)S(1)}) custom-call(s32[3]{0:T(128)S(1)} %pad_add_fusion.pos_ref, f32[128,128]{1,0:T(8,128)S(1)} %bitcast.20, f32[2,2,8,32,128]{4,3,2,1,0:T(8,128)S(1)} %bitcast.16), custom_call_target="tpu_custom_call" | custom-call | flops 100000 | bytes 100000 | tf_op jit(solution)/shard_map/pallas_call | solution.py:458
  28.2 2.0 %collective-permute-start.2 = (f32[2,13,32,128]{3,2,1,0:T(8,128)S(1)}, f32[2,13,32,128]{3,2,1,0:T(8,128)S(1)}, u32[]{:S(2)}, u32[]{:S(2)}) collective-permute-start(f32[2,13,32,128]{3,2,1,0:T(8,128)S(1)} %get-tuple-element.16), channel_id=1, source_target_pairs={{0,16},{16,32},{17,1},{32,48},{33,17},{48,64},{49,33},{64,80},{65,... | collective-permute-start | bytes 1277960 | tf_op jit(solution)/shard_map/ppermute | solution.py:413
  30.2 8.1 %collective-permute-done.2 = f32[2,13,32,128]{3,2,1,0:T(8,128)S(1)} collective-permute-done((f32[2,13,32,128]{3,2,1,0:T(8,128)S(1)}, f32[2,13,32,128]{3,2,1,0:T(8,128)S(1)}, u32[]{:S(2)}, u32[]{:S(2)}) %collective-permute-start.2) | collective-permute-done | bytes 426016 | tf_op jit(solution)/shard_map/ppermute | solution.py:413
  38.3 2.8 %all-gather.1 = f32[4,13,32,128]{3,2,1,0:T(8,128)S(1)} all-gather(f32[2,13,32,128]{3,2,1,0:T(8,128)S(1)} %collective-permute-done.2), channel_id=3, replica_groups=mesh['gx'=64,'gy'=8,'gz'=2] {'gz'}, dimensions={0}, use_global_device_ids=true | all-gather | bytes 1277952 | tf_op jit(solution)/shard_map/all_gather | solution.py:424
  41.1 3.5 %shard_map.87 = (f32[8,16,128]{2,1,0:T(8,128)}, f32[6,4,128]{2,1,0:T(4,128)S(1)}) custom-call(s32[3]{0:T(128)S(1)} %pad_add_fusion.pos_ref, f32[2,8,32,128]{3,2,1,0:T(8,128)S(1)} %get-tuple-element.15.source_ref, f32[2,2,8,32,128]{4,3,2,1,0:T(8,128)S(1)} %bitcast.17, f32[2,2,13,32,128]{4,3,2,1,0:T(8,128)S(1)} %bitcast.18), custom_call_target="tpu_custom_call" | custom-call | flops 5000000 | bytes 5000000 | tf_op jit(solution)/shard_map/pallas_call | solution.py:467
  44.6 1.9 %collective-permute-start.3 = (f32[6,4,128]{2,1,0:T(4,128)S(1)}, f32[6,4,128]{2,1,0:T(4,128)S(1)}, u32[]{:S(2)}, u32[]{:S(2)}) collective-permute-start(f32[6,4,128]{2,1,0:T(4,128)S(1)} %get-tuple-element.18), channel_id=1, source_target_pairs={{0,2},{2,4},{3,1},{4,6},{5,3},{6,8},{7,5},{8,10},{9,7},{10,12},{11... | collective-permute-start | bytes 36872 | tf_op jit(solution)/shard_map/ppermute | solution.py:413
  46.5 3.7 %collective-permute-done.3 = f32[6,4,128]{2,1,0:T(4,128)S(1)} collective-permute-done((f32[6,4,128]{2,1,0:T(4,128)S(1)}, f32[6,4,128]{2,1,0:T(4,128)S(1)}, u32[]{:S(2)}, u32[]{:S(2)}) %collective-permute-start.3) | collective-permute-done | bytes 12320 | tf_op jit(solution)/shard_map/ppermute | solution.py:413
  50.2 1.8 %all-gather.2 = f32[12,4,128]{2,1,0:T(4,128)S(1)} all-gather(f32[6,4,128]{2,1,0:T(4,128)S(1)} %collective-permute-done.3), channel_id=4, replica_groups=mesh['gx'=64,'gy'=8,'gz'=2] {'gz'}, dimensions={0}, use_global_device_ids=true | all-gather | bytes 36864 | tf_op jit(solution)/shard_map/all_gather | solution.py:424
  52.1 8.2 %collective-permute-start.5 = (f32[3,6,4,128]{3,2,1,0:T(4,128)S(1)}, f32[3,6,4,128]{3,2,1,0:T(4,128)S(1)}, u32[]{:S(2)}, u32[]{:S(2)}) collective-permute-start(f32[3,6,4,128]{3,2,1,0:T(4,128)S(1)} %pad_maximum_fusion.2.mid_ref), channel_id=1, source_target_pairs={{0,32},{16,48},{32,64},{33,1},{48,80},{49,17},{64,96},{65,33},{80,... | collective-permute-start | bytes 110600 | tf_op jit(solution)/shard_map/ppermute | solution.py:413
  60.3 3.1 %collective-permute-start.4 = (f32[3,6,4,128]{3,2,1,0:T(4,128)S(1)}, f32[3,6,4,128]{3,2,1,0:T(4,128)S(1)}, u32[]{:S(2)}, u32[]{:S(2)}) collective-permute-start(f32[3,6,4,128]{3,2,1,0:T(4,128)S(1)} %pad_maximum_fusion.2.mid_ref), channel_id=1, source_target_pairs={{0,16},{16,32},{17,1},{32,48},{33,17},{48,64},{49,33},{64,80},{65,... | collective-permute-start | bytes 110600 | tf_op jit(solution)/shard_map/ppermute | solution.py:413
  63.4 0.0 collective-permute-done.5
  63.4 2.8 %collective-permute-done.4 = f32[3,6,4,128]{3,2,1,0:T(4,128)S(1)} collective-permute-done((f32[3,6,4,128]{3,2,1,0:T(4,128)S(1)}, f32[3,6,4,128]{3,2,1,0:T(4,128)S(1)}, u32[]{:S(2)}, u32[]{:S(2)}) %collective-permute-start.4) | collective-permute-done | bytes 36896 | tf_op jit(solution)/shard_map/ppermute | solution.py:413
  66.2 1.9 %all-gather.3 = f32[4,3,6,4,128]{4,3,2,1,0:T(4,128)S(1)} all-gather(f32[2,3,6,4,128]{4,3,2,1,0:T(4,128)S(1)} %pad_maximum_fusion.1), channel_id=5, replica_groups=mesh['gx'=64,'gy'=8,'gz'=2] {'gz'}, dimensions={0}, use_global_device_ids=true | all-gather | bytes 221184 | tf_op jit(solution)/shard_map/all_gather | solution.py:424
  68.1 1.8 %shard_map.88 = f32[1,2,16]{2,1,0:T(2,128)} custom-call(s32[3]{0:T(128)S(1)} %pad_add_fusion.pos_ref, f32[3,6,4,128]{3,2,1,0:T(4,128)S(1)} %pad_maximum_fusion.2.mid_ref, f32[2,2,3,6,4,128]{5,4,3,2,1,0:T(4,128)S(1)} %bitcast.19), custom_call_target="tpu_custom_call" | custom-call | flops 100000 | bytes 100000 | tf_op jit(solution)/shard_map/pallas_call | solution.py:480
  (7 shorter events, 0.1 us)
Async XLA Ops:
  4.1 7.7 %copy-start.1 = (f32[2,8,8,128]{3,2,1,0:T(8,128)S(1)}, f32[2,8,8,128]{3,2,1,0:T(8,128)}, u32[]{:S(2)}) copy-start(f32[2,8,8,128]{3,2,1,0:T(8,128)} %get-tuple-element.13) | copy-start | bytes 196612
  4.1 12.0 %copy-start = (f32[2,8,8,128]{3,2,1,0:T(8,128)S(1)}, f32[2,8,8,128]{3,2,1,0:T(8,128)}, u32[]{:S(2)}) copy-start(f32[2,8,8,128]{3,2,1,0:T(8,128)} %get-tuple-element.14) | copy-start | bytes 196612
  4.1 21.9 %all-to-all-start = ((f32[16,8,128]{2,1,0:T(8,128)}), f32[16,8,128]{2,1,0:T(8,128)S(1)}, u32[]{:S(2)}, u32[]{:S(2)}) async-start(f32[16,8,128]{2,1,0:T(8,128)} %bitcast.22), calls=%async_computation | async-start | bytes 131072 | tf_op jit(solution)/shard_map/all_to_all | solution.py:455
  11.8 6.3 %collective-permute-start = (f32[2,8,8,128]{3,2,1,0:T(8,128)S(1)}, f32[2,8,8,128]{3,2,1,0:T(8,128)S(1)}, u32[]{:S(2)}, u32[]{:S(2)}) collective-permute-start(f32[2,8,8,128]{3,2,1,0:T(8,128)S(1)} %copy-done.1), channel_id=1, source_target_pairs={{0,2},{2,4},{4,6},{6,8},{8,10},{10,12},{12,14},{1,3},{3,5},{5,7},{... | collective-permute-start | bytes 196616 | tf_op jit(solution)/shard_map/ppermute | solution.py:420
  16.1 6.2 %collective-permute-start.1 = (f32[2,8,8,128]{3,2,1,0:T(8,128)S(1)}, f32[2,8,8,128]{3,2,1,0:T(8,128)S(1)}, u32[]{:S(2)}, u32[]{:S(2)}) collective-permute-start(f32[2,8,8,128]{3,2,1,0:T(8,128)S(1)} %copy-done), channel_id=1, source_target_pairs={{2,0},{4,2},{6,4},{8,6},{10,8},{12,10},{14,12},{3,1},{5,3},{7,5},{... | collective-permute-start | bytes 196616 | tf_op jit(solution)/shard_map/ppermute | solution.py:420
  28.2 10.1 %collective-permute-start.2 = (f32[2,13,32,128]{3,2,1,0:T(8,128)S(1)}, f32[2,13,32,128]{3,2,1,0:T(8,128)S(1)}, u32[]{:S(2)}, u32[]{:S(2)}) collective-permute-start(f32[2,13,32,128]{3,2,1,0:T(8,128)S(1)} %get-tuple-element.16), channel_id=1, source_target_pairs={{0,16},{16,32},{17,1},{32,48},{33,17},{48,64},{49,33},{64,80},{65,... | collective-permute-start | bytes 1277960 | tf_op jit(solution)/shard_map/ppermute | solution.py:413
  44.6 5.6 %collective-permute-start.3 = (f32[6,4,128]{2,1,0:T(4,128)S(1)}, f32[6,4,128]{2,1,0:T(4,128)S(1)}, u32[]{:S(2)}, u32[]{:S(2)}) collective-permute-start(f32[6,4,128]{2,1,0:T(4,128)S(1)} %get-tuple-element.18), channel_id=1, source_target_pairs={{0,2},{2,4},{3,1},{4,6},{5,3},{6,8},{7,5},{8,10},{9,7},{10,12},{11... | collective-permute-start | bytes 36872 | tf_op jit(solution)/shard_map/ppermute | solution.py:413
  52.1 11.4 %collective-permute-start.5 = (f32[3,6,4,128]{3,2,1,0:T(4,128)S(1)}, f32[3,6,4,128]{3,2,1,0:T(4,128)S(1)}, u32[]{:S(2)}, u32[]{:S(2)}) collective-permute-start(f32[3,6,4,128]{3,2,1,0:T(4,128)S(1)} %pad_maximum_fusion.2.mid_ref), channel_id=1, source_target_pairs={{0,32},{16,48},{32,64},{33,1},{48,80},{49,17},{64,96},{65,33},{80,... | collective-permute-start | bytes 110600 | tf_op jit(solution)/shard_map/ppermute | solution.py:413
  60.3 5.9 %collective-permute-start.4 = (f32[3,6,4,128]{3,2,1,0:T(4,128)S(1)}, f32[3,6,4,128]{3,2,1,0:T(4,128)S(1)}, u32[]{:S(2)}, u32[]{:S(2)}) collective-permute-start(f32[3,6,4,128]{3,2,1,0:T(4,128)S(1)} %pad_maximum_fusion.2.mid_ref), channel_id=1, source_target_pairs={{0,16},{16,32},{17,1},{32,48},{33,17},{48,64},{49,33},{64,80},{65,... | collective-permute-start | bytes 110600 | tf_op jit(solution)/shard_map/ppermute | solution.py:413

commit v4 on v3

--- a/solution.py
+++ b/solution.py
@@ -59,7 +59,7 @@
 
 
 def fine_kernel(
-    count_ref, target_hbm, rhs_hbm, coef_hbm, grid_hbm, cond_hbm, solved_hbm, send_ref, low_ref, high_ref,
+    count_ref, target_hbm, rhs_hbm, coef_hbm, grid_hbm, cond_hbm, solved_hbm, send_ref, own_ref,
     target_ref, rhs_ref, coef_ref, grid_ref, cond_ref, solved_ref, sems
 ):
     live = count_ref[0]
@@ -153,24 +153,13 @@
     send_ref[...] = jnp.where(col < 64, packed[0], packed[1]) + small(lift, tags)
     loads[3].wait()
     loads[4].wait()
-    k = cond_ref[...].astype(F32) * 0.5
-    low_ref[0] = grid_ref[:, 0:8]
-    low_ref[1] = k[:, 0:8]
-    high_ref[0] = grid_ref[:, 8:16]
-    high_ref[1] = k[:, 8:16]
+    own_ref[0] = grid_ref[...]
+    own_ref[1] = cond_ref[...].astype(F32) * 0.5
     store.wait()
 
 
-def place_kernel(pos_ref, got_ref, chip_ref, source_ref, pay_ref, sems):
-    first = jnp.where(pos_ref[2] == 0, 1, 0)
-    copies = [
-        pltpu.make_async_copy(
-            chip_ref.at[number, 1, pl.ds(first, 7)], pay_ref.at[number, pl.ds(6, 7)], sems.at[number]
-        )
-        for number in range(2)
-    ]
-    for copy in copies:
-        copy.start()
+def place_kernel(pos_ref, got_ref, chip_ref, source_ref, pay_ref):
+    first = jnp.where(pos_ref[2] == 0, 2, 0)
     square = (128, 128)
     row, col = iota(square, 0), iota(square, 1)
     slot = (row >> 4) & 1
@@ -224,9 +213,7 @@
                 four = slice(4 * x, 4 * x + 4)
                 source_ref[number, four, lines] = jnp.where(covered[x], placed[four], old[four])
     for number in range(2):
-        pay_ref[number, 0:6] = source_ref[number, pl.ds(2 * first, 6)]
-    for copy in copies:
-        copy.wait()
+        pay_ref[number] = source_ref[number, pl.ds(first, 6)]
 
 
 def pair_matrix(size):
@@ -435,10 +422,9 @@
     smem = pl.BlockSpec(memory_space=pltpu.SMEM)
     struct = jax.ShapeDtypeStruct
     hbm = pl.BlockSpec(memory_space=pltpu.HBM)
-    edge = struct((2, 8, 8, 128), F32)
-    fine_solution, send, low, high = call(
+    fine_solution, send, own = call(
         fine_kernel,
-        (struct(fine_rhs.shape, F32), struct((128, 128), F32), edge, edge),
+        (struct(fine_rhs.shape, F32), struct((128, 128), F32), struct((2, 8, 16, 128), F32)),
         [smem, hbm, hbm, hbm, hbm, hbm],
         [
             pltpu.VMEM((1, 32), jnp.int32),
@@ -449,20 +435,20 @@
             pltpu.VMEM(fine_rhs.shape, F32),
             pltpu.SemaphoreType.DMA((6,)),
         ],
-        outs=[hbm, vmem, vmem, vmem],
+        outs=[hbm, vmem, vmem],
         vmem=MOST_VMEM,
     )(patch_count, patch_target.reshape(1, 32), fine_rhs, fine_coef, coarse_rhs, coarse_coef)
     got = lax.all_to_all(send.reshape(16, 8, 128), ("gy", "gz"), 0, 0).reshape(128, 128)
-    below, above = exchanged(high, low, "gy")
-    chip = shared(jnp.concatenate([below, low, high, above], axis=2))
+    below, above = exchanged(own, own, "gy")
+    chip = shared(jnp.concatenate([below[:, :, 8:], own, above[:, :, :8]], axis=2))
+    edge = split_send(jnp.where(core == 0, chip[:, 1, 1:], chip[:, 1, :7]), "gx", 1)
     source, pay = call(
         place_kernel,
-        (struct((2, 8, 32, 128), F32), struct((2, 13, 32, 128), F32)),
+        (struct((2, 8, 32, 128), F32), struct((2, 6, 32, 128), F32)),
         [smem, vmem, vmem],
-        [pltpu.SemaphoreType.DMA((2,))],
         outs=[vmem] * 2,
     )(pos, got, chip)
-    side = shared(split_send(pay, "gx", 1))
+    side = shared(jnp.concatenate([split_send(pay, "gx", 1), edge], axis=1))
     grid = (32, 256)
     coarse_solution, pay = call(
         functools.partial(base_kernel, sizes),

time: 70.3 us -> 66.8 us (0.950)
  the two profiles are of different devices: /device:TPU:55 before, /device:TPU:521 now
where the time goes in v4:
time: 66.8 us; the launch traced here: 66.4 us
  starting transfers between devices  26.4 us (40%)
  blocking collectives  19.2 us (29%)
  Pallas kernels  9.89 us (15%)
  waiting for transfers between devices  8.52 us (13%)
  between operations  1.41 us (2%)
  local copies, waits for them, and re-layouts  0.87 us (1%)
    all_gather x4, blocking collectives, shared(): return lax.all_gather(values, 'gz')  19.2 us
    ppermute x5, starting transfers between devices, split_send(): return lax.ppermute(values, (axis, 'gz'), pairs)  13 us
    ppermute x5, waiting for transfers between devices, split_send(): return lax.ppermute(values, (axis, 'gz'), pairs)  8.52 us
    all_to_all x1, starting transfers between devices, per_device(): lax.all_to_all(send.reshape(16, 8, 128), ('gy', 'gz'), 0, 0)  8.11 us
    ppermute x2, starting transfers between devices, exchanged(): return (lax.ppermute(up, axis, pairs), lax.ppermute(down, axis, back))  5.28 us
    pallas_call x1, Pallas kernels, per_device(): call(functools.partial(base_kernel, sizes), (struct((8, 16, 128), F32), s...  3.43 us
    pallas_call x1, Pallas kernels, per_device(): call(fine_kernel, (struct(fine_rhs.shape, F32), struct((128, 128), F32),...  2.78 us
    pallas_call x1, Pallas kernels, per_device(): call(place_kernel, (struct((2, 8, 32, 128), F32), struct((2, 6, 32, 128),...  1.91 us
  transfers between devices with their start and end apart: 8, of which 4 were waited for; matrix products, arithmetic and copies ran while one was open for 0% of the time, Pallas kernels for 3%

profile of v4, /device:TPU:521, one launch (start us, length us, event | category | flops | bytes accessed | tf_op | source)
XLA Modules:
  0.0 66.4 jit_solution(12564507840904400431)
XLA Ops:
  1.3 2.8 %shard_map.85 = (f32[32,8,64]{2,1,0:T(8,128)}, f32[128,128]{1,0:T(8,128)}, f32[2,8,16,128]{3,2,1,0:T(8,128)}) custom-call(s32[1]{0:T(128)S(6)} %copy.9.count_ref, s32[1,32]{1,0:T(1,128)} %bitcast.28, f32[32,8,64]{2,1,0:T(8,128)} %rhs_hbm.1, bf16[32,8,64]{2,1,0:T(8,128)(2,1)} %coef_hbm.1, f32[8,16,128]{2,1,0:T(8,128)} %grid_hbm.1, bf16[8,16,128]{2,1,0:T(8,128)(2,1)} %cond_hbm.1), custom_call_target="tpu_custom_call" | custom-call | flops 100000 | bytes 100000 | tf_op jit(solution)/shard_map/pallas_call | solution.py:425
  4.1 2.2 %collective-permute-start.1 = (f32[2,8,16,128]{3,2,1,0:T(8,128)}, f32[2,8,16,128]{3,2,1,0:T(8,128)S(1)}, u32[]{:S(2)}, u32[]{:S(2)}) collective-permute-start(f32[2,8,16,128]{3,2,1,0:T(8,128)} %get-tuple-element.12), channel_id=1, source_target_pairs={{2,0},{4,2},{6,4},{8,6},{10,8},{12,10},{14,12},{3,1},{5,3},{7,5},{... | collective-permute-start | bytes 393224 | tf_op jit(solution)/shard_map/ppermute | solution.py:407
  6.2 3.1 %collective-permute-start = (f32[2,8,16,128]{3,2,1,0:T(8,128)}, f32[2,8,16,128]{3,2,1,0:T(8,128)S(1)}, u32[]{:S(2)}, u32[]{:S(2)}) collective-permute-start(f32[2,8,16,128]{3,2,1,0:T(8,128)} %get-tuple-element.12), channel_id=1, source_target_pairs={{0,2},{2,4},{4,6},{6,8},{8,10},{10,12},{12,14},{1,3},{3,5},{5,7},{... | collective-permute-start | bytes 393224 | tf_op jit(solution)/shard_map/ppermute | solution.py:407
  9.4 8.1 %all-to-all-start = ((f32[16,8,128]{2,1,0:T(8,128)}), f32[16,8,128]{2,1,0:T(8,128)S(1)}, u32[]{:S(2)}, u32[]{:S(2)}) async-start(f32[16,8,128]{2,1,0:T(8,128)} %bitcast.25), calls=%async_computation | async-start | bytes 131072 | tf_op jit(solution)/shard_map/all_to_all | solution.py:441
  17.5 0.0 collective-permute-done.1
  17.5 0.0 collective-permute-done
  17.5 0.8 %copy-done = f32[2,8,16,128]{3,2,1,0:T(8,128)S(1)} copy-done((f32[2,8,16,128]{3,2,1,0:T(8,128)S(1)}, f32[2,8,16,128]{3,2,1,0:T(8,128)}, u32[]{:S(2)}) %copy-start) | copy-done | bytes 131096
  18.4 2.2 %all-gather = f32[4,8,32,128]{3,2,1,0:T(8,128)S(1)} all-gather(f32[2,8,32,128]{3,2,1,0:T(8,128)S(1)} %pad_maximum_fusion.1), channel_id=2, replica_groups=mesh['gx'=64,'gy'=8,'gz'=2] {'gz'}, dimensions={0}, use_global_device_ids=true | all-gather | bytes 786432 | tf_op jit(solution)/shard_map/all_gather | solution.py:411
  20.6 4.1 %collective-permute-start.3 = (f32[2,7,32,128]{3,2,1,0:T(8,128)S(1)}, f32[2,7,32,128]{3,2,1,0:T(8,128)S(1)}, u32[]{:S(2)}, u32[]{:S(2)}) collective-permute-start(f32[2,7,32,128]{3,2,1,0:T(8,128)S(1)} %fusion), channel_id=1, source_target_pairs={{0,16},{16,32},{17,1},{32,48},{33,17},{48,64},{49,33},{64,80},{65,... | collective-permute-start | bytes 688136 | tf_op jit(solution)/shard_map/ppermute | solution.py:400
  24.7 0.1 pad_add_fusion.pos_ref
  24.8 1.9 %shard_map.86 = (f32[2,8,32,128]{3,2,1,0:T(8,128)S(1)}, f32[2,6,32,128]{3,2,1,0:T(8,128)S(1)}) custom-call(s32[3]{0:T(128)S(1)} %pad_add_fusion.pos_ref, f32[128,128]{1,0:T(8,128)S(1)} %bitcast.23, f32[2,2,8,32,128]{4,3,2,1,0:T(8,128)S(1)} %bitcast.19), custom_call_target="tpu_custom_call" | custom-call | flops 100000 | bytes 100000 | tf_op jit(solution)/shard_map/pallas_call | solution.py:445
  26.7 2.9 %collective-permute-start.2 = (f32[2,6,32,128]{3,2,1,0:T(8,128)S(1)}, f32[2,6,32,128]{3,2,1,0:T(8,128)S(1)}, u32[]{:S(2)}, u32[]{:S(2)}) collective-permute-start(f32[2,6,32,128]{3,2,1,0:T(8,128)S(1)} %get-tuple-element.14), channel_id=1, source_target_pairs={{0,16},{16,32},{17,1},{32,48},{33,17},{48,64},{49,33},{64,80},{65,... | collective-permute-start | bytes 589832 | tf_op jit(solution)/shard_map/ppermute | solution.py:400
  29.6 3.5 %collective-permute-done.2 = f32[2,6,32,128]{3,2,1,0:T(8,128)S(1)} collective-permute-done((f32[2,6,32,128]{3,2,1,0:T(8,128)S(1)}, f32[2,6,32,128]{3,2,1,0:T(8,128)S(1)}, u32[]{:S(2)}, u32[]{:S(2)}) %collective-permute-start.2) | collective-permute-done | bytes 196640 | tf_op jit(solution)/shard_map/ppermute | solution.py:400
  33.1 6.4 %all-gather.1 = f32[4,13,32,128]{3,2,1,0:T(8,128)S(1)} all-gather(f32[2,13,32,128]{3,2,1,0:T(8,128)S(1)} %pad_maximum_fusion), channel_id=3, replica_groups=mesh['gx'=64,'gy'=8,'gz'=2] {'gz'}, dimensions={0}, use_global_device_ids=true | all-gather | bytes 1277952 | tf_op jit(solution)/shard_map/all_gather | solution.py:411
  39.5 3.4 %shard_map.87 = (f32[8,16,128]{2,1,0:T(8,128)}, f32[6,4,128]{2,1,0:T(4,128)S(1)}) custom-call(s32[3]{0:T(128)S(1)} %pad_add_fusion.pos_ref, f32[2,8,32,128]{3,2,1,0:T(8,128)S(1)} %get-tuple-element.13.source_ref, f32[2,2,8,32,128]{4,3,2,1,0:T(8,128)S(1)} %bitcast.20, f32[2,2,13,32,128]{4,3,2,1,0:T(8,128)S(1)} %bitcast.21), custom_call_target="tpu_custom_call" | custom-call | flops 5000000 | bytes 5000000 | tf_op jit(solution)/shard_map/pallas_call | solution.py:453
  43.0 2.2 %collective-permute-start.4 = (f32[6,4,128]{2,1,0:T(4,128)S(1)}, f32[6,4,128]{2,1,0:T(4,128)S(1)}, u32[]{:S(2)}, u32[]{:S(2)}) collective-permute-start(f32[6,4,128]{2,1,0:T(4,128)S(1)} %get-tuple-element.16), channel_id=1, source_target_pairs={{0,2},{2,4},{3,1},{4,6},{5,3},{6,8},{7,5},{8,10},{9,7},{10,12},{11... | collective-permute-start | bytes 36872 | tf_op jit(solution)/shard_map/ppermute | solution.py:400
  45.2 2.2 %collective-permute-done.4 = f32[6,4,128]{2,1,0:T(4,128)S(1)} collective-permute-done((f32[6,4,128]{2,1,0:T(4,128)S(1)}, f32[6,4,128]{2,1,0:T(4,128)S(1)}, u32[]{:S(2)}, u32[]{:S(2)}) %collective-permute-start.4) | collective-permute-done | bytes 12320 | tf_op jit(solution)/shard_map/ppermute | solution.py:400
  47.4 4.2 %all-gather.2 = f32[12,4,128]{2,1,0:T(4,128)S(1)} all-gather(f32[6,4,128]{2,1,0:T(4,128)S(1)} %collective-permute-done.4), channel_id=4, replica_groups=mesh['gx'=64,'gy'=8,'gz'=2] {'gz'}, dimensions={0}, use_global_device_ids=true | all-gather | bytes 36864 | tf_op jit(solution)/shard_map/all_gather | solution.py:411
  51.6 1.9 %collective-permute-start.6 = (f32[3,6,4,128]{3,2,1,0:T(4,128)S(1)}, f32[3,6,4,128]{3,2,1,0:T(4,128)S(1)}, u32[]{:S(2)}, u32[]{:S(2)}) collective-permute-start(f32[3,6,4,128]{3,2,1,0:T(4,128)S(1)} %pad_maximum_fusion.3.mid_ref), channel_id=1, source_target_pairs={{0,32},{16,48},{32,64},{33,1},{48,80},{49,17},{64,96},{65,33},{80,... | collective-permute-start | bytes 110600 | tf_op jit(solution)/shard_map/ppermute | solution.py:400
  53.6 2.0 %collective-permute-start.5 = (f32[3,6,4,128]{3,2,1,0:T(4,128)S(1)}, f32[3,6,4,128]{3,2,1,0:T(4,128)S(1)}, u32[]{:S(2)}, u32[]{:S(2)}) collective-permute-start(f32[3,6,4,128]{3,2,1,0:T(4,128)S(1)} %pad_maximum_fusion.3.mid_ref), channel_id=1, source_target_pairs={{0,16},{16,32},{17,1},{32,48},{33,17},{48,64},{49,33},{64,80},{65,... | collective-permute-start | bytes 110600 | tf_op jit(solution)/shard_map/ppermute | solution.py:400
  55.5 1.7 %collective-permute-done.6 = f32[3,6,4,128]{3,2,1,0:T(4,128)S(1)} collective-permute-done((f32[3,6,4,128]{3,2,1,0:T(4,128)S(1)}, f32[3,6,4,128]{3,2,1,0:T(4,128)S(1)}, u32[]{:S(2)}, u32[]{:S(2)}) %collective-permute-start.6) | collective-permute-done | bytes 36896 | tf_op jit(solution)/shard_map/ppermute | solution.py:400
  57.2 1.0 %collective-permute-done.5 = f32[3,6,4,128]{3,2,1,0:T(4,128)S(1)} collective-permute-done((f32[3,6,4,128]{3,2,1,0:T(4,128)S(1)}, f32[3,6,4,128]{3,2,1,0:T(4,128)S(1)}, u32[]{:S(2)}, u32[]{:S(2)}) %collective-permute-start.5) | collective-permute-done | bytes 36896 | tf_op jit(solution)/shard_map/ppermute | solution.py:400
  58.3 6.4 %all-gather.3 = f32[4,3,6,4,128]{4,3,2,1,0:T(4,128)S(1)} all-gather(f32[2,3,6,4,128]{4,3,2,1,0:T(4,128)S(1)} %pad_maximum_fusion.2), channel_id=5, replica_groups=mesh['gx'=64,'gy'=8,'gz'=2] {'gz'}, dimensions={0}, use_global_device_ids=true | all-gather | bytes 221184 | tf_op jit(solution)/shard_map/all_gather | solution.py:411
  64.7 1.8 %shard_map.88 = f32[1,2,16]{2,1,0:T(2,128)} custom-call(s32[3]{0:T(128)S(1)} %pad_add_fusion.pos_ref, f32[3,6,4,128]{3,2,1,0:T(4,128)S(1)} %pad_maximum_fusion.3.mid_ref, f32[2,2,3,6,4,128]{5,4,3,2,1,0:T(4,128)S(1)} %bitcast.22), custom_call_target="tpu_custom_call" | custom-call | flops 100000 | bytes 100000 | tf_op jit(solution)/shard_map/pallas_call | solution.py:466
  (11 shorter events, 0.1 us)
Async XLA Ops:
  4.1 13.4 %collective-permute-start.1 = (f32[2,8,16,128]{3,2,1,0:T(8,128)}, f32[2,8,16,128]{3,2,1,0:T(8,128)S(1)}, u32[]{:S(2)}, u32[]{:S(2)}) collective-permute-start(f32[2,8,16,128]{3,2,1,0:T(8,128)} %get-tuple-element.12), channel_id=1, source_target_pairs={{2,0},{4,2},{6,4},{8,6},{10,8},{12,10},{14,12},{3,1},{5,3},{7,5},{... | collective-permute-start | bytes 393224 | tf_op jit(solution)/shard_map/ppermute | solution.py:407
  6.2 11.3 %collective-permute-start = (f32[2,8,16,128]{3,2,1,0:T(8,128)}, f32[2,8,16,128]{3,2,1,0:T(8,128)S(1)}, u32[]{:S(2)}, u32[]{:S(2)}) collective-permute-start(f32[2,8,16,128]{3,2,1,0:T(8,128)} %get-tuple-element.12), channel_id=1, source_target_pairs={{0,2},{2,4},{4,6},{6,8},{8,10},{10,12},{12,14},{1,3},{3,5},{5,7},{... | collective-permute-start | bytes 393224 | tf_op jit(solution)/shard_map/ppermute | solution.py:407
  9.4 15.4 %all-to-all-start = ((f32[16,8,128]{2,1,0:T(8,128)}), f32[16,8,128]{2,1,0:T(8,128)S(1)}, u32[]{:S(2)}, u32[]{:S(2)}) async-start(f32[16,8,128]{2,1,0:T(8,128)} %bitcast.25), calls=%async_computation | async-start | bytes 131072 | tf_op jit(solution)/shard_map/all_to_all | solution.py:441
  17.5 0.9 %copy-start = (f32[2,8,16,128]{3,2,1,0:T(8,128)S(1)}, f32[2,8,16,128]{3,2,1,0:T(8,128)}, u32[]{:S(2)}) copy-start(f32[2,8,16,128]{3,2,1,0:T(8,128)} %get-tuple-element.12) | copy-start | bytes 393220
  20.6 12.5 %collective-permute-start.3 = (f32[2,7,32,128]{3,2,1,0:T(8,128)S(1)}, f32[2,7,32,128]{3,2,1,0:T(8,128)S(1)}, u32[]{:S(2)}, u32[]{:S(2)}) collective-permute-start(f32[2,7,32,128]{3,2,1,0:T(8,128)S(1)} %fusion), channel_id=1, source_target_pairs={{0,16},{16,32},{17,1},{32,48},{33,17},{48,64},{49,33},{64,80},{65,... | collective-permute-start | bytes 688136 | tf_op jit(solution)/shard_map/ppermute | solution.py:400
  26.7 6.4 %collective-permute-start.2 = (f32[2,6,32,128]{3,2,1,0:T(8,128)S(1)}, f32[2,6,32,128]{3,2,1,0:T(8,128)S(1)}, u32[]{:S(2)}, u32[]{:S(2)}) collective-permute-start(f32[2,6,32,128]{3,2,1,0:T(8,128)S(1)} %get-tuple-element.14), channel_id=1, source_target_pairs={{0,16},{16,32},{17,1},{32,48},{33,17},{48,64},{49,33},{64,80},{65,... | collective-permute-start | bytes 589832 | tf_op jit(solution)/shard_map/ppermute | solution.py:400
  43.0 4.4 %collective-permute-start.4 = (f32[6,4,128]{2,1,0:T(4,128)S(1)}, f32[6,4,128]{2,1,0:T(4,128)S(1)}, u32[]{:S(2)}, u32[]{:S(2)}) collective-permute-start(f32[6,4,128]{2,1,0:T(4,128)S(1)} %get-tuple-element.16), channel_id=1, source_target_pairs={{0,2},{2,4},{3,1},{4,6},{5,3},{6,8},{7,5},{8,10},{9,7},{10,12},{11... | collective-permute-start | bytes 36872 | tf_op jit(solution)/shard_map/ppermute | solution.py:400
  51.6 5.6 %collective-permute-start.6 = (f32[3,6,4,128]{3,2,1,0:T(4,128)S(1)}, f32[3,6,4,128]{3,2,1,0:T(4,128)S(1)}, u32[]{:S(2)}, u32[]{:S(2)}) collective-permute-start(f32[3,6,4,128]{3,2,1,0:T(4,128)S(1)} %pad_maximum_fusion.3.mid_ref), channel_id=1, source_target_pairs={{0,32},{16,48},{32,64},{33,1},{48,80},{49,17},{64,96},{65,33},{80,... | collective-permute-start | bytes 110600 | tf_op jit(solution)/shard_map/ppermute | solution.py:400
  53.6 4.7 %collective-permute-start.5 = (f32[3,6,4,128]{3,2,1,0:T(4,128)S(1)}, f32[3,6,4,128]{3,2,1,0:T(4,128)S(1)}, u32[]{:S(2)}, u32[]{:S(2)}) collective-permute-start(f32[3,6,4,128]{3,2,1,0:T(4,128)S(1)} %pad_maximum_fusion.3.mid_ref), channel_id=1, source_target_pairs={{0,16},{16,32},{17,1},{32,48},{33,17},{48,64},{49,33},{64,80},{65,... | collective-permute-start | bytes 110600 | tf_op jit(solution)/shard_map/ppermute | solution.py:400

commit v5 on v4

--- a/solution.py
+++ b/solution.py
@@ -158,7 +158,7 @@
     store.wait()
 
 
-def place_kernel(pos_ref, got_ref, chip_ref, source_ref, pay_ref):
+def place_kernel(pos_ref, got_ref, chip_ref, halo_ref, source_ref, pay_ref):
     first = jnp.where(pos_ref[2] == 0, 2, 0)
     square = (128, 128)
     row, col = iota(square, 0), iota(square, 1)
@@ -205,10 +205,11 @@
         return placed, covered
 
     for number in range(2):
+        olds = (halo_ref[0, number, 0], chip_ref[number, 0], halo_ref[1, number, 0])
         for part, (tiles, start) in enumerate((((1,), 0), ((0, 1), 8), ((0,), 24))):
             placed, covered = place(2 * part + number, tiles)
             lines = slice(start, start + 8 * len(tiles))
-            old = chip_ref[number, 0, :, lines]
+            old = olds[part]
             for x in range(2):
                 four = slice(4 * x, 4 * x + 4)
                 source_ref[number, four, lines] = jnp.where(covered[x], placed[four], old[four])
@@ -260,7 +261,7 @@
 
 
 def base_kernel(
-    sizes, pos_ref, source_ref, chip_ref, side_ref, out_ref, pay_ref,
+    sizes, pos_ref, source_ref, chip_ref, halo_ref, side_ref, out_ref, pay_ref,
     s_ref, h_ref, wx_ref, wy_ref, wz_ref, diag_ref, scale_ref, first_ref, second_ref,
     res_ref, rows_ref,
 ):
@@ -271,7 +272,9 @@
         s_ref[6:14, :, lanes] = source_ref[number]
         s_ref[14:20, :, lanes] = side_ref[1, number, 0:6]
         h_ref[0:7, :, lanes] = side_ref[0, number, 6:13]
-        h_ref[7:15, :, lanes] = chip_ref[number, 1]
+        h_ref[7:15, 0:8, lanes] = halo_ref[0, number, 1]
+        h_ref[7:15, 8:24, lanes] = chip_ref[number, 1]
+        h_ref[7:15, 24:32, lanes] = halo_ref[1, number, 1]
         h_ref[15:22, :, lanes] = side_ref[1, number, 6:13]
     shape = (32, 256)
     lane = iota(shape, 1)
@@ -398,13 +401,6 @@
         if place - step >= 0:
             pairs.append((place * CORES + 1, (place - step) * CORES + 1))
     return lax.ppermute(values, (axis, "gz"), pairs)
-
-
-def exchanged(up, down, axis):
-    count = lax.axis_size(axis)
-    pairs = [(place, place + 1) for place in range(count - 1)]
-    back = [(target, source) for source, target in pairs]
-    return lax.ppermute(up, axis, pairs), lax.ppermute(down, axis, back)
 
 
 def shared(values):
@@ -439,27 +435,28 @@
         vmem=MOST_VMEM,
     )(patch_count, patch_target.reshape(1, 32), fine_rhs, fine_coef, coarse_rhs, coarse_coef)
     got = lax.all_to_all(send.reshape(16, 8, 128), ("gy", "gz"), 0, 0).reshape(128, 128)
-    below, above = exchanged(own, own, "gy")
-    chip = shared(jnp.concatenate([below[:, :, 8:], own, above[:, :, :8]], axis=2))
-    edge = split_send(jnp.where(core == 0, chip[:, 1, 1:], chip[:, 1, :7]), "gx", 1)
+    chip = shared(own)
+    halo = shared(split_send(jnp.where(core == 0, chip[:, :, :, 8:], chip[:, :, :, :8]), "gy", 1))
+    conduct = jnp.concatenate([halo[0, :, 1], chip[:, 1], halo[1, :, 1]], axis=2)
+    edge = split_send(jnp.where(core == 0, conduct[:, 1:], conduct[:, :7]), "gx", 1)
     source, pay = call(
         place_kernel,
         (struct((2, 8, 32, 128), F32), struct((2, 6, 32, 128), F32)),
-        [smem, vmem, vmem],
+        [smem, vmem, vmem, vmem],
         outs=[vmem] * 2,
-    )(pos, got, chip)
+    )(pos, got, chip, halo)
     side = shared(jnp.concatenate([split_send(pay, "gx", 1), edge], axis=1))
     grid = (32, 256)
     coarse_solution, pay = call(
         functools.partial(base_kernel, sizes),
         (struct((8, 16, 128), F32), struct((6, 4, 128), F32)),
-        [smem, vmem, vmem, vmem],
+        [smem, vmem, vmem, vmem, vmem],
         [pltpu.VMEM((20, *grid), F32), pltpu.VMEM((22, *grid), F32)]
         + [pltpu.VMEM((20, *grid), F32)] * 7
         + [pltpu.VMEM((16, *grid), F32), pltpu.VMEM((320, 128), F32)],
         flops=5_000_000,
         outs=[vmem] * 2,
-    )(pos, source, chip, side)
+    )(pos, source, chip, halo, side)
     halo = shared(split_send(pay, "gy", 1))
     mid = jnp.stack([halo[0], pay, halo[1]])
     sides = shared(jnp.stack([split_send(mid, "gx", 1), split_send(mid, "gx", 2)]))

time: 66.8 us -> 70.1 us (1.049)
  blocking collectives: 19.2 us -> 23.3 us
  starting transfers between devices: 26.4 us -> 22.6 us
  waiting for transfers between devices: 8.52 us -> 12.3 us
  local copies, waits for them, and re-layouts: 0.87 us -> 0.03 us
    ppermute x2 -> x0, starting transfers between devices: 5.28 us -> none  [exchanged(): return (lax.ppermute(up, axis, pairs), lax.ppermute(down, axis, back))]
    all_gather x4 -> x5, blocking collectives: 19.2 us -> 23.3 us  [shared(): return lax.all_gather(values, 'gz')]
    ppermute x5 -> x6, waiting for transfers between devices: 8.52 us -> 12.3 us  [split_send(): return lax.ppermute(values, (axis, 'gz'), pairs)]
    ppermute x5 -> x6, starting transfers between devices: 13 us -> 14.9 us  [split_send(): return lax.ppermute(values, (axis, 'gz'), pairs)]
    unnamed x2, local copies, waits for them, and re-layouts: 0.85 us -> 0.01 us
  transfers between devices with their start and end apart: 8 -> 7, of which waited for: 4 -> 5; matrix products, arithmetic and copies ran while one was open for 0% -> 0% of each run, Pallas kernels for 3% -> 3%
where the time goes in v5:
time: 70.1 us; the launch traced here: 69.7 us
  blocking collectives  23.3 us (33%)
  starting transfers between devices  22.6 us (32%)
  waiting for transfers between devices  12.3 us (18%)
  Pallas kernels  9.87 us (14%)
  between operations  1.4 us (2%)
    all_gather x5, blocking collectives, shared(): return lax.all_gather(values, 'gz')  23.3 us
    ppermute x6, starting transfers between devices, split_send(): return lax.ppermute(values, (axis, 'gz'), pairs)  14.9 us
    ppermute x6, waiting for transfers between devices, split_send(): return lax.ppermute(values, (axis, 'gz'), pairs)  12.3 us
    all_to_all x1, starting transfers between devices, per_device(): lax.all_to_all(send.reshape(16, 8, 128), ('gy', 'gz'), 0, 0)  7.68 us
    pallas_call x1, Pallas kernels, per_device(): call(functools.partial(base_kernel, sizes), (struct((8, 16, 128), F32), s...  3.42 us
    pallas_call x1, Pallas kernels, per_device(): call(fine_kernel, (struct(fine_rhs.shape, F32), struct((128, 128), F32),...  2.78 us
    pallas_call x1, Pallas kernels, per_device(): call(place_kernel, (struct((2, 8, 32, 128), F32), struct((2, 6, 32, 128),...  1.91 us
    pallas_call x1, Pallas kernels, per_device(): call(functools.partial(deep_kernel, sizes), struct((1, 2, 16), F32), [sme...  1.76 us
  transfers between devices with their start and end apart: 7, of which 5 were waited for; matrix products, arithmetic and copies ran while one was open for 0% of the time, Pallas kernels for 3%

profile of v5, /device:TPU:521, one launch (start us, length us, event | category | flops | bytes accessed | tf_op | source)
XLA Modules:
  0.0 69.7 jit_solution(8127322899596046652)
XLA Ops:
  1.3 2.8 %shard_map.85 = (f32[32,8,64]{2,1,0:T(8,128)}, f32[128,128]{1,0:T(8,128)}, f32[2,8,16,128]{3,2,1,0:T(8,128)}) custom-call(s32[1]{0:T(128)S(6)} %copy.9.count_ref, s32[1,32]{1,0:T(1,128)} %bitcast.37, f32[32,8,64]{2,1,0:T(8,128)} %rhs_hbm.1, bf16[32,8,64]{2,1,0:T(8,128)(2,1)} %coef_hbm.1, f32[8,16,128]{2,1,0:T(8,128)} %grid_hbm.1, bf16[8,16,128]{2,1,0:T(8,128)(2,1)} %cond_hbm.1), custom_call_target="tpu_custom_call" | custom-call | flops 100000 | bytes 100000 | tf_op jit(solution)/shard_map/pallas_call | solution.py:421
  4.1 7.7 %all-to-all-start = ((f32[16,8,128]{2,1,0:T(8,128)}), f32[16,8,128]{2,1,0:T(8,128)S(1)}, u32[]{:S(2)}, u32[]{:S(2)}) async-start(f32[16,8,128]{2,1,0:T(8,128)} %bitcast.34), calls=%async_computation | async-start | bytes 131072 | tf_op jit(solution)/shard_map/all_to_all | solution.py:437
  11.8 2.0 %all-gather = f32[4,8,16,128]{3,2,1,0:T(8,128)S(1)} all-gather(f32[2,8,16,128]{3,2,1,0:T(8,128)S(1)} %copy-done), channel_id=2, replica_groups=mesh['gx'=64,'gy'=8,'gz'=2] {'gz'}, dimensions={0}, use_global_device_ids=true | all-gather | bytes 393216 | tf_op jit(solution)/shard_map/all_gather | solution.py:407
  13.8 2.2 %collective-permute-start = (f32[2,2,8,8,128]{4,3,2,1,0:T(8,128)S(1)}, f32[2,2,8,8,128]{4,3,2,1,0:T(8,128)S(1)}, u32[]{:S(2)}, u32[]{:S(2)}) collective-permute-start(f32[2,2,8,8,128]{4,3,2,1,0:T(8,128)S(1)} %slice_select_fusion.1), channel_id=1, source_target_pairs={{0,2},{2,4},{3,1},{4,6},{5,3},{6,8},{7,5},{8,10},{9,7},{10,12},{11... | collective-permute-start | bytes 393224 | tf_op jit(solution)/shard_map/ppermute | solution.py:403
  16.0 3.5 %collective-permute-done = f32[2,2,8,8,128]{4,3,2,1,0:T(8,128)S(1)} collective-permute-done((f32[2,2,8,8,128]{4,3,2,1,0:T(8,128)S(1)}, f32[2,2,8,8,128]{4,3,2,1,0:T(8,128)S(1)}, u32[]{:S(2)}, u32[]{:S(2)}) %collective-permute-start) | collective-permute-done | bytes 131104 | tf_op jit(solution)/shard_map/ppermute | solution.py:403
  19.5 4.3 %all-gather.1 = f32[4,2,8,8,128]{4,3,2,1,0:T(8,128)S(1)} all-gather(f32[2,2,8,8,128]{4,3,2,1,0:T(8,128)S(1)} %collective-permute-done), channel_id=3, replica_groups=mesh['gx'=64,'gy'=8,'gz'=2] {'gz'}, dimensions={0}, use_global_device_ids=true | all-gather | bytes 393216 | tf_op jit(solution)/shard_map/all_gather | solution.py:407
  23.9 4.1 %collective-permute-start.2 = (f32[2,7,32,128]{3,2,1,0:T(8,128)S(1)}, f32[2,7,32,128]{3,2,1,0:T(8,128)S(1)}, u32[]{:S(2)}, u32[]{:S(2)}) collective-permute-start(f32[2,7,32,128]{3,2,1,0:T(8,128)S(1)} %slice_select_fusion), channel_id=1, source_target_pairs={{0,16},{16,32},{17,1},{32,48},{33,17},{48,64},{49,33},{64,80},{65,... | collective-permute-start | bytes 688136 | tf_op jit(solution)/shard_map/ppermute | solution.py:403
  28.0 0.1 pad_add_fusion.pos_ref
  28.1 0.0 all-to-all-done
  28.1 1.9 %shard_map.86 = (f32[2,8,32,128]{3,2,1,0:T(8,128)S(1)}, f32[2,6,32,128]{3,2,1,0:T(8,128)S(1)}) custom-call(s32[3]{0:T(128)S(1)} %pad_add_fusion.pos_ref, f32[128,128]{1,0:T(8,128)S(1)} %bitcast.32, f32[2,2,8,16,128]{4,3,2,1,0:T(8,128)S(1)} %bitcast.25, f32[2,2,2,8,8,128]{5,4,3,2,1,0:T(8,128)S(1)} %bitcast.29), custom_call_target="tpu_custom_call" | custom-call | flops 100000 | bytes 100000 | tf_op jit(solution)/shard_map/pallas_call | solution.py:442
  30.0 2.9 %collective-permute-start.1 = (f32[2,6,32,128]{3,2,1,0:T(8,128)S(1)}, f32[2,6,32,128]{3,2,1,0:T(8,128)S(1)}, u32[]{:S(2)}, u32[]{:S(2)}) collective-permute-start(f32[2,6,32,128]{3,2,1,0:T(8,128)S(1)} %get-tuple-element.14), channel_id=1, source_target_pairs={{0,16},{16,32},{17,1},{32,48},{33,17},{48,64},{49,33},{64,80},{65,... | collective-permute-start | bytes 589832 | tf_op jit(solution)/shard_map/ppermute | solution.py:403
  32.9 3.5 %collective-permute-done.1 = f32[2,6,32,128]{3,2,1,0:T(8,128)S(1)} collective-permute-done((f32[2,6,32,128]{3,2,1,0:T(8,128)S(1)}, f32[2,6,32,128]{3,2,1,0:T(8,128)S(1)}, u32[]{:S(2)}, u32[]{:S(2)}) %collective-permute-start.1) | collective-permute-done | bytes 196640 | tf_op jit(solution)/shard_map/ppermute | solution.py:403
  36.4 0.0 collective-permute-done.2
  36.4 6.4 %all-gather.2 = f32[4,13,32,128]{3,2,1,0:T(8,128)S(1)} all-gather(f32[2,13,32,128]{3,2,1,0:T(8,128)S(1)} %pad_maximum_fusion), channel_id=4, replica_groups=mesh['gx'=64,'gy'=8,'gz'=2] {'gz'}, dimensions={0}, use_global_device_ids=true | all-gather | bytes 1277952 | tf_op jit(solution)/shard_map/all_gather | solution.py:407
  42.8 3.4 %shard_map.87 = (f32[8,16,128]{2,1,0:T(8,128)}, f32[6,4,128]{2,1,0:T(4,128)S(1)}) custom-call(s32[3]{0:T(128)S(1)} %pad_add_fusion.pos_ref, f32[2,8,32,128]{3,2,1,0:T(8,128)S(1)} %get-tuple-element.13.source_ref, f32[2,2,8,16,128]{4,3,2,1,0:T(8,128)S(1)} %bitcast.26, f32[2,2,2,8,8,128]{5,4,3,2,1,0:T(8,128)S(1)} %bitcast.30, f32[2,2,13,32,128]{4,3,2,1,0:T(8,128)S(1)} %bitcast.27), custom_call_target="tpu_custom_call" | custom-call | flops 5000000 | bytes 5000000 | tf_op jit(solution)/shard_map/pallas_call | solution.py:450
  46.3 1.9 %collective-permute-start.3 = (f32[6,4,128]{2,1,0:T(4,128)S(1)}, f32[6,4,128]{2,1,0:T(4,128)S(1)}, u32[]{:S(2)}, u32[]{:S(2)}) collective-permute-start(f32[6,4,128]{2,1,0:T(4,128)S(1)} %get-tuple-element.16), channel_id=1, source_target_pairs={{0,2},{2,4},{3,1},{4,6},{5,3},{6,8},{7,5},{8,10},{9,7},{10,12},{11... | collective-permute-start | bytes 36872 | tf_op jit(solution)/shard_map/ppermute | solution.py:403
  48.2 2.5 %collective-permute-done.3 = f32[6,4,128]{2,1,0:T(4,128)S(1)} collective-permute-done((f32[6,4,128]{2,1,0:T(4,128)S(1)}, f32[6,4,128]{2,1,0:T(4,128)S(1)}, u32[]{:S(2)}, u32[]{:S(2)}) %collective-permute-start.3) | collective-permute-done | bytes 12320 | tf_op jit(solution)/shard_map/ppermute | solution.py:403
  50.7 4.2 %all-gather.3 = f32[12,4,128]{2,1,0:T(4,128)S(1)} all-gather(f32[6,4,128]{2,1,0:T(4,128)S(1)} %collective-permute-done.3), channel_id=5, replica_groups=mesh['gx'=64,'gy'=8,'gz'=2] {'gz'}, dimensions={0}, use_global_device_ids=true | all-gather | bytes 36864 | tf_op jit(solution)/shard_map/all_gather | solution.py:407
  54.9 1.9 %collective-permute-start.5 = (f32[3,6,4,128]{3,2,1,0:T(4,128)S(1)}, f32[3,6,4,128]{3,2,1,0:T(4,128)S(1)}, u32[]{:S(2)}, u32[]{:S(2)}) collective-permute-start(f32[3,6,4,128]{3,2,1,0:T(4,128)S(1)} %pad_maximum_fusion.3.mid_ref), channel_id=1, source_target_pairs={{0,32},{16,48},{32,64},{33,1},{48,80},{49,17},{64,96},{65,33},{80,... | collective-permute-start | bytes 110600 | tf_op jit(solution)/shard_map/ppermute | solution.py:403
  56.8 2.0 %collective-permute-start.4 = (f32[3,6,4,128]{3,2,1,0:T(4,128)S(1)}, f32[3,6,4,128]{3,2,1,0:T(4,128)S(1)}, u32[]{:S(2)}, u32[]{:S(2)}) collective-permute-start(f32[3,6,4,128]{3,2,1,0:T(4,128)S(1)} %pad_maximum_fusion.3.mid_ref), channel_id=1, source_target_pairs={{0,16},{16,32},{17,1},{32,48},{33,17},{48,64},{49,33},{64,80},{65,... | collective-permute-start | bytes 110600 | tf_op jit(solution)/shard_map/ppermute | solution.py:403
  58.8 1.7 %collective-permute-done.5 = f32[3,6,4,128]{3,2,1,0:T(4,128)S(1)} collective-permute-done((f32[3,6,4,128]{3,2,1,0:T(4,128)S(1)}, f32[3,6,4,128]{3,2,1,0:T(4,128)S(1)}, u32[]{:S(2)}, u32[]{:S(2)}) %collective-permute-start.5) | collective-permute-done | bytes 36896 | tf_op jit(solution)/shard_map/ppermute | solution.py:403
  60.5 1.0 %collective-permute-done.4 = f32[3,6,4,128]{3,2,1,0:T(4,128)S(1)} collective-permute-done((f32[3,6,4,128]{3,2,1,0:T(4,128)S(1)}, f32[3,6,4,128]{3,2,1,0:T(4,128)S(1)}, u32[]{:S(2)}, u32[]{:S(2)}) %collective-permute-start.4) | collective-permute-done | bytes 36896 | tf_op jit(solution)/shard_map/ppermute | solution.py:403
  61.6 6.4 %all-gather.4 = f32[4,3,6,4,128]{4,3,2,1,0:T(4,128)S(1)} all-gather(f32[2,3,6,4,128]{4,3,2,1,0:T(4,128)S(1)} %pad_maximum_fusion.2), channel_id=6, replica_groups=mesh['gx'=64,'gy'=8,'gz'=2] {'gz'}, dimensions={0}, use_global_device_ids=true | all-gather | bytes 221184 | tf_op jit(solution)/shard_map/all_gather | solution.py:407
  67.9 1.8 %shard_map.88 = f32[1,2,16]{2,1,0:T(2,128)} custom-call(s32[3]{0:T(128)S(1)} %pad_add_fusion.pos_ref, f32[3,6,4,128]{3,2,1,0:T(4,128)S(1)} %pad_maximum_fusion.3.mid_ref, f32[2,2,3,6,4,128]{5,4,3,2,1,0:T(4,128)S(1)} %bitcast.31), custom_call_target="tpu_custom_call" | custom-call | flops 100000 | bytes 100000 | tf_op jit(solution)/shard_map/pallas_call | solution.py:463
  (11 shorter events, 0.1 us)
Async XLA Ops:
  4.1 7.7 %copy-start = (f32[2,8,16,128]{3,2,1,0:T(8,128)S(1)}, f32[2,8,16,128]{3,2,1,0:T(8,128)}, u32[]{:S(2)}) copy-start(f32[2,8,16,128]{3,2,1,0:T(8,128)} %get-tuple-element.12) | copy-start | bytes 393220
  4.1 24.0 %all-to-all-start = ((f32[16,8,128]{2,1,0:T(8,128)}), f32[16,8,128]{2,1,0:T(8,128)S(1)}, u32[]{:S(2)}, u32[]{:S(2)}) async-start(f32[16,8,128]{2,1,0:T(8,128)} %bitcast.34), calls=%async_computation | async-start | bytes 131072 | tf_op jit(solution)/shard_map/all_to_all | solution.py:437
  13.8 5.7 %collective-permute-start = (f32[2,2,8,8,128]{4,3,2,1,0:T(8,128)S(1)}, f32[2,2,8,8,128]{4,3,2,1,0:T(8,128)S(1)}, u32[]{:S(2)}, u32[]{:S(2)}) collective-permute-start(f32[2,2,8,8,128]{4,3,2,1,0:T(8,128)S(1)} %slice_select_fusion.1), channel_id=1, source_target_pairs={{0,2},{2,4},{3,1},{4,6},{5,3},{6,8},{7,5},{8,10},{9,7},{10,12},{11... | collective-permute-start | bytes 393224 | tf_op jit(solution)/shard_map/ppermute | solution.py:403
  23.9 12.5 %collective-permute-start.2 = (f32[2,7,32,128]{3,2,1,0:T(8,128)S(1)}, f32[2,7,32,128]{3,2,1,0:T(8,128)S(1)}, u32[]{:S(2)}, u32[]{:S(2)}) collective-permute-start(f32[2,7,32,128]{3,2,1,0:T(8,128)S(1)} %slice_select_fusion), channel_id=1, source_target_pairs={{0,16},{16,32},{17,1},{32,48},{33,17},{48,64},{49,33},{64,80},{65,... | collective-permute-start | bytes 688136 | tf_op jit(solution)/shard_map/ppermute | solution.py:403
  30.0 6.4 %collective-permute-start.1 = (f32[2,6,32,128]{3,2,1,0:T(8,128)S(1)}, f32[2,6,32,128]{3,2,1,0:T(8,128)S(1)}, u32[]{:S(2)}, u32[]{:S(2)}) collective-permute-start(f32[2,6,32,128]{3,2,1,0:T(8,128)S(1)} %get-tuple-element.14), channel_id=1, source_target_pairs={{0,16},{16,32},{17,1},{32,48},{33,17},{48,64},{49,33},{64,80},{65,... | collective-permute-start | bytes 589832 | tf_op jit(solution)/shard_map/ppermute | solution.py:403
  46.3 4.4 %collective-permute-start.3 = (f32[6,4,128]{2,1,0:T(4,128)S(1)}, f32[6,4,128]{2,1,0:T(4,128)S(1)}, u32[]{:S(2)}, u32[]{:S(2)}) collective-permute-start(f32[6,4,128]{2,1,0:T(4,128)S(1)} %get-tuple-element.16), channel_id=1, source_target_pairs={{0,2},{2,4},{3,1},{4,6},{5,3},{6,8},{7,5},{8,10},{9,7},{10,12},{11... | collective-permute-start | bytes 36872 | tf_op jit(solution)/shard_map/ppermute | solution.py:403
  54.9 5.6 %collective-permute-start.5 = (f32[3,6,4,128]{3,2,1,0:T(4,128)S(1)}, f32[3,6,4,128]{3,2,1,0:T(4,128)S(1)}, u32[]{:S(2)}, u32[]{:S(2)}) collective-permute-start(f32[3,6,4,128]{3,2,1,0:T(4,128)S(1)} %pad_maximum_fusion.3.mid_ref), channel_id=1, source_target_pairs={{0,32},{16,48},{32,64},{33,1},{48,80},{49,17},{64,96},{65,33},{80,... | collective-permute-start | bytes 110600 | tf_op jit(solution)/shard_map/ppermute | solution.py:403
  56.8 4.7 %collective-permute-start.4 = (f32[3,6,4,128]{3,2,1,0:T(4,128)S(1)}, f32[3,6,4,128]{3,2,1,0:T(4,128)S(1)}, u32[]{:S(2)}, u32[]{:S(2)}) collective-permute-start(f32[3,6,4,128]{3,2,1,0:T(4,128)S(1)} %pad_maximum_fusion.3.mid_ref), channel_id=1, source_target_pairs={{0,16},{16,32},{17,1},{32,48},{33,17},{48,64},{49,33},{64,80},{65,... | collective-permute-start | bytes 110600 | tf_op jit(solution)/shard_map/ppermute | solution.py:403

commit v6 on v4

--- a/solution.py
+++ b/solution.py
@@ -12,6 +12,7 @@
 F32 = jnp.float32
 BF16 = jnp.bfloat16
 CORES = 2
+PACK = 2048.0
 VMEM_BYTES = 40 * 1024 * 1024
 MOST_VMEM = 60 * 1024 * 1024
 
@@ -59,7 +60,7 @@
 
 
 def fine_kernel(
-    count_ref, target_hbm, rhs_hbm, coef_hbm, grid_hbm, cond_hbm, solved_hbm, send_ref, own_ref,
+    count_ref, target_hbm, rhs_hbm, coef_hbm, grid_hbm, cond_hbm, solved_hbm, send_ref, away_ref, own_ref,
     target_ref, rhs_ref, coef_ref, grid_ref, cond_ref, solved_ref, sems
 ):
     live = count_ref[0]
@@ -153,8 +154,9 @@
     send_ref[...] = jnp.where(col < 64, packed[0], packed[1]) + small(lift, tags)
     loads[3].wait()
     loads[4].wait()
-    own_ref[0] = grid_ref[...]
-    own_ref[1] = cond_ref[...].astype(F32) * 0.5
+    for ref in (away_ref, own_ref):
+        ref[0] = grid_ref[...]
+        ref[1] = cond_ref[...].astype(F32) * 0.5
     store.wait()
 
 
@@ -259,20 +261,21 @@
     return total.reshape(layers // 2, rows // 2, 128)
 
 
-def base_kernel(
-    sizes, pos_ref, source_ref, chip_ref, side_ref, out_ref, pay_ref,
-    s_ref, h_ref, wx_ref, wy_ref, wz_ref, diag_ref, scale_ref, first_ref, second_ref,
-    res_ref, rows_ref,
+def weight_kernel(
+    sizes, pos_ref, chip_ref, side_ref,
+    wx_ref, wy_ref, wz_ref, diag_ref, scale_ref,
+    mid_wx_ref, mid_wy_ref, mid_wz_ref, mid_diag_ref, mid_scale_ref, low_scale_ref, low_h_ref,
+    h_ref, rows_ref,
 ):
-    gx, gy, core = pos_ref[0], pos_ref[1], pos_ref[2]
+    gx, gy = pos_ref[0], pos_ref[1]
     for number in range(2):
         lanes = slice(128 * number, 128 * number + 128)
-        s_ref[0:6, :, lanes] = side_ref[0, number, 0:6]
-        s_ref[6:14, :, lanes] = source_ref[number]
-        s_ref[14:20, :, lanes] = side_ref[1, number, 0:6]
-        h_ref[0:7, :, lanes] = side_ref[0, number, 6:13]
+        for place, part in ((0, 0), (15, 1)):
+            both = side_ref[part, number]
+            upper = jnp.floor(both * (1.0 / PACK))
+            h_ref[place : place + 4, :, lanes] = upper * (1.0 / 1024.0)
+            h_ref[place + 3 : place + 7, :, lanes] = (both - upper * PACK) * (1.0 / 1024.0)
         h_ref[7:15, :, lanes] = chip_ref[number, 1]
-        h_ref[15:22, :, lanes] = side_ref[1, number, 6:13]
     shape = (32, 256)
     lane = iota(shape, 1)
     y = iota(shape, 0) + (gy * 16 - 8)
@@ -287,16 +290,45 @@
         diagonal += jnp.where(lane > 0, before(h, 1), 0.0)
         x = gx * 8 + layer - 6
         inside = rows_in & (x >= 0) & (x < sizes[0])
-        scale = jnp.where(inside, DAMPING * inverse(diagonal), 0.0)
         diag_ref[layer] = diagonal
-        scale_ref[layer] = scale
+        scale_ref[layer] = jnp.where(inside, DAMPING * inverse(diagonal), 0.0)
         wx_ref[layer] = h + above
         wy_ref[layer] = h + hy
         wz_ref[layer] = jnp.where(lane < 255, h + hz, 0.0)
-        first_ref[layer] = s_ref[layer] * scale
         return 0
 
     lax.fori_loop(0, 20, weigh, 0, unroll=True)
+    h = coarser(h_ref[1:21], pair_matrix(256), 0.125, rows_ref)
+    inside = within((8, 16, 128), (gx * 4, gy * 8), -2, -4, (sizes[0] // 2, sizes[1] // 2))
+    diagonal, scale, wx, wy, wz = prepare(h, inside, 128)
+    mid_wx_ref[...] = wx
+    mid_wy_ref[...] = wy
+    mid_wz_ref[...] = wz
+    mid_diag_ref[...] = diagonal
+    mid_scale_ref[...] = scale
+    h = coarser(h[1:-1], pair_matrix(128), 0.125, rows_ref)
+    _, scale, _, _, _ = prepare(h, jnp.full((2, 8, 128), True), 64)
+    low_scale_ref[...] = scale
+    low_h_ref[...] = h[1:3]
+
+
+def base_kernel(
+    core_ref, source_ref, side_ref,
+    wx_ref, wy_ref, wz_ref, diag_ref, scale_ref,
+    mid_wx_ref, mid_wy_ref, mid_wz_ref, mid_diag_ref, mid_scale_ref, low_scale_ref, low_h_ref,
+    out_ref, pay_ref, s_ref, first_ref, second_ref, res_ref, rows_ref,
+):
+    for number in range(2):
+        lanes = slice(128 * number, 128 * number + 128)
+        s_ref[0:6, :, lanes] = side_ref[0, number]
+        s_ref[6:14, :, lanes] = source_ref[number]
+        s_ref[14:20, :, lanes] = side_ref[1, number]
+
+    def begin(layer, _):
+        first_ref[layer] = s_ref[layer] * scale_ref[layer]
+        return 0
+
+    lax.fori_loop(0, 20, begin, 0, unroll=True)
 
     def sides(ref, layer):
         u, wy, wz = ref[layer], wy_ref[layer], wz_ref[layer]
@@ -318,26 +350,19 @@
 
     lax.fori_loop(2, 18, leave, 0, unroll=True)
     own = second_ref[6:14, 8:24, :]
-    out_ref[...] = jnp.where(core == 0, own[:, :, :128], own[:, :, 128:])
-
-    zoom = pair_matrix(256)
-    source = coarser(res_ref[...], zoom, 0.5, rows_ref)
-    h = coarser(h_ref[1:21], zoom, 0.125, rows_ref)
-    inside = within(source.shape, (gx * 4, gy * 8), -2, -4, (sizes[0] // 2, sizes[1] // 2))
-    diagonal, scale, wx, wy, wz = prepare(h, inside, 128)
+    out_ref[...] = jnp.where(core_ref[2] == 0, own[:, :, :128], own[:, :, 128:])
+
+    source = coarser(res_ref[...], pair_matrix(256), 0.5, rows_ref)
+    scale, wx, wy, wz = mid_scale_ref[...], mid_wx_ref[...], mid_wy_ref[...], mid_wz_ref[...]
     first = source * scale
     total = neighbours(first, wx[1:-1], wy[1:-1], wz[1:-1])
     second = first[1:-1] + scale[1:-1] * (REST * source[1:-1] + total)
     total = neighbours(second, wx[2:-2], wy[2:-2], wz[2:-2])
-    residue = source[2:-2] - diagonal[2:-2] * second[1:-1] + total
-
-    zoom = pair_matrix(128)
-    source = coarser(residue, zoom, 0.5, rows_ref)
-    h = coarser(h[1:-1], zoom, 0.125, rows_ref)
-    _, scale, _, _, _ = prepare(h, jnp.full(source.shape, True), 64)
+    residue = source[2:-2] - mid_diag_ref[2:-2] * second[1:-1] + total
+    source = coarser(residue, pair_matrix(128), 0.5, rows_ref)
     pay_ref[0:2] = source[:, 2:6]
-    pay_ref[2:4] = (source * scale)[:, 2:6]
-    pay_ref[4:6] = h[1:3, 2:6]
+    pay_ref[2:4] = (source * low_scale_ref[...])[:, 2:6]
+    pay_ref[4:6] = low_h_ref[:, 2:6]
 
 
 def deep_kernel(sizes, pos_ref, mid_ref, side_ref, out_ref, win_ref, rows_ref):
@@ -422,9 +447,10 @@
     smem = pl.BlockSpec(memory_space=pltpu.SMEM)
     struct = jax.ShapeDtypeStruct
     hbm = pl.BlockSpec(memory_space=pltpu.HBM)
-    fine_solution, send, own = call(
+    own_block = struct((2, *coarse_rhs.shape), F32)
+    fine_solution, send, away, own = call(
         fine_kernel,
-        (struct(fine_rhs.shape, F32), struct((128, 128), F32), struct((2, 8, 16, 128), F32)),
+        (struct(fine_rhs.shape, F32), struct((128, 128), F32), own_block, own_block),
         [smem, hbm, hbm, hbm, hbm, hbm],
         [
             pltpu.VMEM((1, 32), jnp.int32),
@@ -435,31 +461,43 @@
             pltpu.VMEM(fine_rhs.shape, F32),
             pltpu.SemaphoreType.DMA((6,)),
         ],
-        outs=[hbm, vmem, vmem],
+        outs=[hbm, vmem, vmem, vmem],
         vmem=MOST_VMEM,
     )(patch_count, patch_target.reshape(1, 32), fine_rhs, fine_coef, coarse_rhs, coarse_coef)
     got = lax.all_to_all(send.reshape(16, 8, 128), ("gy", "gz"), 0, 0).reshape(128, 128)
-    below, above = exchanged(own, own, "gy")
+    below, above = exchanged(away, away, "gy")
     chip = shared(jnp.concatenate([below[:, :, 8:], own, above[:, :, :8]], axis=2))
-    edge = split_send(jnp.where(core == 0, chip[:, 1, 1:], chip[:, 1, :7]), "gx", 1)
+    edge = jnp.where(core == 0, chip[:, 1, 1:], chip[:, 1, :7])
+    edge = split_send(edge[:, :4] * (1024.0 * PACK) + edge[:, 3:] * 1024.0, "gx", 1)
     source, pay = call(
         place_kernel,
         (struct((2, 8, 32, 128), F32), struct((2, 6, 32, 128), F32)),
         [smem, vmem, vmem],
         outs=[vmem] * 2,
     )(pos, got, chip)
-    side = shared(jnp.concatenate([split_send(pay, "gx", 1), edge], axis=1))
     grid = (32, 256)
+    window = struct((20, *grid), F32)
+    block = struct((8, 16, 128), F32)
+    low = struct((2, 8, 128), F32)
+    weights = call(
+        functools.partial(weight_kernel, sizes),
+        (window,) * 5 + (struct((9, 16, 128), F32),) + (block,) * 4 + (low,) * 2,
+        [smem, vmem, vmem],
+        [pltpu.VMEM((22, *grid), F32), pltpu.VMEM((320, 128), F32)],
+        flops=5_000_000,
+        outs=[vmem] * 12,
+    )(pos, chip, shared(edge))
+    moved, last = lax.optimization_barrier((split_send(pay, "gx", 1), weights[-1]))
+    side = shared(moved)
     coarse_solution, pay = call(
-        functools.partial(base_kernel, sizes),
-        (struct((8, 16, 128), F32), struct((6, 4, 128), F32)),
-        [smem, vmem, vmem, vmem],
-        [pltpu.VMEM((20, *grid), F32), pltpu.VMEM((22, *grid), F32)]
-        + [pltpu.VMEM((20, *grid), F32)] * 7
+        base_kernel,
+        (block, struct((6, 4, 128), F32)),
+        [smem] + [vmem] * 14,
+        [pltpu.VMEM((20, *grid), F32)] * 3
         + [pltpu.VMEM((16, *grid), F32), pltpu.VMEM((320, 128), F32)],
         flops=5_000_000,
         outs=[vmem] * 2,
-    )(pos, source, chip, side)
+    )(pos, source, side, *weights[:-1], last)
     halo = shared(split_send(pay, "gy", 1))
     mid = jnp.stack([halo[0], pay, halo[1]])
     sides = shared(jnp.stack([split_send(mid, "gx", 1), split_send(mid, "gx", 2)]))

time: 66.8 us -> 67.6 us (1.012)
  waiting for transfers between devices: 8.52 us -> 5.93 us
  blocking collectives: 19.2 us -> 20.8 us
  starting transfers between devices: 26.4 us -> 27.6 us
    ppermute x5, waiting for transfers between devices: 8.52 us -> 5.92 us  [split_send(): return lax.ppermute(values, (axis, 'gz'), pairs)]
    all_gather x4 -> x5, blocking collectives: 19.2 us -> 20.8 us  [shared(): return lax.all_gather(values, 'gz')]
    ppermute x2, starting transfers between devices: 5.28 us -> 6.49 us  [exchanged(): return (lax.ppermute(up, axis, pairs), lax.ppermute(down, axis, back))]
    pallas_call x1 -> x2, Pallas kernels: 3.43 us -> 3.84 us  [the longest x1 2.4 us: per_device(): call(base_kernel, (block, struct((6, 4, 128), F32)), [smem] + [vmem] * 14...]
  transfers between devices with their start and end apart: 8 -> 8, of which waited for: 4 -> 3; matrix products, arithmetic and copies ran while one was open for 0% -> 0% of each run, Pallas kernels for 3% -> 5%
where the time goes in v6:
time: 67.6 us; the launch traced here: 67.2 us
  starting transfers between devices  27.6 us (41%)
  blocking collectives  20.8 us (31%)
  Pallas kernels  10.3 us (15%)
  waiting for transfers between devices  5.93 us (9%)
  between operations  1.43 us (2%)
  local copies, waits for them, and re-layouts  0.87 us (1%)
    all_gather x5, blocking collectives, shared(): return lax.all_gather(values, 'gz')  20.8 us
    ppermute x5, starting transfers between devices, split_send(): return lax.ppermute(values, (axis, 'gz'), pairs)  13 us
    all_to_all x1, starting transfers between devices, per_device(): lax.all_to_all(send.reshape(16, 8, 128), ('gy', 'gz'), 0, 0)  8.11 us
    ppermute x2, starting transfers between devices, exchanged(): return (lax.ppermute(up, axis, pairs), lax.ppermute(down, axis, back))  6.49 us
    ppermute x5, waiting for transfers between devices, split_send(): return lax.ppermute(values, (axis, 'gz'), pairs)  5.92 us
    pallas_call x1, Pallas kernels, per_device(): call(fine_kernel, (struct(fine_rhs.shape, F32), struct((128, 128), F32),...  2.83 us
    pallas_call x1, Pallas kernels, per_device(): call(base_kernel, (block, struct((6, 4, 128), F32)), [smem] + [vmem] * 14...  2.4 us
    pallas_call x1, Pallas kernels, per_device(): call(place_kernel, (struct((2, 8, 32, 128), F32), struct((2, 6, 32, 128),...  1.91 us
  transfers between devices with their start and end apart: 8, of which 3 were waited for; matrix products, arithmetic and copies ran while one was open for 0% of the time, Pallas kernels for 5%

profile of v6, /device:TPU:521, one launch (start us, length us, event | category | flops | bytes accessed | tf_op | source)
XLA Modules:
  0.0 67.2 jit_solution(15685060700128213104)
XLA Ops:
  1.3 2.8 %shard_map.85 = (f32[32,8,64]{2,1,0:T(8,128)}, f32[128,128]{1,0:T(8,128)}, f32[2,8,16,128]{3,2,1,0:T(8,128)}, f32[2,8,16,128]{3,2,1,0:T(8,128)}) custom-call(s32[1]{0:T(128)S(6)} %copy.9.count_ref, s32[1,32]{1,0:T(1,128)} %bitcast.30, f32[32,8,64]{2,1,0:T(8,128)} %rhs_hbm.1, bf16[32,8,64]{2,1,0:T(8,128)(2,1)} %coef_hbm.1, f32[8,16,128]{2,1,0:T(8,128)} %grid_hbm.1, ...), custom_call_target="tpu_custom_call" | custom-call | flops 100000 | bytes 100000 | tf_op jit(solution)/shard_map/pallas_call | solution.py:451
  4.1 2.2 %collective-permute-start = (f32[2,8,16,128]{3,2,1,0:T(8,128)}, f32[2,8,16,128]{3,2,1,0:T(8,128)S(1)}, u32[]{:S(2)}, u32[]{:S(2)}) collective-permute-start(f32[2,8,16,128]{3,2,1,0:T(8,128)} %get-tuple-element.27), channel_id=1, source_target_pairs={{0,2},{2,4},{4,6},{6,8},{8,10},{10,12},{12,14},{1,3},{3,5},{5,7},{... | collective-permute-start | bytes 393224 | tf_op jit(solution)/shard_map/ppermute | solution.py:432
  6.3 4.3 %collective-permute-start.1 = (f32[2,8,16,128]{3,2,1,0:T(8,128)}, f32[2,8,16,128]{3,2,1,0:T(8,128)S(1)}, u32[]{:S(2)}, u32[]{:S(2)}) collective-permute-start(f32[2,8,16,128]{3,2,1,0:T(8,128)} %get-tuple-element.27), channel_id=1, source_target_pairs={{2,0},{4,2},{6,4},{8,6},{10,8},{12,10},{14,12},{3,1},{5,3},{7,5},{... | collective-permute-start | bytes 393224 | tf_op jit(solution)/shard_map/ppermute | solution.py:432
  10.6 8.1 %all-to-all-start = ((f32[16,8,128]{2,1,0:T(8,128)}), f32[16,8,128]{2,1,0:T(8,128)S(1)}, u32[]{:S(2)}, u32[]{:S(2)}) async-start(f32[16,8,128]{2,1,0:T(8,128)} %bitcast.27), calls=%async_computation | async-start | bytes 131072 | tf_op jit(solution)/shard_map/all_to_all | solution.py:467
  18.8 0.8 %copy-done = f32[2,8,16,128]{3,2,1,0:T(8,128)S(1)} copy-done((f32[2,8,16,128]{3,2,1,0:T(8,128)S(1)}, f32[2,8,16,128]{3,2,1,0:T(8,128)}, u32[]{:S(2)}) %copy-start) | copy-done | bytes 131096
  19.7 2.2 %all-gather = f32[4,8,32,128]{3,2,1,0:T(8,128)S(1)} all-gather(f32[2,8,32,128]{3,2,1,0:T(8,128)S(1)} %pad_maximum_fusion), channel_id=2, replica_groups=mesh['gx'=64,'gy'=8,'gz'=2] {'gz'}, dimensions={0}, use_global_device_ids=true | all-gather | bytes 786432 | tf_op jit(solution)/shard_map/all_gather | solution.py:436
  21.9 4.1 %collective-permute-start.3 = (f32[2,4,32,128]{3,2,1,0:T(8,128)S(1)}, f32[2,4,32,128]{3,2,1,0:T(8,128)S(1)}, u32[]{:S(2)}, u32[]{:S(2)}) collective-permute-start(f32[2,4,32,128]{3,2,1,0:T(8,128)S(1)} %fusion.1), channel_id=1, source_target_pairs={{0,16},{16,32},{17,1},{32,48},{33,17},{48,64},{49,33},{64,80},{65,... | collective-permute-start | bytes 393224 | tf_op jit(solution)/shard_map/ppermute | solution.py:425
  26.0 0.1 pad_add_fusion.pos_ref.core_ref
  26.1 0.0 all-to-all-done
  26.1 1.9 %shard_map.86 = (f32[2,8,32,128]{3,2,1,0:T(8,128)S(1)}, f32[2,6,32,128]{3,2,1,0:T(8,128)S(1)}) custom-call(s32[3]{0:T(128)S(1)} %pad_add_fusion.pos_ref.core_ref, f32[128,128]{1,0:T(8,128)S(1)} %bitcast.25, f32[2,2,8,32,128]{4,3,2,1,0:T(8,128)S(1)} %bitcast.20), custom_call_target="tpu_custom_call" | custom-call | flops 100000 | bytes 100000 | tf_op jit(solution)/shard_map/pallas_call | solution.py:472
  28.0 2.9 %collective-permute-start.2 = (f32[2,6,32,128]{3,2,1,0:T(8,128)S(1)}, f32[2,6,32,128]{3,2,1,0:T(8,128)S(1)}, u32[]{:S(2)}, u32[]{:S(2)}) collective-permute-start(f32[2,6,32,128]{3,2,1,0:T(8,128)S(1)} %get-tuple-element.30), channel_id=1, source_target_pairs={{0,16},{16,32},{17,1},{32,48},{33,17},{48,64},{49,33},{64,80},{65,... | collective-permute-start | bytes 589832 | tf_op jit(solution)/shard_map/ppermute | solution.py:425
  30.9 3.2 %all-gather.1 = f32[4,4,32,128]{3,2,1,0:T(8,128)S(1)} all-gather(f32[2,4,32,128]{3,2,1,0:T(8,128)S(1)} %collective-permute-done.3), channel_id=3, replica_groups=mesh['gx'=64,'gy'=8,'gz'=2] {'gz'}, dimensions={0}, use_global_device_ids=true | all-gather | bytes 393216 | tf_op jit(solution)/shard_map/all_gather | solution.py:436
  34.1 1.4 %shard_map.87 = (f32[20,32,256]{2,1,0:T(8,128)S(1)}, f32[20,32,256]{2,1,0:T(8,128)S(1)}, f32[20,32,256]{2,1,0:T(8,128)S(1)}, f32[20,32,256]{2,1,0:T(8,128)S(1)},...) custom-call(s32[3]{0:T(128)S(1)} %pad_add_fusion.pos_ref.core_ref, ...), custom_call_target="tpu_custom_call" | custom-call | flops 5000000 | bytes 5000000 | tf_op jit(solution)/shard_map/pallas_call | solution.py:482
  35.5 4.9 %all-gather.2 = f32[4,6,32,128]{3,2,1,0:T(8,128)S(1)} all-gather(f32[2,6,32,128]{3,2,1,0:T(8,128)S(1)} %collective-permute-done.2), channel_id=4, replica_groups=mesh['gx'=64,'gy'=8,'gz'=2] {'gz'}, dimensions={0}, use_global_device_ids=true | all-gather | bytes 589824 | tf_op jit(solution)/shard_map/all_gather | solution.py:436
  40.5 2.4 %shard_map.88 = (f32[8,16,128]{2,1,0:T(8,128)}, f32[6,4,128]{2,1,0:T(4,128)S(1)}) custom-call(s32[3]{0:T(128)S(1)} %pad_add_fusion.pos_ref.core_ref, f32[2,8,32,128]{3,2,1,0:T(8,128)S(1)} %get-tuple-element.29.source_ref, f32[2,2,6,32,128]{4,3,2,1,0:T(8,128)S(1)} %bitcast.22, f32[20,32,256]{2,1,0:T(8,128)S(1)} %get-tuple-element.33.wx_ref, ...), custom_call_target="tpu_custom_call" | custom-call | flops 5000000 | bytes 5000000 | tf_op jit(solution)/shard_map/pallas_call | solution.py:492
  42.9 2.2 %collective-permute-start.4 = (f32[6,4,128]{2,1,0:T(4,128)S(1)}, f32[6,4,128]{2,1,0:T(4,128)S(1)}, u32[]{:S(2)}, u32[]{:S(2)}) collective-permute-start(f32[6,4,128]{2,1,0:T(4,128)S(1)} %get-tuple-element.46), channel_id=1, source_target_pairs={{0,2},{2,4},{3,1},{4,6},{5,3},{6,8},{7,5},{8,10},{9,7},{10,12},{11... | collective-permute-start | bytes 36872 | tf_op jit(solution)/shard_map/ppermute | solution.py:425
  45.0 2.2 %collective-permute-done.4 = f32[6,4,128]{2,1,0:T(4,128)S(1)} collective-permute-done((f32[6,4,128]{2,1,0:T(4,128)S(1)}, f32[6,4,128]{2,1,0:T(4,128)S(1)}, u32[]{:S(2)}, u32[]{:S(2)}) %collective-permute-start.4) | collective-permute-done | bytes 12320 | tf_op jit(solution)/shard_map/ppermute | solution.py:425
  47.3 4.2 %all-gather.3 = f32[12,4,128]{2,1,0:T(4,128)S(1)} all-gather(f32[6,4,128]{2,1,0:T(4,128)S(1)} %collective-permute-done.4), channel_id=5, replica_groups=mesh['gx'=64,'gy'=8,'gz'=2] {'gz'}, dimensions={0}, use_global_device_ids=true | all-gather | bytes 36864 | tf_op jit(solution)/shard_map/all_gather | solution.py:436
  51.5 2.0 %collective-permute-start.5 = (f32[3,6,4,128]{3,2,1,0:T(4,128)S(1)}, f32[3,6,4,128]{3,2,1,0:T(4,128)S(1)}, u32[]{:S(2)}, u32[]{:S(2)}) collective-permute-start(f32[3,6,4,128]{3,2,1,0:T(4,128)S(1)} %pad_maximum_fusion.2.mid_ref), channel_id=1, source_target_pairs={{0,16},{16,32},{17,1},{32,48},{33,17},{48,64},{49,33},{64,80},{65,... | collective-permute-start | bytes 110600 | tf_op jit(solution)/shard_map/ppermute | solution.py:425
  53.5 1.9 %collective-permute-start.6 = (f32[3,6,4,128]{3,2,1,0:T(4,128)S(1)}, f32[3,6,4,128]{3,2,1,0:T(4,128)S(1)}, u32[]{:S(2)}, u32[]{:S(2)}) collective-permute-start(f32[3,6,4,128]{3,2,1,0:T(4,128)S(1)} %pad_maximum_fusion.2.mid_ref), channel_id=1, source_target_pairs={{0,32},{16,48},{32,64},{33,1},{48,80},{49,17},{64,96},{65,33},{80,... | collective-permute-start | bytes 110600 | tf_op jit(solution)/shard_map/ppermute | solution.py:425
  55.4 0.8 %collective-permute-done.5 = f32[3,6,4,128]{3,2,1,0:T(4,128)S(1)} collective-permute-done((f32[3,6,4,128]{3,2,1,0:T(4,128)S(1)}, f32[3,6,4,128]{3,2,1,0:T(4,128)S(1)}, u32[]{:S(2)}, u32[]{:S(2)}) %collective-permute-start.5) | collective-permute-done | bytes 36896 | tf_op jit(solution)/shard_map/ppermute | solution.py:425
  56.2 2.9 %collective-permute-done.6 = f32[3,6,4,128]{3,2,1,0:T(4,128)S(1)} collective-permute-done((f32[3,6,4,128]{3,2,1,0:T(4,128)S(1)}, f32[3,6,4,128]{3,2,1,0:T(4,128)S(1)}, u32[]{:S(2)}, u32[]{:S(2)}) %collective-permute-start.6) | collective-permute-done | bytes 36896 | tf_op jit(solution)/shard_map/ppermute | solution.py:425
  59.1 6.3 %all-gather.4 = f32[4,3,6,4,128]{4,3,2,1,0:T(4,128)S(1)} all-gather(f32[2,3,6,4,128]{4,3,2,1,0:T(4,128)S(1)} %pad_maximum_fusion.1), channel_id=6, replica_groups=mesh['gx'=64,'gy'=8,'gz'=2] {'gz'}, dimensions={0}, use_global_device_ids=true | all-gather | bytes 221184 | tf_op jit(solution)/shard_map/all_gather | solution.py:436
  65.4 1.8 %shard_map.89 = f32[1,2,16]{2,1,0:T(2,128)} custom-call(s32[3]{0:T(128)S(1)} %pad_add_fusion.pos_ref.core_ref, f32[3,6,4,128]{3,2,1,0:T(4,128)S(1)} %pad_maximum_fusion.2.mid_ref, f32[2,2,3,6,4,128]{5,4,3,2,1,0:T(4,128)S(1)} %bitcast.24), custom_call_target="tpu_custom_call" | custom-call | flops 100000 | bytes 100000 | tf_op jit(solution)/shard_map/pallas_call | solution.py:504
  (13 shorter events, 0.1 us)
Async XLA Ops:
  4.1 14.6 %collective-permute-start = (f32[2,8,16,128]{3,2,1,0:T(8,128)}, f32[2,8,16,128]{3,2,1,0:T(8,128)S(1)}, u32[]{:S(2)}, u32[]{:S(2)}) collective-permute-start(f32[2,8,16,128]{3,2,1,0:T(8,128)} %get-tuple-element.27), channel_id=1, source_target_pairs={{0,2},{2,4},{4,6},{6,8},{8,10},{10,12},{12,14},{1,3},{3,5},{5,7},{... | collective-permute-start | bytes 393224 | tf_op jit(solution)/shard_map/ppermute | solution.py:432
  6.3 12.4 %collective-permute-start.1 = (f32[2,8,16,128]{3,2,1,0:T(8,128)}, f32[2,8,16,128]{3,2,1,0:T(8,128)S(1)}, u32[]{:S(2)}, u32[]{:S(2)}) collective-permute-start(f32[2,8,16,128]{3,2,1,0:T(8,128)} %get-tuple-element.27), channel_id=1, source_target_pairs={{2,0},{4,2},{6,4},{8,6},{10,8},{12,10},{14,12},{3,1},{5,3},{7,5},{... | collective-permute-start | bytes 393224 | tf_op jit(solution)/shard_map/ppermute | solution.py:432
  10.6 15.4 %all-to-all-start = ((f32[16,8,128]{2,1,0:T(8,128)}), f32[16,8,128]{2,1,0:T(8,128)S(1)}, u32[]{:S(2)}, u32[]{:S(2)}) async-start(f32[16,8,128]{2,1,0:T(8,128)} %bitcast.27), calls=%async_computation | async-start | bytes 131072 | tf_op jit(solution)/shard_map/all_to_all | solution.py:467
  18.7 0.9 %copy-start = (f32[2,8,16,128]{3,2,1,0:T(8,128)S(1)}, f32[2,8,16,128]{3,2,1,0:T(8,128)}, u32[]{:S(2)}) copy-start(f32[2,8,16,128]{3,2,1,0:T(8,128)} %get-tuple-element.28) | copy-start | bytes 393220
  21.9 9.0 %collective-permute-start.3 = (f32[2,4,32,128]{3,2,1,0:T(8,128)S(1)}, f32[2,4,32,128]{3,2,1,0:T(8,128)S(1)}, u32[]{:S(2)}, u32[]{:S(2)}) collective-permute-start(f32[2,4,32,128]{3,2,1,0:T(8,128)S(1)} %fusion.1), channel_id=1, source_target_pairs={{0,16},{16,32},{17,1},{32,48},{33,17},{48,64},{49,33},{64,80},{65,... | collective-permute-start | bytes 393224 | tf_op jit(solution)/shard_map/ppermute | solution.py:425
  28.0 7.5 %collective-permute-start.2 = (f32[2,6,32,128]{3,2,1,0:T(8,128)S(1)}, f32[2,6,32,128]{3,2,1,0:T(8,128)S(1)}, u32[]{:S(2)}, u32[]{:S(2)}) collective-permute-start(f32[2,6,32,128]{3,2,1,0:T(8,128)S(1)} %get-tuple-element.30), channel_id=1, source_target_pairs={{0,16},{16,32},{17,1},{32,48},{33,17},{48,64},{49,33},{64,80},{65,... | collective-permute-start | bytes 589832 | tf_op jit(solution)/shard_map/ppermute | solution.py:425
  42.9 4.4 %collective-permute-start.4 = (f32[6,4,128]{2,1,0:T(4,128)S(1)}, f32[6,4,128]{2,1,0:T(4,128)S(1)}, u32[]{:S(2)}, u32[]{:S(2)}) collective-permute-start(f32[6,4,128]{2,1,0:T(4,128)S(1)} %get-tuple-element.46), channel_id=1, source_target_pairs={{0,2},{2,4},{3,1},{4,6},{5,3},{6,8},{7,5},{8,10},{9,7},{10,12},{11... | collective-permute-start | bytes 36872 | tf_op jit(solution)/shard_map/ppermute | solution.py:425
  51.5 4.7 %collective-permute-start.5 = (f32[3,6,4,128]{3,2,1,0:T(4,128)S(1)}, f32[3,6,4,128]{3,2,1,0:T(4,128)S(1)}, u32[]{:S(2)}, u32[]{:S(2)}) collective-permute-start(f32[3,6,4,128]{3,2,1,0:T(4,128)S(1)} %pad_maximum_fusion.2.mid_ref), channel_id=1, source_target_pairs={{0,16},{16,32},{17,1},{32,48},{33,17},{48,64},{49,33},{64,80},{65,... | collective-permute-start | bytes 110600 | tf_op jit(solution)/shard_map/ppermute | solution.py:425
  53.5 5.6 %collective-permute-start.6 = (f32[3,6,4,128]{3,2,1,0:T(4,128)S(1)}, f32[3,6,4,128]{3,2,1,0:T(4,128)S(1)}, u32[]{:S(2)}, u32[]{:S(2)}) collective-permute-start(f32[3,6,4,128]{3,2,1,0:T(4,128)S(1)} %pad_maximum_fusion.2.mid_ref), channel_id=1, source_target_pairs={{0,32},{16,48},{32,64},{33,1},{48,80},{49,17},{64,96},{65,33},{80,... | collective-permute-start | bytes 110600 | tf_op jit(solution)/shard_map/ppermute | solution.py:425

commit v7 on v6

--- a/solution.py
+++ b/solution.py
@@ -60,8 +60,8 @@
 
 
 def fine_kernel(
-    count_ref, target_hbm, rhs_hbm, coef_hbm, grid_hbm, cond_hbm, solved_hbm, send_ref, away_ref, own_ref,
-    target_ref, rhs_ref, coef_ref, grid_ref, cond_ref, solved_ref, sems
+    count_ref, target_hbm, rhs_hbm, coef_hbm, grid_hbm, cond_hbm, second_ref, send_ref, away_ref, own_ref,
+    target_ref, rhs_ref, coef_ref, grid_ref, cond_ref, sems
 ):
     live = count_ref[0]
     loads = [
@@ -106,11 +106,7 @@
     first = source * scale
     second = first + scale * (REST * source + sides(first))
     residue = source - diagonal * second + sides(second)
-    slot = iota((half, 8, 64), 0)
-    solved_ref[:half] = jnp.where(slot < live, second[:, :, :64], 0.0)
-    solved_ref[half:] = jnp.where(slot + half < live, second[:, :, 64:], 0.0)
-    store = pltpu.make_async_copy(solved_ref, solved_hbm, sems.at[5])
-    store.start()
+    second_ref[...] = second
 
     loads[2].wait()
     square = (128, 128)
@@ -157,11 +153,19 @@
     for ref in (away_ref, own_ref):
         ref[0] = grid_ref[...]
         ref[1] = cond_ref[...].astype(F32) * 0.5
-    store.wait()
-
-
-def place_kernel(pos_ref, got_ref, chip_ref, source_ref, pay_ref):
-    first = jnp.where(pos_ref[2] == 0, 2, 0)
+
+
+def store_kernel(count_ref, second_ref, solved_ref):
+    live = count_ref[0]
+    second = second_ref[...]
+    half = second.shape[0]
+    slot = iota((half, 8, 64), 0)
+    solved_ref[:half] = jnp.where(slot < live, second[:, :, :64], 0.0)
+    solved_ref[half:] = jnp.where(slot + half < live, second[:, :, 64:], 0.0)
+
+
+def place_kernel(got_ref, chip_ref, source_ref, pay_ref):
+    first = jnp.where(lax.axis_index("gz") == 0, 2, 0)
     square = (128, 128)
     row, col = iota(square, 0), iota(square, 1)
     slot = (row >> 4) & 1
@@ -262,12 +266,12 @@
 
 
 def weight_kernel(
-    sizes, pos_ref, chip_ref, side_ref,
+    sizes, chip_ref, side_ref,
     wx_ref, wy_ref, wz_ref, diag_ref, scale_ref,
     mid_wx_ref, mid_wy_ref, mid_wz_ref, mid_diag_ref, mid_scale_ref, low_scale_ref, low_h_ref,
     h_ref, rows_ref,
 ):
-    gx, gy = pos_ref[0], pos_ref[1]
+    gx, gy = lax.axis_index("gx"), lax.axis_index("gy")
     for number in range(2):
         lanes = slice(128 * number, 128 * number + 128)
         for place, part in ((0, 0), (15, 1)):
@@ -313,7 +317,7 @@
 
 
 def base_kernel(
-    core_ref, source_ref, side_ref,
+    source_ref, side_ref,
     wx_ref, wy_ref, wz_ref, diag_ref, scale_ref,
     mid_wx_ref, mid_wy_ref, mid_wz_ref, mid_diag_ref, mid_scale_ref, low_scale_ref, low_h_ref,
     out_ref, pay_ref, s_ref, first_ref, second_ref, res_ref, rows_ref,
@@ -350,7 +354,7 @@
 
     lax.fori_loop(2, 18, leave, 0, unroll=True)
     own = second_ref[6:14, 8:24, :]
-    out_ref[...] = jnp.where(core_ref[2] == 0, own[:, :, :128], own[:, :, 128:])
+    out_ref[...] = jnp.where(lax.axis_index("gz") == 0, own[:, :, :128], own[:, :, 128:])
 
     source = coarser(res_ref[...], pair_matrix(256), 0.5, rows_ref)
     scale, wx, wy, wz = mid_scale_ref[...], mid_wx_ref[...], mid_wy_ref[...], mid_wz_ref[...]
@@ -365,8 +369,8 @@
     pay_ref[4:6] = low_h_ref[:, 2:6]
 
 
-def deep_kernel(sizes, pos_ref, mid_ref, side_ref, out_ref, win_ref, rows_ref):
-    gx, gy, core = pos_ref[0], pos_ref[1], pos_ref[2]
+def deep_kernel(sizes, mid_ref, side_ref, out_ref, win_ref, rows_ref):
+    gx, gy, core = (lax.axis_index(name) for name in ("gx", "gy", "gz"))
     win_ref[...] = jnp.zeros(win_ref.shape, F32)
     for number in range(3):
         for part in range(3):
@@ -438,7 +442,6 @@
 
 def per_device(fine_rhs, fine_coef, coarse_rhs, coarse_coef, patch_count, patch_target):
     core = lax.axis_index("gz")
-    pos = jnp.stack([lax.axis_index("gx"), lax.axis_index("gy"), core])
     sizes = (
         lax.axis_size("gx") * coarse_rhs.shape[0],
         lax.axis_size("gy") * coarse_rhs.shape[1],
@@ -448,9 +451,9 @@
     struct = jax.ShapeDtypeStruct
     hbm = pl.BlockSpec(memory_space=pltpu.HBM)
     own_block = struct((2, *coarse_rhs.shape), F32)
-    fine_solution, send, away, own = call(
+    second, send, away, own = call(
         fine_kernel,
-        (struct(fine_rhs.shape, F32), struct((128, 128), F32), own_block, own_block),
+        (struct((16, 8, 128), F32), struct((128, 128), F32), own_block, own_block),
         [smem, hbm, hbm, hbm, hbm, hbm],
         [
             pltpu.VMEM((1, 32), jnp.int32),
@@ -458,12 +461,14 @@
             pltpu.VMEM(fine_coef.shape, fine_coef.dtype),
             pltpu.VMEM(coarse_rhs.shape, F32),
             pltpu.VMEM(coarse_coef.shape, coarse_coef.dtype),
-            pltpu.VMEM(fine_rhs.shape, F32),
-            pltpu.SemaphoreType.DMA((6,)),
+            pltpu.SemaphoreType.DMA((5,)),
         ],
-        outs=[hbm, vmem, vmem, vmem],
+        outs=[vmem] * 4,
         vmem=MOST_VMEM,
     )(patch_count, patch_target.reshape(1, 32), fine_rhs, fine_coef, coarse_rhs, coarse_coef)
+    fine_solution = call(store_kernel, struct(fine_rhs.shape, F32), [smem, vmem])(
+        patch_count, second
+    )
     got = lax.all_to_all(send.reshape(16, 8, 128), ("gy", "gz"), 0, 0).reshape(128, 128)
     below, above = exchanged(away, away, "gy")
     chip = shared(jnp.concatenate([below[:, :, 8:], own, above[:, :, :8]], axis=2))
@@ -472,9 +477,9 @@
     source, pay = call(
         place_kernel,
         (struct((2, 8, 32, 128), F32), struct((2, 6, 32, 128), F32)),
-        [smem, vmem, vmem],
+        [vmem, vmem],
         outs=[vmem] * 2,
-    )(pos, got, chip)
+    )(got, chip)
     grid = (32, 256)
     window = struct((20, *grid), F32)
     block = struct((8, 16, 128), F32)
@@ -482,31 +487,31 @@
     weights = call(
         functools.partial(weight_kernel, sizes),
         (window,) * 5 + (struct((9, 16, 128), F32),) + (block,) * 4 + (low,) * 2,
-        [smem, vmem, vmem],
+        [vmem, vmem],
         [pltpu.VMEM((22, *grid), F32), pltpu.VMEM((320, 128), F32)],
         flops=5_000_000,
         outs=[vmem] * 12,
-    )(pos, chip, shared(edge))
+    )(chip, shared(edge))
     moved, last = lax.optimization_barrier((split_send(pay, "gx", 1), weights[-1]))
     side = shared(moved)
     coarse_solution, pay = call(
         base_kernel,
         (block, struct((6, 4, 128), F32)),
-        [smem] + [vmem] * 14,
+        [vmem] * 14,
         [pltpu.VMEM((20, *grid), F32)] * 3
         + [pltpu.VMEM((16, *grid), F32), pltpu.VMEM((320, 128), F32)],
         flops=5_000_000,
         outs=[vmem] * 2,
-    )(pos, source, side, *weights[:-1], last)
+    )(source, side, *weights[:-1], last)
     halo = shared(split_send(pay, "gy", 1))
     mid = jnp.stack([halo[0], pay, halo[1]])
     sides = shared(jnp.stack([split_send(mid, "gx", 1), split_send(mid, "gx", 2)]))
     deep_solution = call(
         functools.partial(deep_kernel, sizes),
         struct((1, 2, 16), F32),
-        [smem, vmem, vmem],
+        [vmem, vmem],
         [pltpu.VMEM((3, 10, 16, 128), F32), pltpu.VMEM((320, 128), F32)],
-    )(pos, mid, sides)
+    )(mid, sides)
     return (fine_solution, coarse_solution, deep_solution)
 
 

time: 67.6 us -> 65.9 us (0.975)
  Pallas kernels: 10.3 us -> 8.72 us
  waiting for transfers between devices: 5.93 us -> 5.18 us
    ppermute x5, waiting for transfers between devices: 5.92 us -> 5.17 us  [split_send(): return lax.ppermute(values, (axis, 'gz'), pairs)]
    pallas_call x3 -> x4, Pallas kernels: 6.98 us -> 6.47 us  [the longest x1 2.79 us: per_device(): call(fine_kernel, (struct((16, 8, 128), F32), struct((128, 128), F32), ow...]
  transfers between devices with their start and end apart: 8 -> 8, of which waited for: 3 -> 2; matrix products, arithmetic and copies ran while one was open for 0% -> 0% of each run, Pallas kernels for 5% -> 5%
where the time goes in v7:
time: 65.9 us; the launch traced here: 65.4 us
  starting transfers between devices  27.7 us (42%)
  blocking collectives  21.4 us (32%)
  Pallas kernels  8.72 us (13%)
  waiting for transfers between devices  5.18 us (8%)
  between operations  1.45 us (2%)
  local copies, waits for them, and re-layouts  0.87 us (1%)
    all_gather x5, blocking collectives, shared(): return lax.all_gather(values, 'gz')  21.4 us
    ppermute x5, starting transfers between devices, split_send(): return lax.ppermute(values, (axis, 'gz'), pairs)  13.1 us
    all_to_all x1, starting transfers between devices, per_device(): lax.all_to_all(send.reshape(16, 8, 128), ('gy', 'gz'), 0, 0)  8.11 us
    ppermute x2, starting transfers between devices, exchanged(): return (lax.ppermute(up, axis, pairs), lax.ppermute(down, axis, back))  6.49 us
    ppermute x5, waiting for transfers between devices, split_send(): return lax.ppermute(values, (axis, 'gz'), pairs)  5.17 us
    pallas_call x1, Pallas kernels, per_device(): call(fine_kernel, (struct((16, 8, 128), F32), struct((128, 128), F32), ow...  2.79 us
    pallas_call x1, Pallas kernels, per_device(): call(base_kernel, (block, struct((6, 4, 128), F32)), [vmem] * 14, [pltpu....  1.72 us
    pallas_call x1, Pallas kernels, per_device(): call(place_kernel, (struct((2, 8, 32, 128), F32), struct((2, 6, 32, 128),...  1.37 us
  transfers between devices with their start and end apart: 8, of which 2 were waited for; matrix products, arithmetic and copies ran while one was open for 0% of the time, Pallas kernels for 5%

profile of v7, /device:TPU:521, one launch (start us, length us, event | category | flops | bytes accessed | tf_op | source)
XLA Modules:
  0.0 65.4 jit_solution(10782293515993777526)
XLA Ops:
  1.3 2.8 %shard_map.85 = (f32[16,8,128]{2,1,0:T(8,128)}, f32[128,128]{1,0:T(8,128)}, f32[2,8,16,128]{3,2,1,0:T(8,128)}, f32[2,8,16,128]{3,2,1,0:T(8,128)}) custom-call(s32[1]{0:T(128)S(6)} %copy.9.count_ref, s32[1,32]{1,0:T(1,128)} %bitcast.27, f32[32,8,64]{2,1,0:T(8,128)} %rhs_hbm.1, bf16[32,8,64]{2,1,0:T(8,128)(2,1)} %coef_hbm.1, f32[8,16,128]{2,1,0:T(8,128)} %grid_hbm.1, ...), custom_call_target="tpu_custom_call" | custom-call | flops 100000 | bytes 100000 | tf_op jit(solution)/shard_map/pallas_call | solution.py:454
  4.1 2.2 %collective-permute-start = (f32[2,8,16,128]{3,2,1,0:T(8,128)}, f32[2,8,16,128]{3,2,1,0:T(8,128)S(1)}, u32[]{:S(2)}, u32[]{:S(2)}) collective-permute-start(f32[2,8,16,128]{3,2,1,0:T(8,128)} %get-tuple-element.27), channel_id=1, source_target_pairs={{0,2},{2,4},{4,6},{6,8},{8,10},{10,12},{12,14},{1,3},{3,5},{5,7},{... | collective-permute-start | bytes 393224 | tf_op jit(solution)/shard_map/ppermute | solution.py:436
  6.3 4.3 %collective-permute-start.1 = (f32[2,8,16,128]{3,2,1,0:T(8,128)}, f32[2,8,16,128]{3,2,1,0:T(8,128)S(1)}, u32[]{:S(2)}, u32[]{:S(2)}) collective-permute-start(f32[2,8,16,128]{3,2,1,0:T(8,128)} %get-tuple-element.27), channel_id=1, source_target_pairs={{2,0},{4,2},{6,4},{8,6},{10,8},{12,10},{14,12},{3,1},{5,3},{7,5},{... | collective-permute-start | bytes 393224 | tf_op jit(solution)/shard_map/ppermute | solution.py:436
  10.6 8.1 %all-to-all-start = ((f32[16,8,128]{2,1,0:T(8,128)}), f32[16,8,128]{2,1,0:T(8,128)S(1)}, u32[]{:S(2)}, u32[]{:S(2)}) async-start(f32[16,8,128]{2,1,0:T(8,128)} %bitcast.24), calls=%async_computation | async-start | bytes 131072 | tf_op jit(solution)/shard_map/all_to_all | solution.py:472
  18.8 0.8 %copy-done.1 = f32[2,8,16,128]{3,2,1,0:T(8,128)S(1)} copy-done((f32[2,8,16,128]{3,2,1,0:T(8,128)S(1)}, f32[2,8,16,128]{3,2,1,0:T(8,128)}, u32[]{:S(2)}) %copy-start.1) | copy-done | bytes 131096
  19.6 2.2 %all-gather = f32[4,8,32,128]{3,2,1,0:T(8,128)S(1)} all-gather(f32[2,8,32,128]{3,2,1,0:T(8,128)S(1)} %pad_maximum_fusion), channel_id=2, replica_groups=mesh['gx'=64,'gy'=8,'gz'=2] {'gz'}, dimensions={0}, use_global_device_ids=true | all-gather | bytes 786432 | tf_op jit(solution)/shard_map/all_gather | solution.py:440
  21.9 4.1 %collective-permute-start.3 = (f32[2,4,32,128]{3,2,1,0:T(8,128)S(1)}, f32[2,4,32,128]{3,2,1,0:T(8,128)S(1)}, u32[]{:S(2)}, u32[]{:S(2)}) collective-permute-start(f32[2,4,32,128]{3,2,1,0:T(8,128)S(1)} %fusion.1), channel_id=1, source_target_pairs={{0,16},{16,32},{17,1},{32,48},{33,17},{48,64},{49,33},{64,80},{65,... | collective-permute-start | bytes 393224 | tf_op jit(solution)/shard_map/ppermute | solution.py:429
  25.9 1.4 %shard_map.87 = (f32[2,8,32,128]{3,2,1,0:T(8,128)S(1)}, f32[2,6,32,128]{3,2,1,0:T(8,128)S(1)}) custom-call(f32[128,128]{1,0:T(8,128)S(1)} %bitcast.22, f32[2,2,8,32,128]{4,3,2,1,0:T(8,128)S(1)} %bitcast.17), custom_call_target="tpu_custom_call" | custom-call | flops 100000 | bytes 100000 | tf_op jit(solution)/shard_map/pallas_call | solution.py:477
  27.3 2.9 %collective-permute-start.2 = (f32[2,6,32,128]{3,2,1,0:T(8,128)S(1)}, f32[2,6,32,128]{3,2,1,0:T(8,128)S(1)}, u32[]{:S(2)}, u32[]{:S(2)}) collective-permute-start(f32[2,6,32,128]{3,2,1,0:T(8,128)S(1)} %get-tuple-element.30), channel_id=1, source_target_pairs={{0,16},{16,32},{17,1},{32,48},{33,17},{48,64},{49,33},{64,80},{65,... | collective-permute-start | bytes 589832 | tf_op jit(solution)/shard_map/ppermute | solution.py:429
  30.2 0.0 collective-permute-done.3
  30.2 3.8 %all-gather.1 = f32[4,4,32,128]{3,2,1,0:T(8,128)S(1)} all-gather(f32[2,4,32,128]{3,2,1,0:T(8,128)S(1)} %collective-permute-done.3), channel_id=3, replica_groups=mesh['gx'=64,'gy'=8,'gz'=2] {'gz'}, dimensions={0}, use_global_device_ids=true | all-gather | bytes 393216 | tf_op jit(solution)/shard_map/all_gather | solution.py:440
  34.0 0.9 %shard_map.88 = (f32[20,32,256]{2,1,0:T(8,128)S(1)}, f32[20,32,256]{2,1,0:T(8,128)S(1)}, f32[20,32,256]{2,1,0:T(8,128)S(1)}, f32[20,32,256]{2,1,0:T(8,128)S(1)},...) custom-call(f32[2,2,8,32,128]{4,3,2,1,0:T(8,128)S(1)} %bitcast.18, ...), custom_call_target="tpu_custom_call" | custom-call | flops 5000000 | bytes 5000000 | tf_op jit(solution)/shard_map/pallas_call | solution.py:487
  34.9 4.9 %all-gather.2 = f32[4,6,32,128]{3,2,1,0:T(8,128)S(1)} all-gather(f32[2,6,32,128]{3,2,1,0:T(8,128)S(1)} %collective-permute-done.2), channel_id=4, replica_groups=mesh['gx'=64,'gy'=8,'gz'=2] {'gz'}, dimensions={0}, use_global_device_ids=true | all-gather | bytes 589824 | tf_op jit(solution)/shard_map/all_gather | solution.py:440
  39.8 1.7 %shard_map.89 = (f32[8,16,128]{2,1,0:T(8,128)}, f32[6,4,128]{2,1,0:T(4,128)S(1)}) custom-call(f32[2,8,32,128]{3,2,1,0:T(8,128)S(1)} %get-tuple-element.29.source_ref, f32[2,2,6,32,128]{4,3,2,1,0:T(8,128)S(1)} %bitcast.19, f32[20,32,256]{2,1,0:T(8,128)S(1)} %get-tuple-element.33.wx_ref, f32[20,32,256]{2,1,0:T(8,128)S(1)} %get-tuple-element.34.wy_ref, ...), custom_call_target="tpu_custom_call" | custom-call | flops 5000000 | bytes 5000000 | tf_op jit(solution)/shard_map/pallas_call | solution.py:497
  41.5 2.2 %collective-permute-start.4 = (f32[6,4,128]{2,1,0:T(4,128)S(1)}, f32[6,4,128]{2,1,0:T(4,128)S(1)}, u32[]{:S(2)}, u32[]{:S(2)}) collective-permute-start(f32[6,4,128]{2,1,0:T(4,128)S(1)} %get-tuple-element.46), channel_id=1, source_target_pairs={{0,2},{2,4},{3,1},{4,6},{5,3},{6,8},{7,5},{8,10},{9,7},{10,12},{11... | collective-permute-start | bytes 36872 | tf_op jit(solution)/shard_map/ppermute | solution.py:429
  43.7 2.2 %collective-permute-done.4 = f32[6,4,128]{2,1,0:T(4,128)S(1)} collective-permute-done((f32[6,4,128]{2,1,0:T(4,128)S(1)}, f32[6,4,128]{2,1,0:T(4,128)S(1)}, u32[]{:S(2)}, u32[]{:S(2)}) %collective-permute-start.4) | collective-permute-done | bytes 12320 | tf_op jit(solution)/shard_map/ppermute | solution.py:429
  46.0 4.2 %all-gather.3 = f32[12,4,128]{2,1,0:T(4,128)S(1)} all-gather(f32[6,4,128]{2,1,0:T(4,128)S(1)} %collective-permute-done.4), channel_id=5, replica_groups=mesh['gx'=64,'gy'=8,'gz'=2] {'gz'}, dimensions={0}, use_global_device_ids=true | all-gather | bytes 36864 | tf_op jit(solution)/shard_map/all_gather | solution.py:440
  50.2 2.1 %collective-permute-start.5 = (f32[3,6,4,128]{3,2,1,0:T(4,128)S(1)}, f32[3,6,4,128]{3,2,1,0:T(4,128)S(1)}, u32[]{:S(2)}, u32[]{:S(2)}) collective-permute-start(f32[3,6,4,128]{3,2,1,0:T(4,128)S(1)} %pad_maximum_fusion.2.mid_ref), channel_id=1, source_target_pairs={{0,16},{16,32},{17,1},{32,48},{33,17},{48,64},{49,33},{64,80},{65,... | collective-permute-start | bytes 110600 | tf_op jit(solution)/shard_map/ppermute | solution.py:429
  52.3 1.9 %collective-permute-start.6 = (f32[3,6,4,128]{3,2,1,0:T(4,128)S(1)}, f32[3,6,4,128]{3,2,1,0:T(4,128)S(1)}, u32[]{:S(2)}, u32[]{:S(2)}) collective-permute-start(f32[3,6,4,128]{3,2,1,0:T(4,128)S(1)} %pad_maximum_fusion.2.mid_ref), channel_id=1, source_target_pairs={{0,32},{16,48},{32,64},{33,1},{48,80},{49,17},{64,96},{65,33},{80,... | collective-permute-start | bytes 110600 | tf_op jit(solution)/shard_map/ppermute | solution.py:429
  54.2 0.7 %shard_map.86 = f32[32,8,64]{2,1,0:T(8,128)} custom-call(s32[1]{0:T(128)S(6)} %copy.9.count_ref, f32[16,8,128]{2,1,0:T(8,128)S(1)} %copy-done), custom_call_target="tpu_custom_call" | custom-call | flops 100000 | bytes 100000 | tf_op jit(solution)/shard_map/pallas_call | solution.py:469
  55.0 0.0 collective-permute-done.5
  55.0 2.9 %collective-permute-done.6 = f32[3,6,4,128]{3,2,1,0:T(4,128)S(1)} collective-permute-done((f32[3,6,4,128]{3,2,1,0:T(4,128)S(1)}, f32[3,6,4,128]{3,2,1,0:T(4,128)S(1)}, u32[]{:S(2)}, u32[]{:S(2)}) %collective-permute-start.6) | collective-permute-done | bytes 36896 | tf_op jit(solution)/shard_map/ppermute | solution.py:429
  57.9 6.3 %all-gather.4 = f32[4,3,6,4,128]{4,3,2,1,0:T(4,128)S(1)} all-gather(f32[2,3,6,4,128]{4,3,2,1,0:T(4,128)S(1)} %pad_maximum_fusion.1), channel_id=6, replica_groups=mesh['gx'=64,'gy'=8,'gz'=2] {'gz'}, dimensions={0}, use_global_device_ids=true | all-gather | bytes 221184 | tf_op jit(solution)/shard_map/all_gather | solution.py:440
  64.2 1.2 %shard_map.90 = f32[1,2,16]{2,1,0:T(2,128)} custom-call(f32[3,6,4,128]{3,2,1,0:T(4,128)S(1)} %pad_maximum_fusion.2.mid_ref, f32[2,2,3,6,4,128]{5,4,3,2,1,0:T(4,128)S(1)} %bitcast.21), custom_call_target="tpu_custom_call" | custom-call | flops 100000 | bytes 100000 | tf_op jit(solution)/shard_map/pallas_call | solution.py:509
  (15 shorter events, 0.1 us)
Async XLA Ops:
  4.1 14.6 %collective-permute-start = (f32[2,8,16,128]{3,2,1,0:T(8,128)}, f32[2,8,16,128]{3,2,1,0:T(8,128)S(1)}, u32[]{:S(2)}, u32[]{:S(2)}) collective-permute-start(f32[2,8,16,128]{3,2,1,0:T(8,128)} %get-tuple-element.27), channel_id=1, source_target_pairs={{0,2},{2,4},{4,6},{6,8},{8,10},{10,12},{12,14},{1,3},{3,5},{5,7},{... | collective-permute-start | bytes 393224 | tf_op jit(solution)/shard_map/ppermute | solution.py:436
  6.3 12.4 %collective-permute-start.1 = (f32[2,8,16,128]{3,2,1,0:T(8,128)}, f32[2,8,16,128]{3,2,1,0:T(8,128)S(1)}, u32[]{:S(2)}, u32[]{:S(2)}) collective-permute-start(f32[2,8,16,128]{3,2,1,0:T(8,128)} %get-tuple-element.27), channel_id=1, source_target_pairs={{2,0},{4,2},{6,4},{8,6},{10,8},{12,10},{14,12},{3,1},{5,3},{7,5},{... | collective-permute-start | bytes 393224 | tf_op jit(solution)/shard_map/ppermute | solution.py:436
  10.6 15.4 %all-to-all-start = ((f32[16,8,128]{2,1,0:T(8,128)}), f32[16,8,128]{2,1,0:T(8,128)S(1)}, u32[]{:S(2)}, u32[]{:S(2)}) async-start(f32[16,8,128]{2,1,0:T(8,128)} %bitcast.24), calls=%async_computation | async-start | bytes 131072 | tf_op jit(solution)/shard_map/all_to_all | solution.py:472
  18.7 0.9 %copy-start.1 = (f32[2,8,16,128]{3,2,1,0:T(8,128)S(1)}, f32[2,8,16,128]{3,2,1,0:T(8,128)}, u32[]{:S(2)}) copy-start(f32[2,8,16,128]{3,2,1,0:T(8,128)} %get-tuple-element.28) | copy-start | bytes 393220
  21.9 8.3 %collective-permute-start.3 = (f32[2,4,32,128]{3,2,1,0:T(8,128)S(1)}, f32[2,4,32,128]{3,2,1,0:T(8,128)S(1)}, u32[]{:S(2)}, u32[]{:S(2)}) collective-permute-start(f32[2,4,32,128]{3,2,1,0:T(8,128)S(1)} %fusion.1), channel_id=1, source_target_pairs={{0,16},{16,32},{17,1},{32,48},{33,17},{48,64},{49,33},{64,80},{65,... | collective-permute-start | bytes 393224 | tf_op jit(solution)/shard_map/ppermute | solution.py:429
  27.3 7.6 %collective-permute-start.2 = (f32[2,6,32,128]{3,2,1,0:T(8,128)S(1)}, f32[2,6,32,128]{3,2,1,0:T(8,128)S(1)}, u32[]{:S(2)}, u32[]{:S(2)}) collective-permute-start(f32[2,6,32,128]{3,2,1,0:T(8,128)S(1)} %get-tuple-element.30), channel_id=1, source_target_pairs={{0,16},{16,32},{17,1},{32,48},{33,17},{48,64},{49,33},{64,80},{65,... | collective-permute-start | bytes 589832 | tf_op jit(solution)/shard_map/ppermute | solution.py:429
  41.5 4.4 %collective-permute-start.4 = (f32[6,4,128]{2,1,0:T(4,128)S(1)}, f32[6,4,128]{2,1,0:T(4,128)S(1)}, u32[]{:S(2)}, u32[]{:S(2)}) collective-permute-start(f32[6,4,128]{2,1,0:T(4,128)S(1)} %get-tuple-element.46), channel_id=1, source_target_pairs={{0,2},{2,4},{3,1},{4,6},{5,3},{6,8},{7,5},{8,10},{9,7},{10,12},{11... | collective-permute-start | bytes 36872 | tf_op jit(solution)/shard_map/ppermute | solution.py:429
  50.2 4.1 %copy-start = (f32[16,8,128]{2,1,0:T(8,128)S(1)}, f32[16,8,128]{2,1,0:T(8,128)}, u32[]{:S(2)}) copy-start(f32[16,8,128]{2,1,0:T(8,128)} %get-tuple-element.25.second_ref) | copy-start | bytes 196612
  50.2 4.8 %collective-permute-start.5 = (f32[3,6,4,128]{3,2,1,0:T(4,128)S(1)}, f32[3,6,4,128]{3,2,1,0:T(4,128)S(1)}, u32[]{:S(2)}, u32[]{:S(2)}) collective-permute-start(f32[3,6,4,128]{3,2,1,0:T(4,128)S(1)} %pad_maximum_fusion.2.mid_ref), channel_id=1, source_target_pairs={{0,16},{16,32},{17,1},{32,48},{33,17},{48,64},{49,33},{64,80},{65,... | collective-permute-start | bytes 110600 | tf_op jit(solution)/shard_map/ppermute | solution.py:429
  52.3 5.6 %collective-permute-start.6 = (f32[3,6,4,128]{3,2,1,0:T(4,128)S(1)}, f32[3,6,4,128]{3,2,1,0:T(4,128)S(1)}, u32[]{:S(2)}, u32[]{:S(2)}) collective-permute-start(f32[3,6,4,128]{3,2,1,0:T(4,128)S(1)} %pad_maximum_fusion.2.mid_ref), channel_id=1, source_target_pairs={{0,32},{16,48},{32,64},{33,1},{48,80},{49,17},{64,96},{65,33},{80,... | collective-permute-start | bytes 110600 | tf_op jit(solution)/shard_map/ppermute | solution.py:429

commit v8 on v7

--- a/solution.py
+++ b/solution.py
@@ -60,7 +60,7 @@
 
 
 def fine_kernel(
-    count_ref, target_hbm, rhs_hbm, coef_hbm, grid_hbm, cond_hbm, second_ref, send_ref, away_ref, own_ref,
+    count_ref, target_hbm, rhs_hbm, coef_hbm, grid_hbm, cond_hbm, second_ref, send_ref, own_ref,
     target_ref, rhs_ref, coef_ref, grid_ref, cond_ref, sems
 ):
     live = count_ref[0]
@@ -150,9 +150,8 @@
     send_ref[...] = jnp.where(col < 64, packed[0], packed[1]) + small(lift, tags)
     loads[3].wait()
     loads[4].wait()
-    for ref in (away_ref, own_ref):
-        ref[0] = grid_ref[...]
-        ref[1] = cond_ref[...].astype(F32) * 0.5
+    own_ref[0] = grid_ref[...]
+    own_ref[1] = cond_ref[...].astype(F32) * 0.5
 
 
 def store_kernel(count_ref, second_ref, solved_ref):
@@ -429,13 +428,6 @@
     return lax.ppermute(values, (axis, "gz"), pairs)
 
 
-def exchanged(up, down, axis):
-    count = lax.axis_size(axis)
-    pairs = [(place, place + 1) for place in range(count - 1)]
-    back = [(target, source) for source, target in pairs]
-    return lax.ppermute(up, axis, pairs), lax.ppermute(down, axis, back)
-
-
 def shared(values):
     return lax.all_gather(values, "gz")
 
@@ -451,9 +443,9 @@
     struct = jax.ShapeDtypeStruct
     hbm = pl.BlockSpec(memory_space=pltpu.HBM)
     own_block = struct((2, *coarse_rhs.shape), F32)
-    second, send, away, own = call(
+    second, send, own = call(
         fine_kernel,
-        (struct((16, 8, 128), F32), struct((128, 128), F32), own_block, own_block),
+        (struct((16, 8, 128), F32), struct((128, 128), F32), own_block),
         [smem, hbm, hbm, hbm, hbm, hbm],
         [
             pltpu.VMEM((1, 32), jnp.int32),
@@ -463,15 +455,16 @@
             pltpu.VMEM(coarse_coef.shape, coarse_coef.dtype),
             pltpu.SemaphoreType.DMA((5,)),
         ],
-        outs=[vmem] * 4,
+        outs=[vmem] * 3,
         vmem=MOST_VMEM,
     )(patch_count, patch_target.reshape(1, 32), fine_rhs, fine_coef, coarse_rhs, coarse_coef)
     fine_solution = call(store_kernel, struct(fine_rhs.shape, F32), [smem, vmem])(
         patch_count, second
     )
     got = lax.all_to_all(send.reshape(16, 8, 128), ("gy", "gz"), 0, 0).reshape(128, 128)
-    below, above = exchanged(away, away, "gy")
-    chip = shared(jnp.concatenate([below[:, :, 8:], own, above[:, :, :8]], axis=2))
+    chip = shared(own)
+    halo = shared(split_send(jnp.where(core == 0, chip[:, :, :, 8:], chip[:, :, :, :8]), "gy", 1))
+    chip = jnp.concatenate([halo[0], chip, halo[1]], axis=3)
     edge = jnp.where(core == 0, chip[:, 1, 1:], chip[:, 1, :7])
     edge = split_send(edge[:, :4] * (1024.0 * PACK) + edge[:, 3:] * 1024.0, "gx", 1)
     source, pay = call(

time: 65.9 us -> 62.5 us (0.948)
  starting transfers between devices: 27.7 us -> 22.9 us
  blocking collectives: 21.4 us -> 23.7 us
  local copies, waits for them, and re-layouts: 0.87 us -> 0.02 us
    ppermute x2 -> x0, starting transfers between devices: 6.49 us -> none  [exchanged(): return (lax.ppermute(up, axis, pairs), lax.ppermute(down, axis, back))]
    all_gather x5 -> x6, blocking collectives: 21.4 us -> 23.7 us  [shared(): return lax.all_gather(values, 'gz')]
    ppermute x5 -> x6, starting transfers between devices: 13.1 us -> 15.3 us  [split_send(): return lax.ppermute(values, (axis, 'gz'), pairs)]
    unnamed x4 -> x2, local copies, waits for them, and re-layouts: 0.85 us -> 0.01 us
    ppermute x5 -> x6, waiting for transfers between devices: 5.17 us -> 5.17 us  [split_send(): return lax.ppermute(values, (axis, 'gz'), pairs)]
  transfers between devices with their start and end apart: 8 -> 7, of which waited for: 2 -> 2; matrix products, arithmetic and copies ran while one was open for 0% -> 0% of each run, Pallas kernels for 5% -> 5%
where the time goes in v8:
time: 62.5 us; the launch traced here: 62.1 us
  blocking collectives  23.7 us (38%)
  starting transfers between devices  22.9 us (37%)
  Pallas kernels  8.71 us (14%)
  waiting for transfers between devices  5.17 us (8%)
  between operations  1.43 us (2%)
    all_gather x6, blocking collectives, shared(): return lax.all_gather(values, 'gz')  23.7 us
    ppermute x6, starting transfers between devices, split_send(): return lax.ppermute(values, (axis, 'gz'), pairs)  15.3 us
    all_to_all x1, starting transfers between devices, per_device(): lax.all_to_all(send.reshape(16, 8, 128), ('gy', 'gz'), 0, 0)  7.58 us
    ppermute x6, waiting for transfers between devices, split_send(): return lax.ppermute(values, (axis, 'gz'), pairs)  5.17 us
    pallas_call x1, Pallas kernels, per_device(): call(fine_kernel, (struct((16, 8, 128), F32), struct((128, 128), F32), ow...  2.74 us
    pallas_call x1, Pallas kernels, per_device(): call(base_kernel, (block, struct((6, 4, 128), F32)), [vmem] * 14, [pltpu....  1.75 us
    pallas_call x1, Pallas kernels, per_device(): call(place_kernel, (struct((2, 8, 32, 128), F32), struct((2, 6, 32, 128),...  1.37 us
  transfers between devices with their start and end apart: 7, of which 2 were waited for; matrix products, arithmetic and copies ran while one was open for 0% of the time, Pallas kernels for 5%

profile of v8, /device:TPU:521, one launch (start us, length us, event | category | flops | bytes accessed | tf_op | source)
XLA Modules:
  0.0 62.1 jit_solution(4147414851495317984)
XLA Ops:
  1.3 2.7 %shard_map.85 = (f32[16,8,128]{2,1,0:T(8,128)}, f32[128,128]{1,0:T(8,128)}, f32[2,8,16,128]{3,2,1,0:T(8,128)}) custom-call(s32[1]{0:T(128)S(6)} %copy.9.count_ref, s32[1,32]{1,0:T(1,128)} %bitcast.25, f32[32,8,64]{2,1,0:T(8,128)} %rhs_hbm.1, bf16[32,8,64]{2,1,0:T(8,128)(2,1)} %coef_hbm.1, f32[8,16,128]{2,1,0:T(8,128)} %grid_hbm.1, bf16[8,16,128]{2,1,0:T(8,128)(2,1)} %cond_hbm.1), custom_call_target="tpu_custom_call" | custom-call | flops 100000 | bytes 100000 | tf_op jit(solution)/shard_map/pallas_call | solution.py:446
  4.0 2.5 %all-gather = f32[4,8,16,128]{3,2,1,0:T(8,128)S(1)} all-gather(f32[2,8,16,128]{3,2,1,0:T(8,128)} %get-tuple-element.26), channel_id=2, replica_groups=mesh['gx'=64,'gy'=8,'gz'=2] {'gz'}, dimensions={0}, use_global_device_ids=true | all-gather | bytes 393216 | tf_op jit(solution)/shard_map/all_gather | solution.py:432
  6.6 2.2 %collective-permute-start = (f32[2,2,8,8,128]{4,3,2,1,0:T(8,128)S(1)}, f32[2,2,8,8,128]{4,3,2,1,0:T(8,128)S(1)}, u32[]{:S(2)}, u32[]{:S(2)}) collective-permute-start(f32[2,2,8,8,128]{4,3,2,1,0:T(8,128)S(1)} %slice_select_fusion.1), channel_id=1, source_target_pairs={{0,2},{2,4},{3,1},{4,6},{5,3},{6,8},{7,5},{8,10},{9,7},{10,12},{11... | collective-permute-start | bytes 393224 | tf_op jit(solution)/shard_map/ppermute | solution.py:428
  8.7 7.6 %all-to-all-start = ((f32[16,8,128]{2,1,0:T(8,128)}), f32[16,8,128]{2,1,0:T(8,128)S(1)}, u32[]{:S(2)}, u32[]{:S(2)}) async-start(f32[16,8,128]{2,1,0:T(8,128)} %bitcast.1), calls=%async_computation | async-start | bytes 131072 | tf_op jit(solution)/shard_map/all_to_all | solution.py:464
  16.3 0.0 collective-permute-done
  16.3 2.0 %all-gather.1 = f32[4,2,8,8,128]{4,3,2,1,0:T(8,128)S(1)} all-gather(f32[2,2,8,8,128]{4,3,2,1,0:T(8,128)S(1)} %collective-permute-done), channel_id=3, replica_groups=mesh['gx'=64,'gy'=8,'gz'=2] {'gz'}, dimensions={0}, use_global_device_ids=true | all-gather | bytes 393216 | tf_op jit(solution)/shard_map/all_gather | solution.py:432
  18.5 4.1 %collective-permute-start.2 = (f32[2,4,32,128]{3,2,1,0:T(8,128)S(1)}, f32[2,4,32,128]{3,2,1,0:T(8,128)S(1)}, u32[]{:S(2)}, u32[]{:S(2)}) collective-permute-start(f32[2,4,32,128]{3,2,1,0:T(8,128)S(1)} %fusion.1), channel_id=1, source_target_pairs={{0,16},{16,32},{17,1},{32,48},{33,17},{48,64},{49,33},{64,80},{65,... | collective-permute-start | bytes 393224 | tf_op jit(solution)/shard_map/ppermute | solution.py:428
  22.5 1.4 %shard_map.87 = (f32[2,8,32,128]{3,2,1,0:T(8,128)S(1)}, f32[2,6,32,128]{3,2,1,0:T(8,128)S(1)}) custom-call(f32[128,128]{1,0:T(8,128)S(1)} %bitcast.19, f32[2,2,8,32,128]{4,3,2,1,0:T(8,128)S(1)} %pad_maximum_fusion.chip_ref), custom_call_target="tpu_custom_call" | custom-call | flops 100000 | bytes 100000 | tf_op jit(solution)/shard_map/pallas_call | solution.py:470
  23.9 2.9 %collective-permute-start.1 = (f32[2,6,32,128]{3,2,1,0:T(8,128)S(1)}, f32[2,6,32,128]{3,2,1,0:T(8,128)S(1)}, u32[]{:S(2)}, u32[]{:S(2)}) collective-permute-start(f32[2,6,32,128]{3,2,1,0:T(8,128)S(1)} %get-tuple-element.28), channel_id=1, source_target_pairs={{0,16},{16,32},{17,1},{32,48},{33,17},{48,64},{49,33},{64,80},{65,... | collective-permute-start | bytes 589832 | tf_op jit(solution)/shard_map/ppermute | solution.py:428
  26.8 0.0 collective-permute-done.2
  26.8 3.8 %all-gather.2 = f32[4,4,32,128]{3,2,1,0:T(8,128)S(1)} all-gather(f32[2,4,32,128]{3,2,1,0:T(8,128)S(1)} %collective-permute-done.2), channel_id=4, replica_groups=mesh['gx'=64,'gy'=8,'gz'=2] {'gz'}, dimensions={0}, use_global_device_ids=true | all-gather | bytes 393216 | tf_op jit(solution)/shard_map/all_gather | solution.py:432
  30.6 0.9 %shard_map.88 = (f32[20,32,256]{2,1,0:T(8,128)S(1)}, f32[20,32,256]{2,1,0:T(8,128)S(1)}, f32[20,32,256]{2,1,0:T(8,128)S(1)}, f32[20,32,256]{2,1,0:T(8,128)S(1)},...) custom-call(f32[2,2,8,32,128]{4,3,2,1,0:T(8,128)S(1)} %pad_maximum_f, ...), custom_call_target="tpu_custom_call" | custom-call | flops 5000000 | bytes 5000000 | tf_op jit(solution)/shard_map/pallas_call | solution.py:480
  31.5 4.9 %all-gather.3 = f32[4,6,32,128]{3,2,1,0:T(8,128)S(1)} all-gather(f32[2,6,32,128]{3,2,1,0:T(8,128)S(1)} %collective-permute-done.1), channel_id=5, replica_groups=mesh['gx'=64,'gy'=8,'gz'=2] {'gz'}, dimensions={0}, use_global_device_ids=true | all-gather | bytes 589824 | tf_op jit(solution)/shard_map/all_gather | solution.py:432
  36.4 1.8 %shard_map.89 = (f32[8,16,128]{2,1,0:T(8,128)}, f32[6,4,128]{2,1,0:T(4,128)S(1)}) custom-call(f32[2,8,32,128]{3,2,1,0:T(8,128)S(1)} %get-tuple-element.27.source_ref, f32[2,2,6,32,128]{4,3,2,1,0:T(8,128)S(1)} %bitcast.16, f32[20,32,256]{2,1,0:T(8,128)S(1)} %get-tuple-element.31.wx_ref, f32[20,32,256]{2,1,0:T(8,128)S(1)} %get-tuple-element.32.wy_ref, ...), custom_call_target="tpu_custom_call" | custom-call | flops 5000000 | bytes 5000000 | tf_op jit(solution)/shard_map/pallas_call | solution.py:490
  38.2 2.2 %collective-permute-start.3 = (f32[6,4,128]{2,1,0:T(4,128)S(1)}, f32[6,4,128]{2,1,0:T(4,128)S(1)}, u32[]{:S(2)}, u32[]{:S(2)}) collective-permute-start(f32[6,4,128]{2,1,0:T(4,128)S(1)} %get-tuple-element.44), channel_id=1, source_target_pairs={{0,2},{2,4},{3,1},{4,6},{5,3},{6,8},{7,5},{8,10},{9,7},{10,12},{11... | collective-permute-start | bytes 36872 | tf_op jit(solution)/shard_map/ppermute | solution.py:428
  40.3 2.2 %collective-permute-done.3 = f32[6,4,128]{2,1,0:T(4,128)S(1)} collective-permute-done((f32[6,4,128]{2,1,0:T(4,128)S(1)}, f32[6,4,128]{2,1,0:T(4,128)S(1)}, u32[]{:S(2)}, u32[]{:S(2)}) %collective-permute-start.3) | collective-permute-done | bytes 12320 | tf_op jit(solution)/shard_map/ppermute | solution.py:428
  42.6 4.2 %all-gather.4 = f32[12,4,128]{2,1,0:T(4,128)S(1)} all-gather(f32[6,4,128]{2,1,0:T(4,128)S(1)} %collective-permute-done.3), channel_id=6, replica_groups=mesh['gx'=64,'gy'=8,'gz'=2] {'gz'}, dimensions={0}, use_global_device_ids=true | all-gather | bytes 36864 | tf_op jit(solution)/shard_map/all_gather | solution.py:432
  46.8 2.1 %collective-permute-start.4 = (f32[3,6,4,128]{3,2,1,0:T(4,128)S(1)}, f32[3,6,4,128]{3,2,1,0:T(4,128)S(1)}, u32[]{:S(2)}, u32[]{:S(2)}) collective-permute-start(f32[3,6,4,128]{3,2,1,0:T(4,128)S(1)} %pad_maximum_fusion.2.mid_ref), channel_id=1, source_target_pairs={{0,16},{16,32},{17,1},{32,48},{33,17},{48,64},{49,33},{64,80},{65,... | collective-permute-start | bytes 110600 | tf_op jit(solution)/shard_map/ppermute | solution.py:428
  48.9 1.9 %collective-permute-start.5 = (f32[3,6,4,128]{3,2,1,0:T(4,128)S(1)}, f32[3,6,4,128]{3,2,1,0:T(4,128)S(1)}, u32[]{:S(2)}, u32[]{:S(2)}) collective-permute-start(f32[3,6,4,128]{3,2,1,0:T(4,128)S(1)} %pad_maximum_fusion.2.mid_ref), channel_id=1, source_target_pairs={{0,32},{16,48},{32,64},{33,1},{48,80},{49,17},{64,96},{65,33},{80,... | collective-permute-start | bytes 110600 | tf_op jit(solution)/shard_map/ppermute | solution.py:428
  50.9 0.7 %shard_map.86 = f32[32,8,64]{2,1,0:T(8,128)} custom-call(s32[1]{0:T(128)S(6)} %copy.9.count_ref, f32[16,8,128]{2,1,0:T(8,128)S(1)} %copy-done), custom_call_target="tpu_custom_call" | custom-call | flops 100000 | bytes 100000 | tf_op jit(solution)/shard_map/pallas_call | solution.py:461
  51.6 0.1 collective-permute-done.4
  51.6 2.9 %collective-permute-done.5 = f32[3,6,4,128]{3,2,1,0:T(4,128)S(1)} collective-permute-done((f32[3,6,4,128]{3,2,1,0:T(4,128)S(1)}, f32[3,6,4,128]{3,2,1,0:T(4,128)S(1)}, u32[]{:S(2)}, u32[]{:S(2)}) %collective-permute-start.5) | collective-permute-done | bytes 36896 | tf_op jit(solution)/shard_map/ppermute | solution.py:428
  54.5 6.3 %all-gather.5 = f32[4,3,6,4,128]{4,3,2,1,0:T(4,128)S(1)} all-gather(f32[2,3,6,4,128]{4,3,2,1,0:T(4,128)S(1)} %pad_maximum_fusion.1), channel_id=7, replica_groups=mesh['gx'=64,'gy'=8,'gz'=2] {'gz'}, dimensions={0}, use_global_device_ids=true | all-gather | bytes 221184 | tf_op jit(solution)/shard_map/all_gather | solution.py:432
  60.9 1.2 %shard_map.90 = f32[1,2,16]{2,1,0:T(2,128)} custom-call(f32[3,6,4,128]{3,2,1,0:T(4,128)S(1)} %pad_maximum_fusion.2.mid_ref, f32[2,2,3,6,4,128]{5,4,3,2,1,0:T(4,128)S(1)} %bitcast.18), custom_call_target="tpu_custom_call" | custom-call | flops 100000 | bytes 100000 | tf_op jit(solution)/shard_map/pallas_call | solution.py:502
  (12 shorter events, 0.2 us)
Async XLA Ops:
  6.6 9.8 %collective-permute-start = (f32[2,2,8,8,128]{4,3,2,1,0:T(8,128)S(1)}, f32[2,2,8,8,128]{4,3,2,1,0:T(8,128)S(1)}, u32[]{:S(2)}, u32[]{:S(2)}) collective-permute-start(f32[2,2,8,8,128]{4,3,2,1,0:T(8,128)S(1)} %slice_select_fusion.1), channel_id=1, source_target_pairs={{0,2},{2,4},{3,1},{4,6},{5,3},{6,8},{7,5},{8,10},{9,7},{10,12},{11... | collective-permute-start | bytes 393224 | tf_op jit(solution)/shard_map/ppermute | solution.py:428
  8.7 13.8 %all-to-all-start = ((f32[16,8,128]{2,1,0:T(8,128)}), f32[16,8,128]{2,1,0:T(8,128)S(1)}, u32[]{:S(2)}, u32[]{:S(2)}) async-start(f32[16,8,128]{2,1,0:T(8,128)} %bitcast.1), calls=%async_computation | async-start | bytes 131072 | tf_op jit(solution)/shard_map/all_to_all | solution.py:464
  18.5 8.3 %collective-permute-start.2 = (f32[2,4,32,128]{3,2,1,0:T(8,128)S(1)}, f32[2,4,32,128]{3,2,1,0:T(8,128)S(1)}, u32[]{:S(2)}, u32[]{:S(2)}) collective-permute-start(f32[2,4,32,128]{3,2,1,0:T(8,128)S(1)} %fusion.1), channel_id=1, source_target_pairs={{0,16},{16,32},{17,1},{32,48},{33,17},{48,64},{49,33},{64,80},{65,... | collective-permute-start | bytes 393224 | tf_op jit(solution)/shard_map/ppermute | solution.py:428
  23.9 7.6 %collective-permute-start.1 = (f32[2,6,32,128]{3,2,1,0:T(8,128)S(1)}, f32[2,6,32,128]{3,2,1,0:T(8,128)S(1)}, u32[]{:S(2)}, u32[]{:S(2)}) collective-permute-start(f32[2,6,32,128]{3,2,1,0:T(8,128)S(1)} %get-tuple-element.28), channel_id=1, source_target_pairs={{0,16},{16,32},{17,1},{32,48},{33,17},{48,64},{49,33},{64,80},{65,... | collective-permute-start | bytes 589832 | tf_op jit(solution)/shard_map/ppermute | solution.py:428
  38.2 4.4 %collective-permute-start.3 = (f32[6,4,128]{2,1,0:T(4,128)S(1)}, f32[6,4,128]{2,1,0:T(4,128)S(1)}, u32[]{:S(2)}, u32[]{:S(2)}) collective-permute-start(f32[6,4,128]{2,1,0:T(4,128)S(1)} %get-tuple-element.44), channel_id=1, source_target_pairs={{0,2},{2,4},{3,1},{4,6},{5,3},{6,8},{7,5},{8,10},{9,7},{10,12},{11... | collective-permute-start | bytes 36872 | tf_op jit(solution)/shard_map/ppermute | solution.py:428
  46.8 4.1 %copy-start = (f32[16,8,128]{2,1,0:T(8,128)S(1)}, f32[16,8,128]{2,1,0:T(8,128)}, u32[]{:S(2)}) copy-start(f32[16,8,128]{2,1,0:T(8,128)} %get-tuple-element.24.second_ref) | copy-start | bytes 196612
  46.8 4.8 %collective-permute-start.4 = (f32[3,6,4,128]{3,2,1,0:T(4,128)S(1)}, f32[3,6,4,128]{3,2,1,0:T(4,128)S(1)}, u32[]{:S(2)}, u32[]{:S(2)}) collective-permute-start(f32[3,6,4,128]{3,2,1,0:T(4,128)S(1)} %pad_maximum_fusion.2.mid_ref), channel_id=1, source_target_pairs={{0,16},{16,32},{17,1},{32,48},{33,17},{48,64},{49,33},{64,80},{65,... | collective-permute-start | bytes 110600 | tf_op jit(solution)/shard_map/ppermute | solution.py:428
  48.9 5.6 %collective-permute-start.5 = (f32[3,6,4,128]{3,2,1,0:T(4,128)S(1)}, f32[3,6,4,128]{3,2,1,0:T(4,128)S(1)}, u32[]{:S(2)}, u32[]{:S(2)}) collective-permute-start(f32[3,6,4,128]{3,2,1,0:T(4,128)S(1)} %pad_maximum_fusion.2.mid_ref), channel_id=1, source_target_pairs={{0,32},{16,48},{32,64},{33,1},{48,80},{49,17},{64,96},{65,33},{80,... | collective-permute-start | bytes 110600 | tf_op jit(solution)/shard_map/ppermute | solution.py:428

commit v9 on v8

--- a/solution.py
+++ b/solution.py
@@ -319,7 +319,7 @@
     source_ref, side_ref,
     wx_ref, wy_ref, wz_ref, diag_ref, scale_ref,
     mid_wx_ref, mid_wy_ref, mid_wz_ref, mid_diag_ref, mid_scale_ref, low_scale_ref, low_h_ref,
-    out_ref, pay_ref, s_ref, first_ref, second_ref, res_ref, rows_ref,
+    out_hbm, pay_ref, s_ref, first_ref, second_ref, res_ref, rows_ref, out_ref, sem,
 ):
     for number in range(2):
         lanes = slice(128 * number, 128 * number + 128)
@@ -346,15 +346,17 @@
 
     lax.fori_loop(1, 19, correct, 0, unroll=True)
 
+    own = second_ref[6:14, 8:24, :]
+    out_ref[...] = jnp.where(lax.axis_index("gz") == 0, own[:, :, :128], own[:, :, 128:])
+    store = pltpu.make_async_copy(out_ref, out_hbm, sem)
+    store.start()
+
     def leave(layer, _):
         u, total = sides(second_ref, layer)
         res_ref[layer - 2] = s_ref[layer] - diag_ref[layer] * u + total
         return 0
 
     lax.fori_loop(2, 18, leave, 0, unroll=True)
-    own = second_ref[6:14, 8:24, :]
-    out_ref[...] = jnp.where(lax.axis_index("gz") == 0, own[:, :, :128], own[:, :, 128:])
-
     source = coarser(res_ref[...], pair_matrix(256), 0.5, rows_ref)
     scale, wx, wy, wz = mid_scale_ref[...], mid_wx_ref[...], mid_wy_ref[...], mid_wz_ref[...]
     first = source * scale
@@ -366,6 +368,7 @@
     pay_ref[0:2] = source[:, 2:6]
     pay_ref[2:4] = (source * low_scale_ref[...])[:, 2:6]
     pay_ref[4:6] = low_h_ref[:, 2:6]
+    store.wait()
 
 
 def deep_kernel(sizes, mid_ref, side_ref, out_ref, win_ref, rows_ref):
@@ -492,9 +495,10 @@
         (block, struct((6, 4, 128), F32)),
         [vmem] * 14,
         [pltpu.VMEM((20, *grid), F32)] * 3
-        + [pltpu.VMEM((16, *grid), F32), pltpu.VMEM((320, 128), F32)],
+        + [pltpu.VMEM((16, *grid), F32), pltpu.VMEM((320, 128), F32)]
+        + [pltpu.VMEM((8, 16, 128), F32), pltpu.SemaphoreType.DMA],
         flops=5_000_000,
-        outs=[vmem] * 2,
+        outs=[hbm, vmem],
     )(source, side, *weights[:-1], last)
     halo = shared(split_send(pay, "gy", 1))
     mid = jnp.stack([halo[0], pay, halo[1]])

time: 62.5 us -> 62.5 us (level)
  no operation moved by 1% of the time
where the time goes in v9:
time: 62.5 us; the launch traced here: 62.1 us
  blocking collectives  23.7 us (38%)
  starting transfers between devices  22.9 us (37%)
  Pallas kernels  8.7 us (14%)
  waiting for transfers between devices  5.17 us (8%)
  between operations  1.43 us (2%)
    all_gather x6, blocking collectives, shared(): return lax.all_gather(values, 'gz')  23.7 us
    ppermute x6, starting transfers between devices, split_send(): return lax.ppermute(values, (axis, 'gz'), pairs)  15.3 us
    all_to_all x1, starting transfers between devices, per_device(): lax.all_to_all(send.reshape(16, 8, 128), ('gy', 'gz'), 0, 0)  7.58 us
    ppermute x6, waiting for transfers between devices, split_send(): return lax.ppermute(values, (axis, 'gz'), pairs)  5.17 us
    pallas_call x1, Pallas kernels, per_device(): call(fine_kernel, (struct((16, 8, 128), F32), struct((128, 128), F32), ow...  2.74 us
    pallas_call x1, Pallas kernels, per_device(): call(base_kernel, (block, struct((6, 4, 128), F32)), [vmem] * 14, [pltpu....  1.75 us
    pallas_call x1, Pallas kernels, per_device(): call(place_kernel, (struct((2, 8, 32, 128), F32), struct((2, 6, 32, 128),...  1.37 us
  transfers between devices with their start and end apart: 7, of which 2 were waited for; matrix products, arithmetic and copies ran while one was open for 0% of the time, Pallas kernels for 5%

profile of v9, /device:TPU:521, one launch (start us, length us, event | category | flops | bytes accessed | tf_op | source)
XLA Modules:
  0.0 62.1 jit_solution(14445610501167829498)
XLA Ops:
  1.3 2.7 %shard_map.85 = (f32[16,8,128]{2,1,0:T(8,128)}, f32[128,128]{1,0:T(8,128)}, f32[2,8,16,128]{3,2,1,0:T(8,128)}) custom-call(s32[1]{0:T(128)S(6)} %copy.9.count_ref, s32[1,32]{1,0:T(1,128)} %bitcast.25, f32[32,8,64]{2,1,0:T(8,128)} %rhs_hbm.1, bf16[32,8,64]{2,1,0:T(8,128)(2,1)} %coef_hbm.1, f32[8,16,128]{2,1,0:T(8,128)} %grid_hbm.1, bf16[8,16,128]{2,1,0:T(8,128)(2,1)} %cond_hbm.1), custom_call_target="tpu_custom_call" | custom-call | flops 100000 | bytes 100000 | tf_op jit(solution)/shard_map/pallas_call | solution.py:449
  4.0 2.5 %all-gather = f32[4,8,16,128]{3,2,1,0:T(8,128)S(1)} all-gather(f32[2,8,16,128]{3,2,1,0:T(8,128)} %get-tuple-element.26), channel_id=2, replica_groups=mesh['gx'=64,'gy'=8,'gz'=2] {'gz'}, dimensions={0}, use_global_device_ids=true | all-gather | bytes 393216 | tf_op jit(solution)/shard_map/all_gather | solution.py:435
  6.6 2.2 %collective-permute-start = (f32[2,2,8,8,128]{4,3,2,1,0:T(8,128)S(1)}, f32[2,2,8,8,128]{4,3,2,1,0:T(8,128)S(1)}, u32[]{:S(2)}, u32[]{:S(2)}) collective-permute-start(f32[2,2,8,8,128]{4,3,2,1,0:T(8,128)S(1)} %slice_select_fusion.1), channel_id=1, source_target_pairs={{0,2},{2,4},{3,1},{4,6},{5,3},{6,8},{7,5},{8,10},{9,7},{10,12},{11... | collective-permute-start | bytes 393224 | tf_op jit(solution)/shard_map/ppermute | solution.py:431
  8.7 7.6 %all-to-all-start = ((f32[16,8,128]{2,1,0:T(8,128)}), f32[16,8,128]{2,1,0:T(8,128)S(1)}, u32[]{:S(2)}, u32[]{:S(2)}) async-start(f32[16,8,128]{2,1,0:T(8,128)} %bitcast.1), calls=%async_computation | async-start | bytes 131072 | tf_op jit(solution)/shard_map/all_to_all | solution.py:467
  16.3 2.0 %all-gather.1 = f32[4,2,8,8,128]{4,3,2,1,0:T(8,128)S(1)} all-gather(f32[2,2,8,8,128]{4,3,2,1,0:T(8,128)S(1)} %collective-permute-done), channel_id=3, replica_groups=mesh['gx'=64,'gy'=8,'gz'=2] {'gz'}, dimensions={0}, use_global_device_ids=true | all-gather | bytes 393216 | tf_op jit(solution)/shard_map/all_gather | solution.py:435
  18.5 4.1 %collective-permute-start.2 = (f32[2,4,32,128]{3,2,1,0:T(8,128)S(1)}, f32[2,4,32,128]{3,2,1,0:T(8,128)S(1)}, u32[]{:S(2)}, u32[]{:S(2)}) collective-permute-start(f32[2,4,32,128]{3,2,1,0:T(8,128)S(1)} %fusion.1), channel_id=1, source_target_pairs={{0,16},{16,32},{17,1},{32,48},{33,17},{48,64},{49,33},{64,80},{65,... | collective-permute-start | bytes 393224 | tf_op jit(solution)/shard_map/ppermute | solution.py:431
  22.5 1.4 %shard_map.87 = (f32[2,8,32,128]{3,2,1,0:T(8,128)S(1)}, f32[2,6,32,128]{3,2,1,0:T(8,128)S(1)}) custom-call(f32[128,128]{1,0:T(8,128)S(1)} %bitcast.19, f32[2,2,8,32,128]{4,3,2,1,0:T(8,128)S(1)} %pad_maximum_fusion.chip_ref), custom_call_target="tpu_custom_call" | custom-call | flops 100000 | bytes 100000 | tf_op jit(solution)/shard_map/pallas_call | solution.py:473
  23.9 2.9 %collective-permute-start.1 = (f32[2,6,32,128]{3,2,1,0:T(8,128)S(1)}, f32[2,6,32,128]{3,2,1,0:T(8,128)S(1)}, u32[]{:S(2)}, u32[]{:S(2)}) collective-permute-start(f32[2,6,32,128]{3,2,1,0:T(8,128)S(1)} %get-tuple-element.28), channel_id=1, source_target_pairs={{0,16},{16,32},{17,1},{32,48},{33,17},{48,64},{49,33},{64,80},{65,... | collective-permute-start | bytes 589832 | tf_op jit(solution)/shard_map/ppermute | solution.py:431
  26.8 0.0 collective-permute-done.2
  26.8 3.8 %all-gather.2 = f32[4,4,32,128]{3,2,1,0:T(8,128)S(1)} all-gather(f32[2,4,32,128]{3,2,1,0:T(8,128)S(1)} %collective-permute-done.2), channel_id=4, replica_groups=mesh['gx'=64,'gy'=8,'gz'=2] {'gz'}, dimensions={0}, use_global_device_ids=true | all-gather | bytes 393216 | tf_op jit(solution)/shard_map/all_gather | solution.py:435
  30.6 0.9 %shard_map.88 = (f32[20,32,256]{2,1,0:T(8,128)S(1)}, f32[20,32,256]{2,1,0:T(8,128)S(1)}, f32[20,32,256]{2,1,0:T(8,128)S(1)}, f32[20,32,256]{2,1,0:T(8,128)S(1)},...) custom-call(f32[2,2,8,32,128]{4,3,2,1,0:T(8,128)S(1)} %pad_maximum_f, ...), custom_call_target="tpu_custom_call" | custom-call | flops 5000000 | bytes 5000000 | tf_op jit(solution)/shard_map/pallas_call | solution.py:483
  31.5 0.0 collective-permute-done.1
  31.5 4.9 %all-gather.3 = f32[4,6,32,128]{3,2,1,0:T(8,128)S(1)} all-gather(f32[2,6,32,128]{3,2,1,0:T(8,128)S(1)} %collective-permute-done.1), channel_id=5, replica_groups=mesh['gx'=64,'gy'=8,'gz'=2] {'gz'}, dimensions={0}, use_global_device_ids=true | all-gather | bytes 589824 | tf_op jit(solution)/shard_map/all_gather | solution.py:435
  36.4 1.8 %shard_map.89 = (f32[8,16,128]{2,1,0:T(8,128)}, f32[6,4,128]{2,1,0:T(4,128)S(1)}) custom-call(f32[2,8,32,128]{3,2,1,0:T(8,128)S(1)} %get-tuple-element.27.source_ref, f32[2,2,6,32,128]{4,3,2,1,0:T(8,128)S(1)} %bitcast.16, f32[20,32,256]{2,1,0:T(8,128)S(1)} %get-tuple-element.31.wx_ref, f32[20,32,256]{2,1,0:T(8,128)S(1)} %get-tuple-element.32.wy_ref, ...), custom_call_target="tpu_custom_call" | custom-call | flops 5000000 | bytes 5000000 | tf_op jit(solution)/shard_map/pallas_call | solution.py:493
  38.2 2.2 %collective-permute-start.3 = (f32[6,4,128]{2,1,0:T(4,128)S(1)}, f32[6,4,128]{2,1,0:T(4,128)S(1)}, u32[]{:S(2)}, u32[]{:S(2)}) collective-permute-start(f32[6,4,128]{2,1,0:T(4,128)S(1)} %get-tuple-element.44), channel_id=1, source_target_pairs={{0,2},{2,4},{3,1},{4,6},{5,3},{6,8},{7,5},{8,10},{9,7},{10,12},{11... | collective-permute-start | bytes 36872 | tf_op jit(solution)/shard_map/ppermute | solution.py:431
  40.4 2.2 %collective-permute-done.3 = f32[6,4,128]{2,1,0:T(4,128)S(1)} collective-permute-done((f32[6,4,128]{2,1,0:T(4,128)S(1)}, f32[6,4,128]{2,1,0:T(4,128)S(1)}, u32[]{:S(2)}, u32[]{:S(2)}) %collective-permute-start.3) | collective-permute-done | bytes 12320 | tf_op jit(solution)/shard_map/ppermute | solution.py:431
  42.6 4.2 %all-gather.4 = f32[12,4,128]{2,1,0:T(4,128)S(1)} all-gather(f32[6,4,128]{2,1,0:T(4,128)S(1)} %collective-permute-done.3), channel_id=6, replica_groups=mesh['gx'=64,'gy'=8,'gz'=2] {'gz'}, dimensions={0}, use_global_device_ids=true | all-gather | bytes 36864 | tf_op jit(solution)/shard_map/all_gather | solution.py:435
  46.8 2.1 %collective-permute-start.4 = (f32[3,6,4,128]{3,2,1,0:T(4,128)S(1)}, f32[3,6,4,128]{3,2,1,0:T(4,128)S(1)}, u32[]{:S(2)}, u32[]{:S(2)}) collective-permute-start(f32[3,6,4,128]{3,2,1,0:T(4,128)S(1)} %pad_maximum_fusion.2.mid_ref), channel_id=1, source_target_pairs={{0,16},{16,32},{17,1},{32,48},{33,17},{48,64},{49,33},{64,80},{65,... | collective-permute-start | bytes 110600 | tf_op jit(solution)/shard_map/ppermute | solution.py:431
  48.9 1.9 %collective-permute-start.5 = (f32[3,6,4,128]{3,2,1,0:T(4,128)S(1)}, f32[3,6,4,128]{3,2,1,0:T(4,128)S(1)}, u32[]{:S(2)}, u32[]{:S(2)}) collective-permute-start(f32[3,6,4,128]{3,2,1,0:T(4,128)S(1)} %pad_maximum_fusion.2.mid_ref), channel_id=1, source_target_pairs={{0,32},{16,48},{32,64},{33,1},{48,80},{49,17},{64,96},{65,33},{80,... | collective-permute-start | bytes 110600 | tf_op jit(solution)/shard_map/ppermute | solution.py:431
  50.9 0.7 %shard_map.86 = f32[32,8,64]{2,1,0:T(8,128)} custom-call(s32[1]{0:T(128)S(6)} %copy.9.count_ref, f32[16,8,128]{2,1,0:T(8,128)S(1)} %copy-done), custom_call_target="tpu_custom_call" | custom-call | flops 100000 | bytes 100000 | tf_op jit(solution)/shard_map/pallas_call | solution.py:464
  51.6 0.1 collective-permute-done.4
  51.7 2.9 %collective-permute-done.5 = f32[3,6,4,128]{3,2,1,0:T(4,128)S(1)} collective-permute-done((f32[3,6,4,128]{3,2,1,0:T(4,128)S(1)}, f32[3,6,4,128]{3,2,1,0:T(4,128)S(1)}, u32[]{:S(2)}, u32[]{:S(2)}) %collective-permute-start.5) | collective-permute-done | bytes 36896 | tf_op jit(solution)/shard_map/ppermute | solution.py:431
  54.6 6.3 %all-gather.5 = f32[4,3,6,4,128]{4,3,2,1,0:T(4,128)S(1)} all-gather(f32[2,3,6,4,128]{4,3,2,1,0:T(4,128)S(1)} %pad_maximum_fusion.1), channel_id=7, replica_groups=mesh['gx'=64,'gy'=8,'gz'=2] {'gz'}, dimensions={0}, use_global_device_ids=true | all-gather | bytes 221184 | tf_op jit(solution)/shard_map/all_gather | solution.py:435
  60.9 1.2 %shard_map.90 = f32[1,2,16]{2,1,0:T(2,128)} custom-call(f32[3,6,4,128]{3,2,1,0:T(4,128)S(1)} %pad_maximum_fusion.2.mid_ref, f32[2,2,3,6,4,128]{5,4,3,2,1,0:T(4,128)S(1)} %bitcast.18), custom_call_target="tpu_custom_call" | custom-call | flops 100000 | bytes 100000 | tf_op jit(solution)/shard_map/pallas_call | solution.py:506
  (12 shorter events, 0.2 us)
Async XLA Ops:
  6.6 9.8 %collective-permute-start = (f32[2,2,8,8,128]{4,3,2,1,0:T(8,128)S(1)}, f32[2,2,8,8,128]{4,3,2,1,0:T(8,128)S(1)}, u32[]{:S(2)}, u32[]{:S(2)}) collective-permute-start(f32[2,2,8,8,128]{4,3,2,1,0:T(8,128)S(1)} %slice_select_fusion.1), channel_id=1, source_target_pairs={{0,2},{2,4},{3,1},{4,6},{5,3},{6,8},{7,5},{8,10},{9,7},{10,12},{11... | collective-permute-start | bytes 393224 | tf_op jit(solution)/shard_map/ppermute | solution.py:431
  8.7 13.8 %all-to-all-start = ((f32[16,8,128]{2,1,0:T(8,128)}), f32[16,8,128]{2,1,0:T(8,128)S(1)}, u32[]{:S(2)}, u32[]{:S(2)}) async-start(f32[16,8,128]{2,1,0:T(8,128)} %bitcast.1), calls=%async_computation | async-start | bytes 131072 | tf_op jit(solution)/shard_map/all_to_all | solution.py:467
  18.5 8.3 %collective-permute-start.2 = (f32[2,4,32,128]{3,2,1,0:T(8,128)S(1)}, f32[2,4,32,128]{3,2,1,0:T(8,128)S(1)}, u32[]{:S(2)}, u32[]{:S(2)}) collective-permute-start(f32[2,4,32,128]{3,2,1,0:T(8,128)S(1)} %fusion.1), channel_id=1, source_target_pairs={{0,16},{16,32},{17,1},{32,48},{33,17},{48,64},{49,33},{64,80},{65,... | collective-permute-start | bytes 393224 | tf_op jit(solution)/shard_map/ppermute | solution.py:431
  23.9 7.6 %collective-permute-start.1 = (f32[2,6,32,128]{3,2,1,0:T(8,128)S(1)}, f32[2,6,32,128]{3,2,1,0:T(8,128)S(1)}, u32[]{:S(2)}, u32[]{:S(2)}) collective-permute-start(f32[2,6,32,128]{3,2,1,0:T(8,128)S(1)} %get-tuple-element.28), channel_id=1, source_target_pairs={{0,16},{16,32},{17,1},{32,48},{33,17},{48,64},{49,33},{64,80},{65,... | collective-permute-start | bytes 589832 | tf_op jit(solution)/shard_map/ppermute | solution.py:431
  38.2 4.4 %collective-permute-start.3 = (f32[6,4,128]{2,1,0:T(4,128)S(1)}, f32[6,4,128]{2,1,0:T(4,128)S(1)}, u32[]{:S(2)}, u32[]{:S(2)}) collective-permute-start(f32[6,4,128]{2,1,0:T(4,128)S(1)} %get-tuple-element.44), channel_id=1, source_target_pairs={{0,2},{2,4},{3,1},{4,6},{5,3},{6,8},{7,5},{8,10},{9,7},{10,12},{11... | collective-permute-start | bytes 36872 | tf_op jit(solution)/shard_map/ppermute | solution.py:431
  46.8 4.1 %copy-start = (f32[16,8,128]{2,1,0:T(8,128)S(1)}, f32[16,8,128]{2,1,0:T(8,128)}, u32[]{:S(2)}) copy-start(f32[16,8,128]{2,1,0:T(8,128)} %get-tuple-element.24.second_ref) | copy-start | bytes 196612
  46.8 4.8 %collective-permute-start.4 = (f32[3,6,4,128]{3,2,1,0:T(4,128)S(1)}, f32[3,6,4,128]{3,2,1,0:T(4,128)S(1)}, u32[]{:S(2)}, u32[]{:S(2)}) collective-permute-start(f32[3,6,4,128]{3,2,1,0:T(4,128)S(1)} %pad_maximum_fusion.2.mid_ref), channel_id=1, source_target_pairs={{0,16},{16,32},{17,1},{32,48},{33,17},{48,64},{49,33},{64,80},{65,... | collective-permute-start | bytes 110600 | tf_op jit(solution)/shard_map/ppermute | solution.py:431
  48.9 5.6 %collective-permute-start.5 = (f32[3,6,4,128]{3,2,1,0:T(4,128)S(1)}, f32[3,6,4,128]{3,2,1,0:T(4,128)S(1)}, u32[]{:S(2)}, u32[]{:S(2)}) collective-permute-start(f32[3,6,4,128]{3,2,1,0:T(4,128)S(1)} %pad_maximum_fusion.2.mid_ref), channel_id=1, source_target_pairs={{0,32},{16,48},{32,64},{33,1},{48,80},{49,17},{64,96},{65,33},{80,... | collective-permute-start | bytes 110600 | tf_op jit(solution)/shard_map/ppermute | solution.py:431

commit v10 on v8

--- a/solution.py
+++ b/solution.py
@@ -373,11 +373,8 @@
     win_ref[...] = jnp.zeros(win_ref.shape, F32)
     for number in range(3):
         for part in range(3):
-            blocks = [
-                side_ref[0, 1, part], side_ref[0, 0, part], mid_ref[part],
-                side_ref[1, 0, part], side_ref[1, 1, part],
-            ]
-            for place, block in enumerate(blocks):
+            for place in range(5):
+                block = (side_ref[0, place], mid_ref[place], side_ref[1, place])[part]
                 win_ref[number, 2 * place : 2 * place + 2, 4 * part : 4 * part + 4] = block[
                     2 * number : 2 * number + 2
                 ]
@@ -496,9 +493,9 @@
         flops=5_000_000,
         outs=[vmem] * 2,
     )(source, side, *weights[:-1], last)
-    halo = shared(split_send(pay, "gy", 1))
-    mid = jnp.stack([halo[0], pay, halo[1]])
-    sides = shared(jnp.stack([split_send(mid, "gx", 1), split_send(mid, "gx", 2)]))
+    far = shared(jnp.stack([split_send(pay, "gx", 1), split_send(pay, "gx", 2)]))
+    mid = jnp.stack([far[0, 1], far[0, 0], pay, far[1, 0], far[1, 1]])
+    sides = shared(split_send(mid, "gy", 1))
     deep_solution = call(
         functools.partial(deep_kernel, sizes),
         struct((1, 2, 16), F32),

time: 62.5 us -> 62.6 us (level)
  transfers between devices with their start and end apart: 7 -> 7, of which waited for: 2 -> 3; matrix products, arithmetic and copies ran while one was open for 0% -> 0% of each run, Pallas kernels for 5% -> 5%
where the time goes in v10:
time: 62.6 us; the launch traced here: 62.2 us
  blocking collectives  23.2 us (37%)
  starting transfers between devices  23 us (37%)
  Pallas kernels  8.71 us (14%)
  waiting for transfers between devices  5.73 us (9%)
  between operations  1.44 us (2%)
    all_gather x6, blocking collectives, shared(): return lax.all_gather(values, 'gz')  23.2 us
    ppermute x6, starting transfers between devices, split_send(): return lax.ppermute(values, (axis, 'gz'), pairs)  15.4 us
    all_to_all x1, starting transfers between devices, per_device(): lax.all_to_all(send.reshape(16, 8, 128), ('gy', 'gz'), 0, 0)  7.58 us
    ppermute x6, waiting for transfers between devices, split_send(): return lax.ppermute(values, (axis, 'gz'), pairs)  5.73 us
    pallas_call x1, Pallas kernels, per_device(): call(fine_kernel, (struct((16, 8, 128), F32), struct((128, 128), F32), ow...  2.74 us
    pallas_call x1, Pallas kernels, per_device(): call(base_kernel, (block, struct((6, 4, 128), F32)), [vmem] * 14, [pltpu....  1.75 us
    pallas_call x1, Pallas kernels, per_device(): call(place_kernel, (struct((2, 8, 32, 128), F32), struct((2, 6, 32, 128),...  1.37 us
  transfers between devices with their start and end apart: 7, of which 3 were waited for; matrix products, arithmetic and copies ran while one was open for 0% of the time, Pallas kernels for 5%

profile of v10, /device:TPU:521, one launch (start us, length us, event | category | flops | bytes accessed | tf_op | source)
XLA Modules:
  0.0 62.2 jit_solution(15844469006857311697)
XLA Ops:
  1.3 2.7 %shard_map.85 = (f32[16,8,128]{2,1,0:T(8,128)}, f32[128,128]{1,0:T(8,128)}, f32[2,8,16,128]{3,2,1,0:T(8,128)}) custom-call(s32[1]{0:T(128)S(6)} %copy.13.count_ref, s32[1,32]{1,0:T(1,128)} %bitcast.42, f32[32,8,64]{2,1,0:T(8,128)} %rhs_hbm.1, bf16[32,8,64]{2,1,0:T(8,128)(2,1)} %coef_hbm.1, f32[8,16,128]{2,1,0:T(8,128)} %grid_hbm.1, bf16[8,16,128]{2,1,0:T(8,128)(2,1)} %cond_hbm.1), custom_call_target="tpu_custom_call" | custom-call | flops 100000 | bytes 100000 | tf_op jit(solution)/shard_map/pallas_call | solution.py:443
  4.0 2.5 %all-gather = f32[4,8,16,128]{3,2,1,0:T(8,128)S(1)} all-gather(f32[2,8,16,128]{3,2,1,0:T(8,128)} %get-tuple-element.26), channel_id=2, replica_groups=mesh['gx'=64,'gy'=8,'gz'=2] {'gz'}, dimensions={0}, use_global_device_ids=true | all-gather | bytes 393216 | tf_op jit(solution)/shard_map/all_gather | solution.py:429
  6.6 2.2 %collective-permute-start = (f32[2,2,8,8,128]{4,3,2,1,0:T(8,128)S(1)}, f32[2,2,8,8,128]{4,3,2,1,0:T(8,128)S(1)}, u32[]{:S(2)}, u32[]{:S(2)}) collective-permute-start(f32[2,2,8,8,128]{4,3,2,1,0:T(8,128)S(1)} %slice_select_fusion.1), channel_id=1, source_target_pairs={{0,2},{2,4},{3,1},{4,6},{5,3},{6,8},{7,5},{8,10},{9,7},{10,12},{11... | collective-permute-start | bytes 393224 | tf_op jit(solution)/shard_map/ppermute | solution.py:425
  8.7 7.6 %all-to-all-start = ((f32[16,8,128]{2,1,0:T(8,128)}), f32[16,8,128]{2,1,0:T(8,128)S(1)}, u32[]{:S(2)}, u32[]{:S(2)}) async-start(f32[16,8,128]{2,1,0:T(8,128)} %bitcast.1), calls=%async_computation | async-start | bytes 131072 | tf_op jit(solution)/shard_map/all_to_all | solution.py:461
  16.3 2.0 %all-gather.1 = f32[4,2,8,8,128]{4,3,2,1,0:T(8,128)S(1)} all-gather(f32[2,2,8,8,128]{4,3,2,1,0:T(8,128)S(1)} %collective-permute-done), channel_id=3, replica_groups=mesh['gx'=64,'gy'=8,'gz'=2] {'gz'}, dimensions={0}, use_global_device_ids=true | all-gather | bytes 393216 | tf_op jit(solution)/shard_map/all_gather | solution.py:429
  18.5 4.1 %collective-permute-start.2 = (f32[2,4,32,128]{3,2,1,0:T(8,128)S(1)}, f32[2,4,32,128]{3,2,1,0:T(8,128)S(1)}, u32[]{:S(2)}, u32[]{:S(2)}) collective-permute-start(f32[2,4,32,128]{3,2,1,0:T(8,128)S(1)} %fusion.1), channel_id=1, source_target_pairs={{0,16},{16,32},{17,1},{32,48},{33,17},{48,64},{49,33},{64,80},{65,... | collective-permute-start | bytes 393224 | tf_op jit(solution)/shard_map/ppermute | solution.py:425
  22.5 1.4 %shard_map.87 = (f32[2,8,32,128]{3,2,1,0:T(8,128)S(1)}, f32[2,6,32,128]{3,2,1,0:T(8,128)S(1)}) custom-call(f32[128,128]{1,0:T(8,128)S(1)} %bitcast.33, f32[2,2,8,32,128]{4,3,2,1,0:T(8,128)S(1)} %pad_maximum_fusion.chip_ref), custom_call_target="tpu_custom_call" | custom-call | flops 100000 | bytes 100000 | tf_op jit(solution)/shard_map/pallas_call | solution.py:467
  23.9 2.9 %collective-permute-start.1 = (f32[2,6,32,128]{3,2,1,0:T(8,128)S(1)}, f32[2,6,32,128]{3,2,1,0:T(8,128)S(1)}, u32[]{:S(2)}, u32[]{:S(2)}) collective-permute-start(f32[2,6,32,128]{3,2,1,0:T(8,128)S(1)} %get-tuple-element.28), channel_id=1, source_target_pairs={{0,16},{16,32},{17,1},{32,48},{33,17},{48,64},{49,33},{64,80},{65,... | collective-permute-start | bytes 589832 | tf_op jit(solution)/shard_map/ppermute | solution.py:425
  26.8 0.0 collective-permute-done.2
  26.8 3.8 %all-gather.2 = f32[4,4,32,128]{3,2,1,0:T(8,128)S(1)} all-gather(f32[2,4,32,128]{3,2,1,0:T(8,128)S(1)} %collective-permute-done.2), channel_id=4, replica_groups=mesh['gx'=64,'gy'=8,'gz'=2] {'gz'}, dimensions={0}, use_global_device_ids=true | all-gather | bytes 393216 | tf_op jit(solution)/shard_map/all_gather | solution.py:429
  30.6 0.9 %shard_map.88 = (f32[20,32,256]{2,1,0:T(8,128)S(1)}, f32[20,32,256]{2,1,0:T(8,128)S(1)}, f32[20,32,256]{2,1,0:T(8,128)S(1)}, f32[20,32,256]{2,1,0:T(8,128)S(1)},...) custom-call(f32[2,2,8,32,128]{4,3,2,1,0:T(8,128)S(1)} %pad_maximum_f, ...), custom_call_target="tpu_custom_call" | custom-call | flops 5000000 | bytes 5000000 | tf_op jit(solution)/shard_map/pallas_call | solution.py:477
  31.5 0.0 collective-permute-done.1
  31.5 4.9 %all-gather.3 = f32[4,6,32,128]{3,2,1,0:T(8,128)S(1)} all-gather(f32[2,6,32,128]{3,2,1,0:T(8,128)S(1)} %collective-permute-done.1), channel_id=5, replica_groups=mesh['gx'=64,'gy'=8,'gz'=2] {'gz'}, dimensions={0}, use_global_device_ids=true | all-gather | bytes 589824 | tf_op jit(solution)/shard_map/all_gather | solution.py:429
  36.4 1.8 %shard_map.89 = (f32[8,16,128]{2,1,0:T(8,128)}, f32[6,4,128]{2,1,0:T(4,128)S(1)}) custom-call(f32[2,8,32,128]{3,2,1,0:T(8,128)S(1)} %get-tuple-element.27.source_ref, f32[2,2,6,32,128]{4,3,2,1,0:T(8,128)S(1)} %bitcast.30, f32[20,32,256]{2,1,0:T(8,128)S(1)} %get-tuple-element.31.wx_ref, f32[20,32,256]{2,1,0:T(8,128)S(1)} %get-tuple-element.32.wy_ref, ...), custom_call_target="tpu_custom_call" | custom-call | flops 5000000 | bytes 5000000 | tf_op jit(solution)/shard_map/pallas_call | solution.py:487
  38.2 2.2 %collective-permute-start.3 = (f32[6,4,128]{2,1,0:T(4,128)S(1)}, f32[6,4,128]{2,1,0:T(4,128)S(1)}, u32[]{:S(2)}, u32[]{:S(2)}) collective-permute-start(f32[6,4,128]{2,1,0:T(4,128)S(1)} %get-tuple-element.44), channel_id=1, source_target_pairs={{0,16},{16,32},{17,1},{32,48},{33,17},{48,64},{49,33},{64,80},{65,... | collective-permute-start | bytes 36872 | tf_op jit(solution)/shard_map/ppermute | solution.py:425
  40.3 1.9 %collective-permute-start.4 = (f32[6,4,128]{2,1,0:T(4,128)S(1)}, f32[6,4,128]{2,1,0:T(4,128)S(1)}, u32[]{:S(2)}, u32[]{:S(2)}) collective-permute-start(f32[6,4,128]{2,1,0:T(4,128)S(1)} %get-tuple-element.44), channel_id=1, source_target_pairs={{0,32},{16,48},{32,64},{33,1},{48,80},{49,17},{64,96},{65,33},{80,... | collective-permute-start | bytes 36872 | tf_op jit(solution)/shard_map/ppermute | solution.py:425
  42.3 0.3 collective-permute-done.3
  42.6 3.4 %collective-permute-done.4 = f32[6,4,128]{2,1,0:T(4,128)S(1)} collective-permute-done((f32[6,4,128]{2,1,0:T(4,128)S(1)}, f32[6,4,128]{2,1,0:T(4,128)S(1)}, u32[]{:S(2)}, u32[]{:S(2)}) %collective-permute-start.4) | collective-permute-done | bytes 12320 | tf_op jit(solution)/shard_map/ppermute | solution.py:425
  46.0 5.8 %all-gather.4 = f32[4,6,4,128]{3,2,1,0:T(4,128)S(1)} all-gather(f32[2,6,4,128]{3,2,1,0:T(4,128)S(1)} %pad_maximum_fusion.1), channel_id=6, replica_groups=mesh['gx'=64,'gy'=8,'gz'=2] {'gz'}, dimensions={0}, use_global_device_ids=true | all-gather | bytes 73728 | tf_op jit(solution)/shard_map/all_gather | solution.py:429
  51.8 2.2 %collective-permute-start.5 = (f32[5,6,4,128]{3,2,1,0:T(4,128)S(1)}, f32[5,6,4,128]{3,2,1,0:T(4,128)S(1)}, u32[]{:S(2)}, u32[]{:S(2)}) collective-permute-start(f32[5,6,4,128]{3,2,1,0:T(4,128)S(1)} %fusion.2.mid_ref), channel_id=1, source_target_pairs={{0,2},{2,4},{3,1},{4,6},{5,3},{6,8},{7,5},{8,10},{9,7},{10,12},{11... | collective-permute-start | bytes 184328 | tf_op jit(solution)/shard_map/ppermute | solution.py:425
  54.0 0.7 %shard_map.86 = f32[32,8,64]{2,1,0:T(8,128)} custom-call(s32[1]{0:T(128)S(6)} %copy.13.count_ref, f32[16,8,128]{2,1,0:T(8,128)S(1)} %copy-done), custom_call_target="tpu_custom_call" | custom-call | flops 100000 | bytes 100000 | tf_op jit(solution)/shard_map/pallas_call | solution.py:458
  54.7 2.0 %collective-permute-done.5 = f32[5,6,4,128]{3,2,1,0:T(4,128)S(1)} collective-permute-done((f32[5,6,4,128]{3,2,1,0:T(4,128)S(1)}, f32[5,6,4,128]{3,2,1,0:T(4,128)S(1)}, u32[]{:S(2)}, u32[]{:S(2)}) %collective-permute-start.5) | collective-permute-done | bytes 61472 | tf_op jit(solution)/shard_map/ppermute | solution.py:425
  56.8 4.2 %all-gather.5 = f32[10,6,4,128]{3,2,1,0:T(4,128)S(1)} all-gather(f32[5,6,4,128]{3,2,1,0:T(4,128)S(1)} %collective-permute-done.5), channel_id=7, replica_groups=mesh['gx'=64,'gy'=8,'gz'=2] {'gz'}, dimensions={0}, use_global_device_ids=true | all-gather | bytes 184320 | tf_op jit(solution)/shard_map/all_gather | solution.py:429
  61.0 1.2 %shard_map.90 = f32[1,2,16]{2,1,0:T(2,128)} custom-call(f32[5,6,4,128]{3,2,1,0:T(4,128)S(1)} %fusion.2.mid_ref, f32[2,5,6,4,128]{4,3,2,1,0:T(4,128)S(1)} %bitcast.32), custom_call_target="tpu_custom_call" | custom-call | flops 100000 | bytes 100000 | tf_op jit(solution)/shard_map/pallas_call | solution.py:499
  (15 shorter events, 0.2 us)
Async XLA Ops:
  6.6 9.8 %collective-permute-start = (f32[2,2,8,8,128]{4,3,2,1,0:T(8,128)S(1)}, f32[2,2,8,8,128]{4,3,2,1,0:T(8,128)S(1)}, u32[]{:S(2)}, u32[]{:S(2)}) collective-permute-start(f32[2,2,8,8,128]{4,3,2,1,0:T(8,128)S(1)} %slice_select_fusion.1), channel_id=1, source_target_pairs={{0,2},{2,4},{3,1},{4,6},{5,3},{6,8},{7,5},{8,10},{9,7},{10,12},{11... | collective-permute-start | bytes 393224 | tf_op jit(solution)/shard_map/ppermute | solution.py:425
  8.7 13.8 %all-to-all-start = ((f32[16,8,128]{2,1,0:T(8,128)}), f32[16,8,128]{2,1,0:T(8,128)S(1)}, u32[]{:S(2)}, u32[]{:S(2)}) async-start(f32[16,8,128]{2,1,0:T(8,128)} %bitcast.1), calls=%async_computation | async-start | bytes 131072 | tf_op jit(solution)/shard_map/all_to_all | solution.py:461
  18.5 8.3 %collective-permute-start.2 = (f32[2,4,32,128]{3,2,1,0:T(8,128)S(1)}, f32[2,4,32,128]{3,2,1,0:T(8,128)S(1)}, u32[]{:S(2)}, u32[]{:S(2)}) collective-permute-start(f32[2,4,32,128]{3,2,1,0:T(8,128)S(1)} %fusion.1), channel_id=1, source_target_pairs={{0,16},{16,32},{17,1},{32,48},{33,17},{48,64},{49,33},{64,80},{65,... | collective-permute-start | bytes 393224 | tf_op jit(solution)/shard_map/ppermute | solution.py:425
  23.9 7.6 %collective-permute-start.1 = (f32[2,6,32,128]{3,2,1,0:T(8,128)S(1)}, f32[2,6,32,128]{3,2,1,0:T(8,128)S(1)}, u32[]{:S(2)}, u32[]{:S(2)}) collective-permute-start(f32[2,6,32,128]{3,2,1,0:T(8,128)S(1)} %get-tuple-element.28), channel_id=1, source_target_pairs={{0,16},{16,32},{17,1},{32,48},{33,17},{48,64},{49,33},{64,80},{65,... | collective-permute-start | bytes 589832 | tf_op jit(solution)/shard_map/ppermute | solution.py:425
  38.2 4.4 %collective-permute-start.3 = (f32[6,4,128]{2,1,0:T(4,128)S(1)}, f32[6,4,128]{2,1,0:T(4,128)S(1)}, u32[]{:S(2)}, u32[]{:S(2)}) collective-permute-start(f32[6,4,128]{2,1,0:T(4,128)S(1)} %get-tuple-element.44), channel_id=1, source_target_pairs={{0,16},{16,32},{17,1},{32,48},{33,17},{48,64},{49,33},{64,80},{65,... | collective-permute-start | bytes 36872 | tf_op jit(solution)/shard_map/ppermute | solution.py:425
  40.3 5.6 %collective-permute-start.4 = (f32[6,4,128]{2,1,0:T(4,128)S(1)}, f32[6,4,128]{2,1,0:T(4,128)S(1)}, u32[]{:S(2)}, u32[]{:S(2)}) collective-permute-start(f32[6,4,128]{2,1,0:T(4,128)S(1)} %get-tuple-element.44), channel_id=1, source_target_pairs={{0,32},{16,48},{32,64},{33,1},{48,80},{49,17},{64,96},{65,33},{80,... | collective-permute-start | bytes 36872 | tf_op jit(solution)/shard_map/ppermute | solution.py:425
  51.7 2.3 %copy-start = (f32[16,8,128]{2,1,0:T(8,128)S(1)}, f32[16,8,128]{2,1,0:T(8,128)}, u32[]{:S(2)}) copy-start(f32[16,8,128]{2,1,0:T(8,128)} %get-tuple-element.24.second_ref) | copy-start | bytes 196612
  51.8 5.0 %collective-permute-start.5 = (f32[5,6,4,128]{3,2,1,0:T(4,128)S(1)}, f32[5,6,4,128]{3,2,1,0:T(4,128)S(1)}, u32[]{:S(2)}, u32[]{:S(2)}) collective-permute-start(f32[5,6,4,128]{3,2,1,0:T(4,128)S(1)} %fusion.2.mid_ref), channel_id=1, source_target_pairs={{0,2},{2,4},{3,1},{4,6},{5,3},{6,8},{7,5},{8,10},{9,7},{10,12},{11... | collective-permute-start | bytes 184328 | tf_op jit(solution)/shard_map/ppermute | solution.py:425

commit v11 on v8

--- a/solution.py
+++ b/solution.py
@@ -71,55 +71,9 @@
         pltpu.make_async_copy(grid_hbm, grid_ref, sems.at[3]),
         pltpu.make_async_copy(cond_hbm, cond_ref, sems.at[4]),
     ]
-    for load in loads:
+    for load in (loads[2], *loads[:2], *loads[3:]):
         load.start()
-    half = rhs_ref.shape[0] // 2
-    loads[0].wait()
-    k = coef_ref[...].astype(F32) * 0.5
-    h = jnp.concatenate([k[:half], k[half:]], axis=2)
-    shape = h.shape
-    x, lane = iota(shape, 1), iota(shape, 2)
-    y, z = (lane >> 3) & 7, lane & 7
-
-    def wrapped(values, amount):
-        return pltpu.roll(values, amount % 128, 2)
-
-    hx = jnp.where(x < 7, after(h, 1), 0.0)
-    hy = jnp.where(y < 7, wrapped(h, -8), 0.0)
-    hz = jnp.where(z < 7, wrapped(h, -1), 0.0)
-    diagonal = 6.0 * h + hx + hy + hz
-    diagonal += jnp.where(x > 0, before(h, 1), 0.0)
-    diagonal += jnp.where(y > 0, wrapped(h, 8), 0.0)
-    diagonal += jnp.where(z > 0, wrapped(h, 1), 0.0)
-    wx = jnp.where(x < 7, h + hx, 0.0)
-    wy = jnp.where(y < 7, h + hy, 0.0)
-    wz = jnp.where(z < 7, h + hz, 0.0)
-
-    def sides(u):
-        total = wx * after(u, 1) + before(wx * u, 1)
-        total += wy * wrapped(u, -8) + wrapped(wy * u, 8)
-        return total + wz * wrapped(u, -1) + wrapped(wz * u, 1)
-
-    scale = DAMPING * inverse(diagonal)
-    loads[1].wait()
-    source = jnp.concatenate([rhs_ref[:half], rhs_ref[half:]], axis=2)
-    first = source * scale
-    second = first + scale * (REST * source + sides(first))
-    residue = source - diagonal * second + sides(second)
-    second_ref[...] = second
-
     loads[2].wait()
-    square = (128, 128)
-    row, col = iota(square, 0), iota(square, 1)
-    iz, ix, iy = (col >> 4) & 3, (col >> 2) & 3, col & 3
-    match = (((row >> 4) & 3) == iy) & (((row >> 1) & 3) == iz)
-    keep = ((row >> 1) & 3) == ix
-    cells = residue.reshape(square)
-    parts = []
-    for number in range(2):
-        gather = jnp.where(match & ((row >> 6) == number), 0.5, 0.0)
-        parts.append(jnp.where(keep, dot(cells, gather), 0.0))
-
     wide = (32, 256)
     spread = jnp.where(iota(wide, 0) == (iota(wide, 1) >> 3), 1.0, 0.0)
     names = jnp.broadcast_to(target_ref[...].astype(F32), (8, 32))
@@ -136,13 +90,59 @@
     owner = chip * 2 + (row & 1)
     wanted = ((row & 7) < 6) & (chip >= 0) & (chip < 8) & ((col >> 3) < live)
     chosen = wanted & (owner == (name >> 8))
-    packed, tags = [], []
+    picked, tags = [], []
     for number in range(2):
         mine = chosen & (rank == number)
-        picked = jnp.where(mine, 1.0, 0.0)
-        packed.append(pick(picked[:, :128], parts[0]) + pick(picked[:, 128:], parts[1]))
+        picked.append(jnp.where(mine, 1.0, 0.0))
         tag = jnp.where(mine & ((col & 7) == 0), (name & 255) + 1, 0).astype(F32)
         tags.append(jnp.sum(tag, axis=1, keepdims=True))
+    half = rhs_ref.shape[0] // 2
+    loads[0].wait()
+    k = coef_ref[...].astype(F32) * 0.5
+    h = jnp.concatenate([k[:half], k[half:]], axis=2)
+    shape = h.shape
+    x, lane = iota(shape, 1), iota(shape, 2)
+    y, z = (lane >> 3) & 7, lane & 7
+
+    def wrapped(values, amount):
+        return pltpu.roll(values, amount % 128, 2)
+
+    hx = jnp.where(x < 7, after(h, 1), 0.0)
+    hy = jnp.where(y < 7, wrapped(h, -8), 0.0)
+    hz = jnp.where(z < 7, wrapped(h, -1), 0.0)
+    diagonal = 6.0 * h + hx + hy + hz
+    diagonal += jnp.where(x > 0, before(h, 1), 0.0)
+    diagonal += jnp.where(y > 0, wrapped(h, 8), 0.0)
+    diagonal += jnp.where(z > 0, wrapped(h, 1), 0.0)
+    wx = jnp.where(x < 7, h + hx, 0.0)
+    wy = jnp.where(y < 7, h + hy, 0.0)
+    wz = jnp.where(z < 7, h + hz, 0.0)
+
+    def sides(u):
+        total = wx * after(u, 1) + before(wx * u, 1)
+        total += wy * wrapped(u, -8) + wrapped(wy * u, 8)
+        return total + wz * wrapped(u, -1) + wrapped(wz * u, 1)
+
+    scale = DAMPING * inverse(diagonal)
+    loads[1].wait()
+    source = jnp.concatenate([rhs_ref[:half], rhs_ref[half:]], axis=2)
+    first = source * scale
+    second = first + scale * (REST * source + sides(first))
+    residue = source - diagonal * second + sides(second)
+    second_ref[...] = second
+
+    square = (128, 128)
+    row, col = iota(square, 0), iota(square, 1)
+    iz, ix, iy = (col >> 4) & 3, (col >> 2) & 3, col & 3
+    match = (((row >> 4) & 3) == iy) & (((row >> 1) & 3) == iz)
+    keep = ((row >> 1) & 3) == ix
+    cells = residue.reshape(square)
+    parts = []
+    for number in range(2):
+        gather = jnp.where(match & ((row >> 6) == number), 0.5, 0.0)
+        parts.append(jnp.where(keep, dot(cells, gather), 0.0))
+
+    packed = [pick(mine[:, :128], parts[0]) + pick(mine[:, 128:], parts[1]) for mine in picked]
     row, col = iota(square, 0), iota(square, 1)
     place = (row & 7) * 2
     tags = jnp.where(col == place, tags[0], 0.0) + jnp.where(col == place + 1, tags[1], 0.0)

time: 62.5 us -> 62.5 us (level)
  no operation moved by 1% of the time
where the time goes in v11:
time: 62.5 us; the launch traced here: 62.1 us
  blocking collectives  23.7 us (38%)
  starting transfers between devices  22.9 us (37%)
  Pallas kernels  8.69 us (14%)
  waiting for transfers between devices  5.17 us (8%)
  between operations  1.43 us (2%)
    all_gather x6, blocking collectives, shared(): return lax.all_gather(values, 'gz')  23.7 us
    ppermute x6, starting transfers between devices, split_send(): return lax.ppermute(values, (axis, 'gz'), pairs)  15.3 us
    all_to_all x1, starting transfers between devices, per_device(): lax.all_to_all(send.reshape(16, 8, 128), ('gy', 'gz'), 0, 0)  7.58 us
    ppermute x6, waiting for transfers between devices, split_send(): return lax.ppermute(values, (axis, 'gz'), pairs)  5.17 us
    pallas_call x1, Pallas kernels, per_device(): call(fine_kernel, (struct((16, 8, 128), F32), struct((128, 128), F32), ow...  2.73 us
    pallas_call x1, Pallas kernels, per_device(): call(base_kernel, (block, struct((6, 4, 128), F32)), [vmem] * 14, [pltpu....  1.75 us
    pallas_call x1, Pallas kernels, per_device(): call(place_kernel, (struct((2, 8, 32, 128), F32), struct((2, 6, 32, 128),...  1.37 us
  transfers between devices with their start and end apart: 7, of which 2 were waited for; matrix products, arithmetic and copies ran while one was open for 0% of the time, Pallas kernels for 5%

profile of v11, /device:TPU:521, one launch (start us, length us, event | category | flops | bytes accessed | tf_op | source)
XLA Modules:
  0.0 62.1 jit_solution(6388571318545876404)
XLA Ops:
  1.3 2.7 %shard_map.85 = (f32[16,8,128]{2,1,0:T(8,128)}, f32[128,128]{1,0:T(8,128)}, f32[2,8,16,128]{3,2,1,0:T(8,128)}) custom-call(s32[1]{0:T(128)S(6)} %copy.9.count_ref, s32[1,32]{1,0:T(1,128)} %bitcast.25, f32[32,8,64]{2,1,0:T(8,128)} %rhs_hbm.1, bf16[32,8,64]{2,1,0:T(8,128)(2,1)} %coef_hbm.1, f32[8,16,128]{2,1,0:T(8,128)} %grid_hbm.1, bf16[8,16,128]{2,1,0:T(8,128)(2,1)} %cond_hbm.1), custom_call_target="tpu_custom_call" | custom-call | flops 100000 | bytes 100000 | tf_op jit(solution)/shard_map/pallas_call | solution.py:446
  4.0 2.5 %all-gather = f32[4,8,16,128]{3,2,1,0:T(8,128)S(1)} all-gather(f32[2,8,16,128]{3,2,1,0:T(8,128)} %get-tuple-element.26), channel_id=2, replica_groups=mesh['gx'=64,'gy'=8,'gz'=2] {'gz'}, dimensions={0}, use_global_device_ids=true | all-gather | bytes 393216 | tf_op jit(solution)/shard_map/all_gather | solution.py:432
  6.6 2.2 %collective-permute-start = (f32[2,2,8,8,128]{4,3,2,1,0:T(8,128)S(1)}, f32[2,2,8,8,128]{4,3,2,1,0:T(8,128)S(1)}, u32[]{:S(2)}, u32[]{:S(2)}) collective-permute-start(f32[2,2,8,8,128]{4,3,2,1,0:T(8,128)S(1)} %slice_select_fusion.1), channel_id=1, source_target_pairs={{0,2},{2,4},{3,1},{4,6},{5,3},{6,8},{7,5},{8,10},{9,7},{10,12},{11... | collective-permute-start | bytes 393224 | tf_op jit(solution)/shard_map/ppermute | solution.py:428
  8.7 7.6 %all-to-all-start = ((f32[16,8,128]{2,1,0:T(8,128)}), f32[16,8,128]{2,1,0:T(8,128)S(1)}, u32[]{:S(2)}, u32[]{:S(2)}) async-start(f32[16,8,128]{2,1,0:T(8,128)} %bitcast.1), calls=%async_computation | async-start | bytes 131072 | tf_op jit(solution)/shard_map/all_to_all | solution.py:464
  16.3 0.0 collective-permute-done
  16.3 2.0 %all-gather.1 = f32[4,2,8,8,128]{4,3,2,1,0:T(8,128)S(1)} all-gather(f32[2,2,8,8,128]{4,3,2,1,0:T(8,128)S(1)} %collective-permute-done), channel_id=3, replica_groups=mesh['gx'=64,'gy'=8,'gz'=2] {'gz'}, dimensions={0}, use_global_device_ids=true | all-gather | bytes 393216 | tf_op jit(solution)/shard_map/all_gather | solution.py:432
  18.4 4.1 %collective-permute-start.2 = (f32[2,4,32,128]{3,2,1,0:T(8,128)S(1)}, f32[2,4,32,128]{3,2,1,0:T(8,128)S(1)}, u32[]{:S(2)}, u32[]{:S(2)}) collective-permute-start(f32[2,4,32,128]{3,2,1,0:T(8,128)S(1)} %fusion.1), channel_id=1, source_target_pairs={{0,16},{16,32},{17,1},{32,48},{33,17},{48,64},{49,33},{64,80},{65,... | collective-permute-start | bytes 393224 | tf_op jit(solution)/shard_map/ppermute | solution.py:428
  22.5 0.0 all-to-all-done
  22.5 1.4 %shard_map.87 = (f32[2,8,32,128]{3,2,1,0:T(8,128)S(1)}, f32[2,6,32,128]{3,2,1,0:T(8,128)S(1)}) custom-call(f32[128,128]{1,0:T(8,128)S(1)} %bitcast.19, f32[2,2,8,32,128]{4,3,2,1,0:T(8,128)S(1)} %pad_maximum_fusion.chip_ref), custom_call_target="tpu_custom_call" | custom-call | flops 100000 | bytes 100000 | tf_op jit(solution)/shard_map/pallas_call | solution.py:470
  23.9 2.9 %collective-permute-start.1 = (f32[2,6,32,128]{3,2,1,0:T(8,128)S(1)}, f32[2,6,32,128]{3,2,1,0:T(8,128)S(1)}, u32[]{:S(2)}, u32[]{:S(2)}) collective-permute-start(f32[2,6,32,128]{3,2,1,0:T(8,128)S(1)} %get-tuple-element.28), channel_id=1, source_target_pairs={{0,16},{16,32},{17,1},{32,48},{33,17},{48,64},{49,33},{64,80},{65,... | collective-permute-start | bytes 589832 | tf_op jit(solution)/shard_map/ppermute | solution.py:428
  26.8 3.8 %all-gather.2 = f32[4,4,32,128]{3,2,1,0:T(8,128)S(1)} all-gather(f32[2,4,32,128]{3,2,1,0:T(8,128)S(1)} %collective-permute-done.2), channel_id=4, replica_groups=mesh['gx'=64,'gy'=8,'gz'=2] {'gz'}, dimensions={0}, use_global_device_ids=true | all-gather | bytes 393216 | tf_op jit(solution)/shard_map/all_gather | solution.py:432
  30.6 0.9 %shard_map.88 = (f32[20,32,256]{2,1,0:T(8,128)S(1)}, f32[20,32,256]{2,1,0:T(8,128)S(1)}, f32[20,32,256]{2,1,0:T(8,128)S(1)}, f32[20,32,256]{2,1,0:T(8,128)S(1)},...) custom-call(f32[2,2,8,32,128]{4,3,2,1,0:T(8,128)S(1)} %pad_maximum_f, ...), custom_call_target="tpu_custom_call" | custom-call | flops 5000000 | bytes 5000000 | tf_op jit(solution)/shard_map/pallas_call | solution.py:480
  31.5 4.9 %all-gather.3 = f32[4,6,32,128]{3,2,1,0:T(8,128)S(1)} all-gather(f32[2,6,32,128]{3,2,1,0:T(8,128)S(1)} %collective-permute-done.1), channel_id=5, replica_groups=mesh['gx'=64,'gy'=8,'gz'=2] {'gz'}, dimensions={0}, use_global_device_ids=true | all-gather | bytes 589824 | tf_op jit(solution)/shard_map/all_gather | solution.py:432
  36.4 1.8 %shard_map.89 = (f32[8,16,128]{2,1,0:T(8,128)}, f32[6,4,128]{2,1,0:T(4,128)S(1)}) custom-call(f32[2,8,32,128]{3,2,1,0:T(8,128)S(1)} %get-tuple-element.27.source_ref, f32[2,2,6,32,128]{4,3,2,1,0:T(8,128)S(1)} %bitcast.16, f32[20,32,256]{2,1,0:T(8,128)S(1)} %get-tuple-element.31.wx_ref, f32[20,32,256]{2,1,0:T(8,128)S(1)} %get-tuple-element.32.wy_ref, ...), custom_call_target="tpu_custom_call" | custom-call | flops 5000000 | bytes 5000000 | tf_op jit(solution)/shard_map/pallas_call | solution.py:490
  38.1 2.2 %collective-permute-start.3 = (f32[6,4,128]{2,1,0:T(4,128)S(1)}, f32[6,4,128]{2,1,0:T(4,128)S(1)}, u32[]{:S(2)}, u32[]{:S(2)}) collective-permute-start(f32[6,4,128]{2,1,0:T(4,128)S(1)} %get-tuple-element.44), channel_id=1, source_target_pairs={{0,2},{2,4},{3,1},{4,6},{5,3},{6,8},{7,5},{8,10},{9,7},{10,12},{11... | collective-permute-start | bytes 36872 | tf_op jit(solution)/shard_map/ppermute | solution.py:428
  40.3 2.2 %collective-permute-done.3 = f32[6,4,128]{2,1,0:T(4,128)S(1)} collective-permute-done((f32[6,4,128]{2,1,0:T(4,128)S(1)}, f32[6,4,128]{2,1,0:T(4,128)S(1)}, u32[]{:S(2)}, u32[]{:S(2)}) %collective-permute-start.3) | collective-permute-done | bytes 12320 | tf_op jit(solution)/shard_map/ppermute | solution.py:428
  42.6 4.2 %all-gather.4 = f32[12,4,128]{2,1,0:T(4,128)S(1)} all-gather(f32[6,4,128]{2,1,0:T(4,128)S(1)} %collective-permute-done.3), channel_id=6, replica_groups=mesh['gx'=64,'gy'=8,'gz'=2] {'gz'}, dimensions={0}, use_global_device_ids=true | all-gather | bytes 36864 | tf_op jit(solution)/shard_map/all_gather | solution.py:432
  46.8 2.1 %collective-permute-start.4 = (f32[3,6,4,128]{3,2,1,0:T(4,128)S(1)}, f32[3,6,4,128]{3,2,1,0:T(4,128)S(1)}, u32[]{:S(2)}, u32[]{:S(2)}) collective-permute-start(f32[3,6,4,128]{3,2,1,0:T(4,128)S(1)} %pad_maximum_fusion.2.mid_ref), channel_id=1, source_target_pairs={{0,16},{16,32},{17,1},{32,48},{33,17},{48,64},{49,33},{64,80},{65,... | collective-permute-start | bytes 110600 | tf_op jit(solution)/shard_map/ppermute | solution.py:428
  48.9 1.9 %collective-permute-start.5 = (f32[3,6,4,128]{3,2,1,0:T(4,128)S(1)}, f32[3,6,4,128]{3,2,1,0:T(4,128)S(1)}, u32[]{:S(2)}, u32[]{:S(2)}) collective-permute-start(f32[3,6,4,128]{3,2,1,0:T(4,128)S(1)} %pad_maximum_fusion.2.mid_ref), channel_id=1, source_target_pairs={{0,32},{16,48},{32,64},{33,1},{48,80},{49,17},{64,96},{65,33},{80,... | collective-permute-start | bytes 110600 | tf_op jit(solution)/shard_map/ppermute | solution.py:428
  50.8 0.7 %shard_map.86 = f32[32,8,64]{2,1,0:T(8,128)} custom-call(s32[1]{0:T(128)S(6)} %copy.9.count_ref, f32[16,8,128]{2,1,0:T(8,128)S(1)} %copy-done), custom_call_target="tpu_custom_call" | custom-call | flops 100000 | bytes 100000 | tf_op jit(solution)/shard_map/pallas_call | solution.py:461
  51.6 0.0 collective-permute-done.4
  51.6 2.9 %collective-permute-done.5 = f32[3,6,4,128]{3,2,1,0:T(4,128)S(1)} collective-permute-done((f32[3,6,4,128]{3,2,1,0:T(4,128)S(1)}, f32[3,6,4,128]{3,2,1,0:T(4,128)S(1)}, u32[]{:S(2)}, u32[]{:S(2)}) %collective-permute-start.5) | collective-permute-done | bytes 36896 | tf_op jit(solution)/shard_map/ppermute | solution.py:428
  54.5 6.3 %all-gather.5 = f32[4,3,6,4,128]{4,3,2,1,0:T(4,128)S(1)} all-gather(f32[2,3,6,4,128]{4,3,2,1,0:T(4,128)S(1)} %pad_maximum_fusion.1), channel_id=7, replica_groups=mesh['gx'=64,'gy'=8,'gz'=2] {'gz'}, dimensions={0}, use_global_device_ids=true | all-gather | bytes 221184 | tf_op jit(solution)/shard_map/all_gather | solution.py:432
  60.8 1.2 %shard_map.90 = f32[1,2,16]{2,1,0:T(2,128)} custom-call(f32[3,6,4,128]{3,2,1,0:T(4,128)S(1)} %pad_maximum_fusion.2.mid_ref, f32[2,2,3,6,4,128]{5,4,3,2,1,0:T(4,128)S(1)} %bitcast.18), custom_call_target="tpu_custom_call" | custom-call | flops 100000 | bytes 100000 | tf_op jit(solution)/shard_map/pallas_call | solution.py:502
  (12 shorter events, 0.2 us)
Async XLA Ops:
  6.6 9.7 %collective-permute-start = (f32[2,2,8,8,128]{4,3,2,1,0:T(8,128)S(1)}, f32[2,2,8,8,128]{4,3,2,1,0:T(8,128)S(1)}, u32[]{:S(2)}, u32[]{:S(2)}) collective-permute-start(f32[2,2,8,8,128]{4,3,2,1,0:T(8,128)S(1)} %slice_select_fusion.1), channel_id=1, source_target_pairs={{0,2},{2,4},{3,1},{4,6},{5,3},{6,8},{7,5},{8,10},{9,7},{10,12},{11... | collective-permute-start | bytes 393224 | tf_op jit(solution)/shard_map/ppermute | solution.py:428
  8.7 13.8 %all-to-all-start = ((f32[16,8,128]{2,1,0:T(8,128)}), f32[16,8,128]{2,1,0:T(8,128)S(1)}, u32[]{:S(2)}, u32[]{:S(2)}) async-start(f32[16,8,128]{2,1,0:T(8,128)} %bitcast.1), calls=%async_computation | async-start | bytes 131072 | tf_op jit(solution)/shard_map/all_to_all | solution.py:464
  18.4 8.3 %collective-permute-start.2 = (f32[2,4,32,128]{3,2,1,0:T(8,128)S(1)}, f32[2,4,32,128]{3,2,1,0:T(8,128)S(1)}, u32[]{:S(2)}, u32[]{:S(2)}) collective-permute-start(f32[2,4,32,128]{3,2,1,0:T(8,128)S(1)} %fusion.1), channel_id=1, source_target_pairs={{0,16},{16,32},{17,1},{32,48},{33,17},{48,64},{49,33},{64,80},{65,... | collective-permute-start | bytes 393224 | tf_op jit(solution)/shard_map/ppermute | solution.py:428
  23.9 7.6 %collective-permute-start.1 = (f32[2,6,32,128]{3,2,1,0:T(8,128)S(1)}, f32[2,6,32,128]{3,2,1,0:T(8,128)S(1)}, u32[]{:S(2)}, u32[]{:S(2)}) collective-permute-start(f32[2,6,32,128]{3,2,1,0:T(8,128)S(1)} %get-tuple-element.28), channel_id=1, source_target_pairs={{0,16},{16,32},{17,1},{32,48},{33,17},{48,64},{49,33},{64,80},{65,... | collective-permute-start | bytes 589832 | tf_op jit(solution)/shard_map/ppermute | solution.py:428
  38.1 4.4 %collective-permute-start.3 = (f32[6,4,128]{2,1,0:T(4,128)S(1)}, f32[6,4,128]{2,1,0:T(4,128)S(1)}, u32[]{:S(2)}, u32[]{:S(2)}) collective-permute-start(f32[6,4,128]{2,1,0:T(4,128)S(1)} %get-tuple-element.44), channel_id=1, source_target_pairs={{0,2},{2,4},{3,1},{4,6},{5,3},{6,8},{7,5},{8,10},{9,7},{10,12},{11... | collective-permute-start | bytes 36872 | tf_op jit(solution)/shard_map/ppermute | solution.py:428
  46.8 4.1 %copy-start = (f32[16,8,128]{2,1,0:T(8,128)S(1)}, f32[16,8,128]{2,1,0:T(8,128)}, u32[]{:S(2)}) copy-start(f32[16,8,128]{2,1,0:T(8,128)} %get-tuple-element.24.second_ref) | copy-start | bytes 196612
  46.8 4.8 %collective-permute-start.4 = (f32[3,6,4,128]{3,2,1,0:T(4,128)S(1)}, f32[3,6,4,128]{3,2,1,0:T(4,128)S(1)}, u32[]{:S(2)}, u32[]{:S(2)}) collective-permute-start(f32[3,6,4,128]{3,2,1,0:T(4,128)S(1)} %pad_maximum_fusion.2.mid_ref), channel_id=1, source_target_pairs={{0,16},{16,32},{17,1},{32,48},{33,17},{48,64},{49,33},{64,80},{65,... | collective-permute-start | bytes 110600 | tf_op jit(solution)/shard_map/ppermute | solution.py:428
  48.9 5.6 %collective-permute-start.5 = (f32[3,6,4,128]{3,2,1,0:T(4,128)S(1)}, f32[3,6,4,128]{3,2,1,0:T(4,128)S(1)}, u32[]{:S(2)}, u32[]{:S(2)}) collective-permute-start(f32[3,6,4,128]{3,2,1,0:T(4,128)S(1)} %pad_maximum_fusion.2.mid_ref), channel_id=1, source_target_pairs={{0,32},{16,48},{32,64},{33,1},{48,80},{49,17},{64,96},{65,33},{80,... | collective-permute-start | bytes 110600 | tf_op jit(solution)/shard_map/ppermute | solution.py:428
